TPU v7x, 32 devices: a whole 2x2x4 slice. The times are simulated.
32 devices in a mesh: seq: 8 (over y, x, core), head: 4 (over z).
Axes of the slice: x: 2, y: 2, z: 4, core: 2. Of those that a mesh axis runs over, the one named last changes fastest.
Arguments:
- tokens: bfloat16 [4, 4096, 1792], P(None, ('seq', 'head')), may hold values from -6 to 6
- cotangent: bfloat16 [4, 4096, 1792], P(None, ('seq', 'head')), may hold values from -6 to 6
- segment_ids: int32 [4, 4096], P(None, 'seq'), may hold values from 0 to 15, as said below
- query_weight: bfloat16 [1792, 256], P('seq', 'head'), may hold values from -0.125 to 0.125
- key_weight: bfloat16 [1792, 256], P('seq', 'head'), may hold values from -0.125 to 0.125
- value_weight: bfloat16 [1792, 1792], P('seq', 'head'), may hold values from -0.125 to 0.125
- filter_weight: bfloat16 [1792, 1792], P('seq', 'head'), may hold values from -0.125 to 0.125
- out_weight: bfloat16 [1792, 1792], P('head', 'seq'), may hold values from -3.5 to 3.5
- gate_weight: bfloat16 [1792, 4864], P('seq', 'head'), may hold values from -0.125 to 0.125
- up_weight: bfloat16 [1792, 4864], P('seq', 'head'), may hold values from -0.125 to 0.125
- down_weight: bfloat16 [1792, 4864], P('seq', 'head'), may hold values from -0.078125 to 0.078125
- norm_gain: bfloat16 [1792], P('seq'), may hold values from 0.5 to 1.5
- ffn_gain: bfloat16 [1792], P('seq'), may hold values from 0.5 to 1.5
- conv_taps: bfloat16 [3, 1792], P(None, ('head', 'seq')), may hold values from -2.5 to 2.5
Outputs:
- layer_output: bfloat16 [4, 4096, 1792], P(None, ('seq', 'head'))
- tokens_grad: bfloat16 [4, 4096, 1792], P(None, ('seq', 'head'))
- query_weight_grad: float32 [1792, 256], P('seq', 'head')
- key_weight_grad: float32 [1792, 256], P('seq', 'head')
- value_weight_grad: float32 [1792, 1792], P('seq', 'head')
- filter_weight_grad: float32 [1792, 1792], P('seq', 'head')
- out_weight_grad: float32 [1792, 1792], P('head', 'seq')
- gate_weight_grad: float32 [1792, 4864], P('seq', 'head')
- up_weight_grad: float32 [1792, 4864], P('seq', 'head')
- down_weight_grad: float32 [1792, 4864], P('seq', 'head')
- norm_gain_grad: float32 [1792], P(('head', 'seq'))
- ffn_gain_grad: float32 [1792], P(('head', 'seq'))
- conv_taps_grad: float32 [3, 1792], P(None, ('head', 'seq'))
Inputs may be any that keep to these rules, and one draw needn't show every extreme that they name: `segment_ids`: within each sequence the ids start at 0, never fall, rise by at most 1 from one token to the next, and reach 15.
All inputs are finite; a program needn't handle non-finite values.
Results may differ from a plain program's by a relative error of at most 0.02.
Values may be sent and summed in bfloat16 or wider, within the bound.
A program may use at most 384 MiB of HBM per device.

v0:
```python
import jax
import jax.numpy as jnp
from jax import lax
from jax.sharding import PartitionSpec as P

D = 1792
HEADS = 16
FEAT = 16
SEQ_MB = 2


EPSILON = 1e-06
HALF_ROOT = 0.5**0.5
HIGHEST = lax.Precision.HIGHEST
FAR_KEY = 1000000000.0


def shifted(block, axis, distance):
    devices = range(lax.axis_size(axis))
    route = [(i - distance, i) for i in devices if i - distance in devices]
    return lax.ppermute(block, axis, route)


def prefix(value, axis, combine, identity):
    length, here = (lax.axis_size(axis), lax.axis_index(axis))
    everything = jax.tree.map(
        lambda part, kind: lax.all_gather(part.astype(kind), axis),
        value,
        (jnp.bfloat16, jnp.bfloat16, jnp.bfloat16),
    )
    start = jax.tree.map(
        lambda part, zero: jnp.broadcast_to(jnp.asarray(zero, part.dtype), part.shape),
        value,
        identity,
    )

    def prefix_turn(k, before):
        reached = k < here
        new = combine(
            before, jax.tree.map(lambda part, own: part[k].astype(own.dtype), everything, value)
        )
        return jax.tree.map(lambda a, b: jnp.where(reached, a, b), new, before)

    return lax.fori_loop(0, length, prefix_turn, start)


def carried_in(value, axis, combine, identity):
    length, here = (lax.axis_size(axis), lax.axis_index(axis))
    everything = jax.tree.map(
        lambda part, kind: lax.all_gather(part.astype(kind), axis),
        value,
        jax.tree.map(lambda a: jnp.bfloat16 if a.dtype == jnp.float32 else a.dtype, value),
    )
    start = jax.tree.map(
        lambda part, zero: jnp.broadcast_to(jnp.asarray(zero, part.dtype), part.shape),
        value,
        identity,
    )

    def carried_turn(k, before):
        at = length - 1 - k
        reached = at > here
        new = combine(
            before, jax.tree.map(lambda part, own: part[at].astype(own.dtype), everything, value)
        )
        return jax.tree.map(lambda a, b: jnp.where(reached, a, b), new, before)

    return lax.fori_loop(0, length, carried_turn, start)


def rms_scale(values, gain_vec):
    return (
        values * lax.rsqrt(jnp.mean(values * values, axis=-1, keepdims=True) + EPSILON) * gain_vec
    )


def feature_map(values):
    outer_part = values[..., :, None] * values[..., None, :]
    outer_part = outer_part.reshape(values.shape[:-1] + (values.shape[-1] * values.shape[-1],))
    constant_part = jnp.ones(values.shape[:-1] + (1,), jnp.float32)
    return jnp.concatenate([constant_part, values, outer_part * HALF_ROOT], axis=-1)


def state_tail(key_rows, values, segments):
    last_seg = segments[:, -1]
    weight = (segments == last_seg[:, None]).astype(jnp.float32)
    mapped = feature_map(key_rows) * weight[:, :, None, None]
    tail_state = jnp.einsum("mthf,mthe->mhfe", mapped, values, precision=HIGHEST)
    return (tail_state, jnp.sum(mapped, axis=1))


def exact_scores(queries, key_rows):
    return jnp.einsum("mthf,mshf->mhts", queries, key_rows, precision=HIGHEST)


def narrow_scores(queries, key_rows):
    return jnp.einsum(
        "mthf,mshf->mhts",
        queries.astype(jnp.bfloat16),
        key_rows.astype(jnp.bfloat16),
        preferred_element_type=jnp.float32,
    )


def local_attend(
    queries, key_rows, values, segments, prior_state, prior_norm, prior_last, score_fn
):
    mapped = feature_map(queries)
    in_prior = (segments == prior_last[:, None]).astype(jnp.float32)
    numerator = (
        jnp.einsum("mthf,mhfe->mthe", mapped, prior_state, precision=HIGHEST)
        * in_prior[:, :, None, None]
    )
    denominator = (
        jnp.einsum("mthf,mhf->mth", mapped, prior_norm, precision=HIGHEST) * in_prior[:, :, None]
    )
    scores = score_fn(queries, key_rows)
    places = jnp.arange(queries.shape[1])
    allowed = (places[:, None] >= places[None, :])[None, :, :] & (
        segments[:, :, None] == segments[:, None, :]
    )
    weights = jnp.where(allowed[:, None, :, :], 1.0 + scores + 0.5 * scores * scores, 0.0)
    numerator = numerator + jnp.einsum("mhts,mshe->mthe", weights, values, precision=HIGHEST)
    denominator = denominator + jnp.transpose(jnp.sum(weights, axis=-1), (0, 2, 1))
    return numerator / denominator[..., None]


def gated_filter(value_rows, edge_rows, gate_pre, seg_rows, prior_seg, tap_rows):
    extended = jnp.concatenate([edge_rows, value_rows], axis=1)
    seg_ext = jnp.concatenate([jnp.stack([prior_seg, prior_seg], axis=1), seg_rows], axis=1)
    span = value_rows.shape[1]
    one_back = (
        extended[:, 1 : span + 1]
        * (seg_rows == seg_ext[:, 1 : span + 1]).astype(jnp.float32)[..., None]
    )
    two_back = extended[:, 0:span] * (seg_rows == seg_ext[:, 0:span]).astype(jnp.float32)[..., None]
    filtered = tap_rows[0] * value_rows + tap_rows[1] * one_back + tap_rows[2] * two_back
    return filtered * jax.nn.silu(gate_pre)


def join_latest(earlier, later):
    largest = jnp.maximum(earlier[2], later[2])
    keep_early = (earlier[2] == largest).astype(jnp.float32)
    keep_late = (later[2] == largest).astype(jnp.float32)
    return (
        earlier[0] * keep_early[:, None, None, None] + later[0] * keep_late[:, None, None, None],
        earlier[1] * keep_early[:, None, None] + later[1] * keep_late[:, None, None],
        largest,
    )


def join_earliest(earlier, later):
    smallest = jnp.minimum(earlier[2], later[2])
    keep_early = (earlier[2] == smallest).astype(jnp.float32)
    keep_late = (later[2] == smallest).astype(jnp.float32)
    return (
        earlier[0] * keep_early[:, None, None, None] + later[0] * keep_late[:, None, None, None],
        earlier[1] * keep_early[:, None, None] + later[1] * keep_late[:, None, None],
        smallest,
    )


def gather_weights(parts):
    return (
        lax.all_gather(parts[0], "seq", axis=0, tiled=True),
        lax.all_gather(parts[1], "seq", axis=0, tiled=True),
        lax.all_gather(parts[2], "seq", axis=0, tiled=True),
        lax.all_gather(parts[3], "seq", axis=0, tiled=True),
        lax.all_gather(parts[4], "seq", axis=1, tiled=True),
        lax.all_gather(parts[5], "seq", axis=0, tiled=True),
        lax.all_gather(parts[6], "seq", axis=0, tiled=True),
        lax.all_gather(parts[7], "seq", axis=0, tiled=True),
        lax.all_gather(parts[8], "seq", axis=0, tiled=True),
        lax.all_gather(parts[9], "seq", axis=0, tiled=True),
        lax.all_gather(parts[10], "seq", axis=1, tiled=True),
    )


def reduce_grads(grads):
    return (
        lax.psum_scatter(
            grads[0].astype(jnp.bfloat16), "seq", scatter_dimension=0, tiled=True
        ).astype(jnp.float32),
        lax.psum_scatter(
            grads[1].astype(jnp.bfloat16), "seq", scatter_dimension=0, tiled=True
        ).astype(jnp.float32),
        lax.psum_scatter(
            grads[2].astype(jnp.bfloat16), "seq", scatter_dimension=0, tiled=True
        ).astype(jnp.float32),
        lax.psum_scatter(
            grads[3].astype(jnp.bfloat16), "seq", scatter_dimension=0, tiled=True
        ).astype(jnp.float32),
        lax.psum_scatter(
            grads[4].astype(jnp.bfloat16), "seq", scatter_dimension=1, tiled=True
        ).astype(jnp.float32),
        lax.psum_scatter(
            grads[5].astype(jnp.bfloat16), "seq", scatter_dimension=0, tiled=True
        ).astype(jnp.float32),
        lax.psum_scatter(
            grads[6].astype(jnp.bfloat16), "seq", scatter_dimension=0, tiled=True
        ).astype(jnp.float32),
        lax.psum_scatter(
            grads[7].astype(jnp.bfloat16), "seq", scatter_dimension=0, tiled=True
        ).astype(jnp.float32),
        lax.psum_scatter(
            grads[8].astype(jnp.bfloat16), "seq", scatter_dimension=0, tiled=True
        ).astype(jnp.float32),
        lax.psum_scatter(
            grads[9].astype(jnp.bfloat16), "seq", scatter_dimension=0, tiled=True
        ).astype(jnp.float32),
        lax.psum_scatter(
            grads[10].astype(jnp.bfloat16), "seq", scatter_dimension=1, tiled=True
        ).astype(jnp.float32),
    )


def dot_float(left, right):
    return jnp.dot(left, right, preferred_element_type=jnp.float32)


def dot_right_t(left, right):
    return lax.dot_general(
        left, right, (((1,), (1,)), ((), ())), preferred_element_type=jnp.float32
    )


def gain_terms(rows, grad):
    scaled = rows * lax.rsqrt(jnp.mean(rows * rows, axis=-1, keepdims=True) + EPSILON)
    return jnp.sum((grad * scaled).reshape(-1, rows.shape[-1]), axis=0)


def norm_back(rows, gain_vec, grad):

    def scale_rows(rows_in):
        return rms_scale(rows_in, gain_vec)

    _, pull_back = jax.vjp(scale_rows, rows)
    return pull_back(grad)[0]


def local(
    tokens,
    cotangent,
    segment_ids,
    query_weight,
    key_weight,
    value_weight,
    filter_weight,
    out_weight,
    gate_weight,
    up_weight,
    down_weight,
    norm_gain,
    ffn_gain,
    conv_taps,
):
    shards = (
        query_weight,
        key_weight,
        value_weight,
        filter_weight,
        out_weight,
        gate_weight,
        up_weight,
        down_weight,
        norm_gain,
        ffn_gain,
        conv_taps,
    )
    per_micro = SEQ_MB
    row_share = tokens.shape[1]
    seq_count = segment_ids.shape[1]
    col_width = value_weight.shape[1]
    head_width = D // HEADS
    start_row = lax.axis_index("head") * row_share
    outputs = []
    input_grads = []
    totals = None
    for micro_index in range(tokens.shape[0] // per_micro):
        first_seq = micro_index * per_micro
        gathered = gather_weights(shards)
        (
            w_query,
            w_key,
            w_value,
            w_filter,
            w_out,
            w_gate,
            w_up,
            w_down,
            gain_one,
            gain_two,
            tap_rows,
        ) = gathered
        local_heads = w_query.shape[1] // FEAT
        gain_one_f = gain_one.astype(jnp.float32)
        gain_two_f = gain_two.astype(jnp.float32)
        taps_float = tap_rows.astype(jnp.float32)
        rows_in = tokens[first_seq : first_seq + per_micro]
        cot_local = cotangent[first_seq : first_seq + per_micro]
        own_rows = rows_in.astype(jnp.float32)
        seg_rows = segment_ids[first_seq : first_seq + per_micro].astype(jnp.float32)
        full_low, cot_full = (
            lax.all_gather(rows_in, "head", axis=1, tiled=True),
            lax.all_gather(cot_local, "head", axis=1, tiled=True),
        )
        full_rows = full_low.astype(jnp.float32).reshape(-1, D)
        normed = rms_scale(full_rows, gain_one_f).astype(jnp.bfloat16)
        query_low = dot_float(normed, w_query).astype(jnp.bfloat16)
        key_low = dot_float(normed, w_key).astype(jnp.bfloat16)
        value_low = dot_float(normed, w_value).astype(jnp.bfloat16)
        gate_pre = dot_float(normed, w_filter).reshape(per_micro, seq_count, col_width)
        head_shape = (per_micro, seq_count, local_heads, FEAT)
        queries = 0.5 * query_low.astype(jnp.float32).reshape(head_shape)
        key_rows = 0.5 * key_low.astype(jnp.float32).reshape(head_shape)
        value_seq = value_low.reshape(per_micro, seq_count, col_width)
        last_seg = seg_rows[:, -1]
        tail_mask = seg_rows[:, -2:] == last_seg[:, None]
        edge_send = jnp.where(
            tail_mask[..., None], value_seq[:, -2:], jnp.zeros_like(value_seq[:, -2:])
        )
        edge_recv, prior_seg = shifted((edge_send, last_seg.astype(jnp.bfloat16)), "seq", 1)
        edge_float = edge_recv.astype(jnp.float32)
        prior_seg = prior_seg.astype(jnp.float32)
        value_float = value_seq.astype(jnp.float32)
        mixed_values = gated_filter(
            value_float, edge_float, gate_pre, seg_rows, prior_seg, taps_float
        )
        head_values = mixed_values.reshape(per_micro, seq_count, local_heads, head_width)
        tail_state, tail_norm = state_tail(key_rows, head_values, seg_rows)
        identity = (
            jnp.zeros_like(tail_state),
            jnp.zeros_like(tail_norm),
            jnp.full((per_micro,), -1.0, jnp.float32),
        )
        prior_state, prior_norm, prior_last = prefix(
            (tail_state, tail_norm, last_seg), "seq", join_latest, identity
        )
        attended = local_attend(
            queries,
            key_rows,
            head_values,
            seg_rows,
            prior_state,
            prior_norm,
            prior_last,
            narrow_scores,
        )
        attended_low = attended.reshape(-1, col_width).astype(jnp.bfloat16)
        attention_terms = dot_float(attended_low, w_out)
        mixed_sum = lax.psum(attention_terms, "head")
        residual = full_rows + mixed_sum
        normed_two = rms_scale(residual, gain_two_f).astype(jnp.bfloat16)
        residual_own = lax.dynamic_slice_in_dim(
            residual.reshape(per_micro, seq_count, D), start_row, row_share, 1
        )
        gate_act = dot_float(normed_two, w_gate)
        up_act = dot_float(normed_two, w_up)
        hidden = (jax.nn.silu(gate_act) * up_act).astype(jnp.bfloat16)
        ffn_terms = dot_right_t(hidden, w_down).reshape(per_micro, seq_count, D)
        ffn_part = lax.psum_scatter(
            ffn_terms.astype(jnp.bfloat16), "head", scatter_dimension=1, tiled=True
        ).astype(jnp.float32)
        outputs.append((residual_own + ffn_part).astype(jnp.bfloat16))
        gathered = gather_weights(shards)
        (
            w_query,
            w_key,
            w_value,
            w_filter,
            w_out,
            w_gate,
            w_up,
            w_down,
            gain_one,
            gain_two,
            tap_rows,
        ) = gathered
        cot_rows = cot_full.reshape(-1, D)
        grad_down = dot_float(cot_rows.T, hidden)
        grad_hidden = dot_float(cot_rows, w_down)
        sigmoid_gate = jax.nn.sigmoid(gate_act)
        grad_gate = (
            grad_hidden * up_act * sigmoid_gate * (1.0 + gate_act * (1.0 - sigmoid_gate))
        ).astype(jnp.bfloat16)
        grad_up = (grad_hidden * gate_act * sigmoid_gate).astype(jnp.bfloat16)
        grad_wgate = dot_float(normed_two.T, grad_gate)
        grad_wup = dot_float(normed_two.T, grad_up)
        back_terms = dot_float(grad_gate, w_gate.T) + dot_float(grad_up, w_up.T)
        back_two = lax.psum(back_terms.astype(jnp.bfloat16), "head").astype(jnp.float32)
        grad_residual = cot_rows.astype(jnp.float32) + norm_back(residual, gain_two_f, back_two)
        grad_residual_low = grad_residual.astype(jnp.bfloat16)
        grad_res_own = lax.dynamic_slice_in_dim(
            grad_residual.reshape(per_micro, seq_count, D), start_row, row_share, 1
        )
        back_two_own = lax.dynamic_slice_in_dim(
            back_two.reshape(per_micro, seq_count, D), start_row, row_share, 1
        )
        gain_two_part = gain_terms(residual_own, back_two_own)
        grad_out = dot_float(attended_low.T, grad_residual_low)
        grad_attended = dot_float(grad_residual_low, w_out.T).reshape(
            per_micro, seq_count, local_heads, head_width
        )

        def attend_part(query_in, key_in, value_in, state_in, norm_in):
            return local_attend(
                query_in, key_in, value_in, seg_rows, state_in, norm_in, prior_last, exact_scores
            )

        _, attend_back = jax.vjp(
            attend_part, queries, key_rows, head_values, prior_state, prior_norm
        )
        grad_queries, grad_keys, grad_values, grad_prior_state, grad_prior_norm = attend_back(
            grad_attended
        )
        far_end = (
            jnp.zeros_like(grad_prior_state),
            jnp.zeros_like(grad_prior_norm),
            jnp.full((per_micro,), FAR_KEY, jnp.float32),
        )
        later_state, later_norm, _ = carried_in(
            (grad_prior_state, grad_prior_norm, prior_last), "seq", join_earliest, far_end
        )

        def tail_part(key_in, value_in):
            return state_tail(key_in, value_in, seg_rows)

        _, tail_back = jax.vjp(tail_part, key_rows, head_values)
        more_keys, more_values = tail_back((later_state, later_norm))
        grad_keys = grad_keys + more_keys
        grad_values = grad_values + more_values

        def filter_part(value_in, edge_in, gate_in, taps_in):
            return gated_filter(value_in, edge_in, gate_in, seg_rows, prior_seg, taps_in)

        _, filter_back = jax.vjp(filter_part, value_float, edge_float, gate_pre, taps_float)
        grad_value, grad_edge, grad_gate_pre, grad_taps = filter_back(
            grad_values.reshape(per_micro, seq_count, col_width)
        )
        edge_back = shifted(grad_edge, "seq", -1)
        edge_back = jnp.where(tail_mask[..., None], edge_back, 0.0)
        grad_value = jnp.concatenate([grad_value[:, :-2], grad_value[:, -2:] + edge_back], axis=1)
        grad_query_low = (0.5 * grad_queries).reshape(-1, w_query.shape[1]).astype(jnp.bfloat16)
        grad_key_low = (0.5 * grad_keys).reshape(-1, w_key.shape[1]).astype(jnp.bfloat16)
        grad_value_low = grad_value.reshape(-1, col_width).astype(jnp.bfloat16)
        grad_filter_low = grad_gate_pre.reshape(-1, col_width).astype(jnp.bfloat16)
        grad_wq = dot_float(normed.T, grad_query_low)
        grad_wk = dot_float(normed.T, grad_key_low)
        grad_wv = dot_float(normed.T, grad_value_low)
        grad_wf = dot_float(normed.T, grad_filter_low)
        back_one_terms = (
            dot_float(grad_query_low, w_query.T)
            + dot_float(grad_key_low, w_key.T)
            + dot_float(grad_value_low, w_value.T)
            + dot_float(grad_filter_low, w_filter.T)
        )
        gain_one_part = gain_terms(full_rows, back_one_terms)
        back_one_own, gain_pair = (
            lax.psum_scatter(
                back_one_terms.reshape(per_micro, seq_count, D).astype(jnp.bfloat16),
                "head",
                scatter_dimension=1,
                tiled=True,
            ).astype(jnp.float32),
            lax.psum_scatter(
                jnp.stack([gain_one_part, gain_two_part]).astype(jnp.bfloat16),
                "head",
                scatter_dimension=1,
                tiled=True,
            ).astype(jnp.float32),
        )
        grad_input = grad_res_own + norm_back(own_rows, gain_one_f, back_one_own)
        input_grads.append(grad_input.astype(jnp.bfloat16))
        grads = (
            grad_wq,
            grad_wk,
            grad_wv,
            grad_wf,
            grad_out,
            grad_wgate,
            grad_wup,
            grad_down,
            gain_pair[0],
            gain_pair[1],
            grad_taps,
        )
        reduced = reduce_grads(grads)
        totals = reduced if totals is None else jax.tree.map(jnp.add, totals, reduced)
    return (
        jnp.concatenate(outputs, axis=0),
        jnp.concatenate(input_grads, axis=0),
        totals[0],
        totals[1],
        totals[2],
        totals[3],
        totals[4],
        totals[5],
        totals[6],
        totals[7],
        totals[8],
        totals[9],
        totals[10],
    )


def solution(mesh):
    placed = (
        P(None, ("seq", "head"), None),
        P(None, ("seq", "head"), None),
        P(None, "seq"),
        P("seq", "head"),
        P("seq", "head"),
        P("seq", "head"),
        P("seq", "head"),
        P("head", "seq"),
        P("seq", "head"),
        P("seq", "head"),
        P("seq", "head"),
        P("seq"),
        P("seq"),
        P(None, ("head", "seq")),
    )
    return jax.shard_map(
        local,
        mesh=mesh,
        in_specs=placed,
        out_specs=(
            P(None, ("seq", "head"), None),
            P(None, ("seq", "head"), None),
            P("seq", "head"),
            P("seq", "head"),
            P("seq", "head"),
            P("seq", "head"),
            P("head", "seq"),
            P("seq", "head"),
            P("seq", "head"),
            P("seq", "head"),
            P(("head", "seq")),
            P(("head", "seq")),
            P(None, ("head", "seq")),
        ),
        check_vma=False,
    )
```

profile of v0, /device:TPU:0, one launch (start us, length us, event | category | flops | bytes accessed | tf_op | source)
XLA Modules:
  0.0 2640.5 jit_solution(14372599836794794997)
XLA Ops:
  31.2 14.2 all-reduce.25
  54.6 30.5 %all-gather.30.cloned.1.call-done = bf16[2,512,1792]{2,1,0:T(8,128)(2,1)} async-done(((bf16[2,128,1792]{2,1,0:T(8,128)(2,1)}), bf16[2,512,1792]{2,1,0:T(8,128)(2,1)}) %all-gather.30.cloned.1.call-update) | async-done | bytes 3670032 | tf_op jit(solution)/shard_map/all_gather | solution.py:304
  87.9 70.0 %all-gather.44.cloned.1.call-done = bf16[2,512,1792]{2,1,0:T(8,128)(2,1)} async-done(((bf16[2,128,1792]{2,1,0:T(8,128)(2,1)}), bf16[2,512,1792]{2,1,0:T(8,128)(2,1)}) %all-gather.44.cloned.1.call-update) | async-done | bytes 3670032 | tf_op jit(solution)/shard_map/all_gather | solution.py:304
  168.9 16.4 all-gather.32.cloned.1.call-done
  331.0 16.8 while.76
  347.9 17.4 while.77
  420.3 14.8 all-reduce.24
  435.0 475.0 %all-reduce.30.cloned.1.call-done = (f32[1024,1792]{1,0:T(8,128)}, f32[1024,1792]{1,0:T(8,128)}) async-done(((f32[1024,1792]{1,0:T(8,128)}, f32[1024,1792]{1,0:T(8,128)}), (f32[1024,1792]{1,0:T(8,128)}, f32[1024,1792]{1,0:T(8,128)})) %all-reduce.30.cloned.1.call-update) | async-done | bytes 14680080 | tf_op jit(solution)/shard_map/psum | solution.py:351
  929.3 19.9 all-gather.40.cloned.1.call-done
  959.7 29.7 %all-gather.38.cloned.1.call-done = bf16[1792,1216]{1,0:T(8,128)(2,1)} async-done(((bf16[224,1216]{1,0:T(8,128)(2,1)}), bf16[1792,1216]{1,0:T(8,128)(2,1)}) %all-gather.38.cloned.1.call-update) | async-done | bytes 4358160 | tf_op jit(solution)/shard_map/all_gather | solution.py:170
  999.8 63.3 %all-gather.46.cloned.1.call-done = bf16[2,512,1792]{2,1,0:T(8,128)(2,1)} async-done(((bf16[2,128,1792]{2,1,0:T(8,128)(2,1)}), bf16[2,512,1792]{2,1,0:T(8,128)(2,1)}) %all-gather.46.cloned.1.call-update) | async-done | bytes 3670032 | tf_op jit(solution)/shard_map/all_gather | solution.py:305
  1063.1 38.7 %all-gather.42.cloned.1.call-done = bf16[1792,1216]{1,0:T(8,128)(2,1)} async-done(((bf16[224,1216]{1,0:T(8,128)(2,1)}), bf16[1792,1216]{1,0:T(8,128)(2,1)}) %all-gather.42.cloned.1.call-update) | async-done | bytes 4358160 | tf_op jit(solution)/shard_map/all_gather | solution.py:172
  1136.0 40.1 %all-gather.48.cloned.1.call-done = bf16[2,512,1792]{2,1,0:T(8,128)(2,1)} async-done(((bf16[2,128,1792]{2,1,0:T(8,128)(2,1)}), bf16[2,512,1792]{2,1,0:T(8,128)(2,1)}) %all-gather.48.cloned.1.call-update) | async-done | bytes 3670032 | tf_op jit(solution)/shard_map/all_gather | solution.py:305
  1236.1 234.2 %all-reduce.32.cloned.1.call-done = (bf16[1024,1792]{1,0:T(8,128)(2,1)}, bf16[1024,1792]{1,0:T(8,128)(2,1)}) async-done(((bf16[1024,1792]{1,0:T(8,128)(2,1)}, bf16[1024,1792]{1,0:T(8,128)(2,1)}), (bf16[1024,1792]{1,0:T(8,128)(2,1)}, bf16[1024,1792]{1,0:T(8,128)(2,1)})) %all-reduce.32.cloned.1.call-update) | async-done | bytes 7340048 | tf_op jit(solution)/shard_map/psum | solution.py:390
  1769.2 14.5 fusion.66
  1794.5 17.0 while.78
  1811.5 17.4 while.79
  1980.7 52.2 %reduce-scatter.67.cloned.1.call-done = bf16[224,1216]{1,0:T(8,128)(2,1)} async-done(((bf16[1792,1216]{1,0:T(8,128)(2,1)}), bf16[224,1216]{1,0:T(8,128)(2,1)}) %reduce-scatter.67.cloned.1.call-update) | async-done | bytes 544784 | tf_op jit(solution)/shard_map/reduce_scatter | solution.py:199
  2038.0 32.0 %reduce-scatter.69.cloned.1.call-done = bf16[224,64]{1,0:T(8,128)(2,1)} async-done(((bf16[1792,64]{1,0:T(8,128)(2,1)}), bf16[224,64]{1,0:T(8,128)(2,1)}) %reduce-scatter.69.cloned.1.call-update) | async-done | bytes 28688
  2070.9 36.8 %reduce-scatter.71.cloned.1.call-done = bf16[224,64]{1,0:T(8,128)(2,1)} async-done(((bf16[1792,64]{1,0:T(8,128)(2,1)}), bf16[224,64]{1,0:T(8,128)(2,1)}) %reduce-scatter.71.cloned.1.call-update) | async-done | bytes 28688
  2109.3 41.4 %reduce-scatter.77.cloned.1.call-done = bf16[224,448]{1,0:T(8,128)(2,1)} async-done(((bf16[1792,448]{1,0:T(8,128)(2,1)}), bf16[224,448]{1,0:T(8,128)(2,1)}) %reduce-scatter.77.cloned.1.call-update) | async-done | bytes 200720
  2151.7 42.0 %reduce-scatter.79.cloned.1.call-done = bf16[224,448]{1,0:T(8,128)(2,1)} async-done(((bf16[1792,448]{1,0:T(8,128)(2,1)}), bf16[224,448]{1,0:T(8,128)(2,1)}) %reduce-scatter.79.cloned.1.call-update) | async-done | bytes 200720
  2195.7 21.4 reduce-scatter.87.cloned.1.call-done
  2218.3 20.5 reduce-scatter.85.cloned.1.call-done
  2240.0 22.8 all-reduce.23
  2275.2 37.0 %reduce-scatter.75.cloned.1.call-done = bf16[224,64]{1,0:T(8,128)(2,1)} async-done(((bf16[1792,64]{1,0:T(8,128)(2,1)}), bf16[224,64]{1,0:T(8,128)(2,1)}) %reduce-scatter.75.cloned.1.call-update) | async-done | bytes 28688
  2313.7 41.4 %reduce-scatter.57.cloned.1.call-done = bf16[224,448]{1,0:T(8,128)(2,1)} async-done(((bf16[1792,448]{1,0:T(8,128)(2,1)}), bf16[224,448]{1,0:T(8,128)(2,1)}) %reduce-scatter.57.cloned.1.call-update) | async-done | bytes 200720 | tf_op jit(solution)/shard_map/reduce_scatter | solution.py:190
  2355.1 43.1 %reduce-scatter.59.cloned.1.call-done = bf16[224,448]{1,0:T(8,128)(2,1)} async-done(((bf16[1792,448]{1,0:T(8,128)(2,1)}), bf16[224,448]{1,0:T(8,128)(2,1)}) %reduce-scatter.59.cloned.1.call-update) | async-done | bytes 200720 | tf_op jit(solution)/shard_map/reduce_scatter | solution.py:190
  2400.1 41.8 %reduce-scatter.55.cloned.1.call-done = bf16[224,448]{1,0:T(8,128)(2,1)} async-done(((bf16[1792,448]{1,0:T(8,128)(2,1)}), bf16[224,448]{1,0:T(8,128)(2,1)}) %reduce-scatter.55.cloned.1.call-update) | async-done | bytes 200720 | tf_op jit(solution)/shard_map/reduce_scatter | solution.py:187
  2441.8 42.9 %reduce-scatter.53.cloned.1.call-done = bf16[224,448]{1,0:T(8,128)(2,1)} async-done(((bf16[1792,448]{1,0:T(8,128)(2,1)}), bf16[224,448]{1,0:T(8,128)(2,1)}) %reduce-scatter.53.cloned.1.call-update) | async-done | bytes 200720 | tf_op jit(solution)/shard_map/reduce_scatter | solution.py:187
  2486.6 68.7 %reduce-scatter.51.cloned.1.call-done = bf16[2,128,1792]{2,1,0:T(8,128)(2,1)} async-done(((bf16[2,512,1792]{2,1,0:T(8,128)(2,1)}), bf16[2,128,1792]{2,1,0:T(8,128)(2,1)}) %reduce-scatter.51.cloned.1.call-update) | async-done | bytes 917520 | tf_op jit(solution)/shard_map/reduce_scatter | solution.py:459
  2555.3 71.1 %reduce-scatter.49.cloned.1.call-done = bf16[2,128,1792]{2,1,0:T(8,128)(2,1)} async-done(((bf16[2,512,1792]{2,1,0:T(8,128)(2,1)}), bf16[2,128,1792]{2,1,0:T(8,128)(2,1)}) %reduce-scatter.49.cloned.1.call-update) | async-done | bytes 917520 | tf_op jit(solution)/shard_map/reduce_scatter | solution.py:459
  (1025 shorter events, 942.0 us)
Async XLA Ops:
  18.9 312.1 %all-gather.50.cloned.1.call-start = ((), (), s32[]{:S(2)}) async-start(), calls=%async_computation.44 | async-start | bytes 5031936 | tf_op jit(solution)/shard_map/all_gather | solution.py:27
  249.6 660.5 %all-reduce.30.cloned.1.call-start = ((), (), s32[]{:S(2)}) async-start(), calls=%async_computation.58 | async-start | bytes 29360128 | tf_op jit(solution)/shard_map/psum | solution.py:351
  415.3 534.0 %all-gather.40.cloned.1.call-start = ((), (), s32[]{:S(2)}) async-start(), calls=%async_computation.27 | async-start | bytes 5160960 | tf_op jit(solution)/shard_map/all_gather | solution.py:171
  416.0 573.4 %all-gather.38.cloned.1.call-start = ((), (), s32[]{:S(2)}) async-start(), calls=%async_computation.26 | async-start | bytes 5160960 | tf_op jit(solution)/shard_map/all_gather | solution.py:170
  416.6 646.5 %all-gather.46.cloned.1.call-start = ((), (), s32[]{:S(2)}) async-start(), calls=%async_computation.32 | async-start | bytes 4587520 | tf_op jit(solution)/shard_map/all_gather | solution.py:305
  418.1 683.7 %all-gather.42.cloned.1.call-start = ((), (), s32[]{:S(2)}) async-start(), calls=%async_computation.28 | async-start | bytes 5160960 | tf_op jit(solution)/shard_map/all_gather | solution.py:172
  418.7 757.4 %all-gather.48.cloned.1.call-start = ((), (), s32[]{:S(2)}) async-start(), calls=%async_computation.34 | async-start | bytes 4587520 | tf_op jit(solution)/shard_map/all_gather | solution.py:305
  419.5 1050.8 %all-reduce.32.cloned.1.call-start = ((), (), s32[]{:S(2)}) async-start(), calls=%async_computation.59 | async-start | bytes 14680064 | tf_op jit(solution)/shard_map/psum | solution.py:390
  1214.4 508.1 %reduce-scatter.45.cloned.1.call-start = ((), (), s32[]{:S(2)}) async-start(), calls=%async_computation.29 | async-start | bytes 4587520 | tf_op jit(solution)/shard_map/reduce_scatter | solution.py:361
  1224.9 513.1 %reduce-scatter.47.cloned.1.call-start = ((), (), s32[]{:S(2)}) async-start(), calls=%async_computation.31 | async-start | bytes 4587520 | tf_op jit(solution)/shard_map/reduce_scatter | solution.py:361
  1235.4 559.1 %all-gather.54.cloned.1.call-start = ((), (), s32[]{:S(2)}) async-start(), calls=%async_computation.46 | async-start | bytes 5031936 | tf_op jit(solution)/shard_map/all_gather | solution.py:50
  1512.6 298.9 %all-gather.56.cloned.1.call-start = ((), (), s32[]{:S(2)}) async-start(), calls=%async_computation.47 | async-start | bytes 5031936 | tf_op jit(solution)/shard_map/all_gather | solution.py:50
  1533.1 441.1 %reduce-scatter.81.cloned.1.call-start = ((), (), s32[]{:S(2)}) async-start(), calls=%async_computation.54 | async-start | bytes 5160960
  1550.1 425.4 %reduce-scatter.83.cloned.1.call-start = ((), (), s32[]{:S(2)}) async-start(), calls=%async_computation.55 | async-start | bytes 5160960
  1567.3 411.1 %reduce-scatter.61.cloned.1.call-start = ((), (), s32[]{:S(2)}) async-start(), calls=%async_computation.40 | async-start | bytes 5160960 | tf_op jit(solution)/shard_map/reduce_scatter | solution.py:196
  1577.3 401.0 %reduce-scatter.63.cloned.1.call-start = ((), (), s32[]{:S(2)}) async-start(), calls=%async_computation.41 | async-start | bytes 5160960 | tf_op jit(solution)/shard_map/reduce_scatter | solution.py:196
  1587.7 393.0 %reduce-scatter.65.cloned.1.call-start = ((), (), s32[]{:S(2)}) async-start(), calls=%async_computation.42 | async-start | bytes 5160960 | tf_op jit(solution)/shard_map/reduce_scatter | solution.py:199
  1597.8 435.2 %reduce-scatter.67.cloned.1.call-start = ((), (), s32[]{:S(2)}) async-start(), calls=%async_computation.43 | async-start | bytes 5160960 | tf_op jit(solution)/shard_map/reduce_scatter | solution.py:199
  1612.1 457.9 %reduce-scatter.69.cloned.1.call-start = ((), (), s32[]{:S(2)}) async-start(), calls=%async_computation.48 | async-start | bytes 516096
  1715.2 392.6 %reduce-scatter.71.cloned.1.call-start = ((), (), s32[]{:S(2)}) async-start(), calls=%async_computation.49 | async-start | bytes 516096
  1722.4 428.3 %reduce-scatter.77.cloned.1.call-start = ((), (), s32[]{:S(2)}) async-start(), calls=%async_computation.52 | async-start | bytes 2064384
  1759.9 433.9 %reduce-scatter.79.cloned.1.call-start = ((), (), s32[]{:S(2)}) async-start(), calls=%async_computation.53 | async-start | bytes 2064384
  1794.4 422.7 %reduce-scatter.87.cloned.1.call-start = ((), (), s32[]{:S(2)}) async-start(), calls=%async_computation.57 | async-start | bytes 573440
  1939.8 299.0 %reduce-scatter.85.cloned.1.call-start = ((), (), s32[]{:S(2)}) async-start(), calls=%async_computation.56 | async-start | bytes 573440
  1940.9 333.4 %reduce-scatter.73.cloned.1.call-start = ((), (), s32[]{:S(2)}) async-start(), calls=%async_computation.50 | async-start | bytes 516096
  1944.8 367.4 %reduce-scatter.75.cloned.1.call-start = ((), (), s32[]{:S(2)}) async-start(), calls=%async_computation.51 | async-start | bytes 516096
  1949.3 405.8 %reduce-scatter.57.cloned.1.call-start = ((), (), s32[]{:S(2)}) async-start(), calls=%async_computation.38 | async-start | bytes 2064384 | tf_op jit(solution)/shard_map/reduce_scatter | solution.py:190
  1954.9 443.3 %reduce-scatter.59.cloned.1.call-start = ((), (), s32[]{:S(2)}) async-start(), calls=%async_computation.39 | async-start | bytes 2064384 | tf_op jit(solution)/shard_map/reduce_scatter | solution.py:190
  1960.6 481.2 %reduce-scatter.55.cloned.1.call-start = ((), (), s32[]{:S(2)}) async-start(), calls=%async_computation.37 | async-start | bytes 2064384 | tf_op jit(solution)/shard_map/reduce_scatter | solution.py:187
  1966.5 518.2 %reduce-scatter.53.cloned.1.call-start = ((), (), s32[]{:S(2)}) async-start(), calls=%async_computation.36 | async-start | bytes 2064384 | tf_op jit(solution)/shard_map/reduce_scatter | solution.py:187
  1972.2 583.2 %reduce-scatter.51.cloned.1.call-start = ((), (), s32[]{:S(2)}) async-start(), calls=%async_computation.35 | async-start | bytes 4587520 | tf_op jit(solution)/shard_map/reduce_scatter | solution.py:459
  1972.7 653.7 %reduce-scatter.49.cloned.1.call-start = ((), (), s32[]{:S(2)}) async-start(), calls=%async_computation.33 | async-start | bytes 4587520 | tf_op jit(solution)/shard_map/reduce_scatter | solution.py:459
  (240 other events, 7463.8 us)
Sparse Core Ops, SparseCore 0:
  10.2 74.7 all-gather.29
  87.2 70.7 all-gather.43
  238.3 37.8 all-gather.49
  278.6 37.9 all-gather.51
  415.4 494.6 all-reduce.29
  912.0 37.2 all-gather.39
  951.0 38.3 all-gather.37
  990.9 72.0 all-gather.45
  1064.8 36.9 all-gather.41
  1104.0 72.0 all-gather.47
  1214.5 255.7 all-reduce.31
  1472.4 67.2 reduce-scatter.44
  1541.9 68.7 reduce-scatter.46
  1613.1 38.2 all-gather.53
  1653.1 37.8 all-gather.55
  1694.5 53.3 reduce-scatter.80
  1751.2 53.3 reduce-scatter.82
  1808.1 53.2 reduce-scatter.60
  1864.9 54.4 reduce-scatter.62
  1922.9 53.2 reduce-scatter.64
  1979.6 53.2 reduce-scatter.66
  2036.0 33.9 reduce-scatter.68
  2073.8 33.8 reduce-scatter.70
  2110.9 39.6 reduce-scatter.76
  2154.0 39.6 reduce-scatter.78
  2278.3 33.9 reduce-scatter.74
  2315.4 39.6 reduce-scatter.56
  2358.5 39.6 reduce-scatter.58
  2402.1 39.6 reduce-scatter.54
  2445.1 39.6 reduce-scatter.52
  2486.9 68.3 reduce-scatter.50
  2557.6 68.7 reduce-scatter.48
  (6 shorter events, 152.6 us)
where the time goes:
time: 2650 us; the launch traced here: 2640 us
  waiting for transfers between devices  1630 us (62%)
  matrix products  533 us (20%)
  other arithmetic  176 us (7%)
  local copies, waits for them, and re-layouts  142 us (5%)
  blocking collectives  114 us (4%)
    psum x1, waiting for transfers between devices, local(): mixed_sum = lax.psum(attention_terms, 'head')  475 us
    dot_general x46, matrix products, dot_float(): return jnp.dot(left, right, preferred_element_type=jnp.float32)  294 us
    unnamed x48, waiting for transfers between devices  246 us
    psum x1, waiting for transfers between devices, local(): lax.psum(back_terms.astype(jnp.bfloat16), 'head').astype(jnp.float32)  234 us
    reduce_scatter x2, waiting for transfers between devices, local(): lax.psum_scatter(back_one_terms.reshape(per_micro, seq_count, D).astype(j...  140 us
    all_gather x2, waiting for transfers between devices, local(): lax.all_gather(cot_local, 'head', axis=1, tiled=True)  103 us
    all_gather x2, waiting for transfers between devices, local(): lax.all_gather(rows_in, 'head', axis=1, tiled=True)  100 us
    reduce_scatter x2, waiting for transfers between devices, reduce_grads(): lax.psum_scatter(grads[2].astype(jnp.bfloat16), 'seq', scatter_dimension=...  84.7 us
  transfers between devices with their start and end apart: 44, of which 26 were waited for; matrix products, arithmetic and copies ran while one was open for 28% of the time, Pallas kernels for 0%

commit v1 on v0

v1 whole, which is shorter than its diff:
```python
import functools

import jax
import jax.numpy as jnp
from jax import lax
from jax.experimental import pallas as pl
from jax.experimental.pallas import tpu as pltpu
from jax.sharding import PartitionSpec as P

D = 1792
HEADS = 16
FEAT = 16
WIDTH = D // HEADS
LANES = 128
VMEM = 60 * 2**20
EPSILON = 1e-06
BOTH = ("seq", "head")
CORE, SIDE_X, SIDE_Y = 1, 2, 4

f32 = jnp.float32
bf16 = jnp.bfloat16


def grouped(value, multiple):
    return -(-value // multiple) * multiple


def cost(flops):
    return pl.CostEstimate(flops=int(flops), bytes_accessed=1, transcendentals=0)


def dot(left, right):
    return jnp.dot(left, right, preferred_element_type=f32)


def dot_rt(left, right):
    return lax.dot_general(left, right, (((1,), (1,)), ((), ())), preferred_element_type=f32)


def dot_lt(left, right):
    return lax.dot_general(left, right, (((0,), (0,)), ((), ())), preferred_element_type=f32)


def swap(block, bit, axis="seq"):
    devices = range(lax.axis_size(axis))
    return lax.ppermute(block, axis, [(i, i ^ bit) for i in devices])


def paired():
    return lax.axis_size("seq") == 8 and lax.axis_size("head") == 4


def tie(value, *others):
    return lax.optimization_barrier((value, others))[0]


def gather(shard):
    whole = lax.all_gather(shard, BOTH)
    return whole.reshape((lax.axis_size("seq"), lax.axis_size("head")) + shard.shape)


class Pieces:
    def __init__(self, shard):
        self.shard = shard
        self.columns = shard.shape[1]
        if paired():
            self.own = jnp.stack([shard] + [swap(shard, r, "head") for r in (1, 2, 3)])
        else:
            own = lax.all_gather(shard, "head")
            self.own = lax.all_gather(own, "seq", axis=1, tiled=True)
            self.pieces, self.offsets = [(self.own, 0)], jnp.zeros((1,), jnp.int32)

    def sides(self):
        if paired():
            self.by_x, self.by_y = swap(self.own, SIDE_X), swap(self.own, SIDE_Y)
            return self.by_x, self.by_y
        return ()

    def far(self):
        if not paired():
            return
        far_a, far_b = swap(self.by_x[:2], SIDE_Y), swap(self.by_y[2:], SIDE_X)
        mine = [(self.own, 0), (self.by_x, 0), (self.by_y, 0), (far_a, 0), (far_b, 2)]
        self.pieces = mine + [(swap(piece, CORE), start) for piece, start in mine]
        sides = (0, SIDE_X, SIDE_Y, SIDE_X | SIDE_Y, SIDE_X | SIDE_Y)
        sides = sides + tuple(side | CORE for side in sides)
        rows = self.shard.shape[0]
        self.offsets = (lax.axis_index("seq") ^ jnp.array(sides, jnp.int32)) * rows

    @property
    def places(self):
        return self.own.shape[0]

    def reorder(self, blocks):
        if not paired():
            return blocks
        here = lax.axis_index("head")
        pick = lambda r: lax.dynamic_index_in_dim(blocks, here ^ r, 0, keepdims=False)
        return jnp.stack([pick(r) for r in range(4)])

    def specs(self):
        def spec(piece, start):
            last = piece.shape[0] - 1
            return pl.BlockSpec(
                (1,) + piece.shape[1:], lambda z, o: (jnp.clip(z - start, 0, last), 0, 0)
            )

        return [spec(piece, start) for piece, start in self.pieces]

    def fill(self, offsets, refs, weight):
        z = pl.program_id(0)
        for i, (ref, (piece, start)) in enumerate(zip(refs, self.pieces)):
            count, rows, _ = piece.shape

            def put():
                at = pl.multiple_of(offsets[i], 16)
                weight[pl.ds(at, rows)] = ref[0]

            if count == self.places:
                put()
            else:
                pl.when((z >= start) & (z < start + count))(put)


def grad_kernel(first, plane, left0, left1, right0, right1, send, keep, rows0, rows1):
    _, width, tokens = left0.shape

    @pl.when((pl.program_id(0) == 0) & (pl.program_id(1) == 0))
    def _():
        for i in range(4):
            rows0[i * width : (i + 1) * width] = left0[plane[0] ^ i]
            rows1[i * width : (i + 1) * width] = left1[plane[0] ^ i]

    total = dot(rows0[...], right0[0, 0]) + dot(rows1[...], right1[0, 0])
    total = total.astype(bf16)
    far = first // 2
    near = 3 ^ far
    for i, at in enumerate((0, near)):
        keep[i, 0, 0] = total[at * width : (at + 1) * width]
        at ^= far
        send[i, 0, 0] = total[at * width : (at + 1) * width]


def weight_grads(plane, left0, left1, right0, right1, start, first):
    count, kinds, tokens, columns = right0.shape
    count //= 2
    width = left0.shape[1]
    left = pl.BlockSpec(left0.shape, lambda z, k, p: (0, 0, 0))
    right = pl.BlockSpec((1, 1, tokens, columns), lambda z, k, p: (z + start, k, 0, 0))
    out = pl.BlockSpec((2, 1, 1, width, columns), lambda z, k, p: (0, z, k, 0, 0))
    shape = jax.ShapeDtypeStruct((2, count, kinds, width, columns), bf16)
    return pl.pallas_call(
        functools.partial(grad_kernel, first),
        grid_spec=pltpu.PrefetchScalarGridSpec(
            num_scalar_prefetch=1,
            grid=(count, kinds),
            in_specs=[left, left, right, right],
            out_specs=[out, out],
            scratch_shapes=[pltpu.VMEM((4 * width, tokens), bf16)] * 2,
        ),
        out_shape=[shape, shape],
        compiler_params=pltpu.CompilerParams(vmem_limit_bytes=VMEM),
        cost_estimate=cost(count * kinds * 20 * width * tokens * columns),
    )(plane, left0, left1, right0, right1)


class Scatter:
    def __init__(self, left, right, relative=False):
        self.right = right
        self.left = left
        self.relative = relative
        if paired():
            rows = left.T.reshape(4, 2, D // 8, -1)
            core = lax.axis_index("seq") % 2
            pick = lambda c: lax.dynamic_index_in_dim(rows, c, 1, keepdims=False)
            self.left0, self.left1 = pick(core), swap(pick(1 - core), CORE)
            self.other = swap(right, CORE)

    def first(self):
        if not paired():
            return ()
        half = self.right.shape[0] // 2
        plane = (lax.axis_index("seq") // 2).reshape(1)
        self.kept, self.arrived = [], []
        made = []
        for start, side in ((0, SIDE_X), (half, SIDE_Y)):
            send, keep = weight_grads(
                plane, self.left0, self.left1, self.right, self.other, start, side
            )
            made.append(send)
            self.arrived.append(swap(send, side))
            self.kept.append(keep)
        self.coming = self.arrived
        return tuple(made)

    def second(self, *after):
        if not paired():
            return ()
        self.sums, made = [], []
        for keep, arrived, side in zip(self.kept, self.arrived, (SIDE_Y, SIDE_X)):
            if after:
                arrived = tie(arrived, *after)
            go = (keep[1].astype(f32) + arrived[1].astype(f32)).astype(bf16)
            stay = keep[0].astype(f32) + arrived[0].astype(f32)
            made.append(go)
            self.sums.append((stay, swap(go, side)))
        self.coming = [arrived for _, arrived in self.sums]
        return tuple(made)

    def pending(self):
        return tuple(self.coming) if paired() else ()

    def third(self, *after):
        if not paired():
            whole = jnp.einsum(
                "td,hktc->hkdc", self.left, self.right, preferred_element_type=f32
            ).astype(bf16)
            seq = lax.axis_size("seq")
            whole = whole.reshape(whole.shape[:2] + (seq, D // seq, -1))
            part = lax.psum_scatter(whole, "seq", scatter_dimension=2)
            self.total = lax.psum_scatter(part, "head", scatter_dimension=0)
            return ()
        sums = [(stay + arrived.astype(f32)).astype(bf16) for stay, arrived in self.sums]
        sums = jnp.concatenate(sums, axis=0)
        if after:
            sums = tie(sums, *after)
        here = lax.axis_index("head")
        if self.relative:
            pick = lambda r: sums[r]
        else:
            pick = lambda r: lax.dynamic_index_in_dim(sums, here ^ r, 0, keepdims=False)
        sent = [pick(r) for r in (1, 2, 3)]
        self.coming = [swap(block, r, "head") for r, block in zip((1, 2, 3), sent)]
        self.mine = pick(0)
        return tuple(sent)

    def finish(self, *after):
        if not paired():
            return self.total
        coming = self.coming
        if after:
            coming = [tie(block, *after) for block in coming]
        return sum([block.astype(f32) for block in coming], self.mine.astype(f32))


def whole_rows(ref, kind=0):
    block = ref[:, 0, kind]
    return block.reshape(D, block.shape[-1])


def weight_spec(weight, kinds=1, at=0):
    seq, _, _, _, columns = weight.shape
    return pl.BlockSpec((seq, 1, kinds, D // seq, columns), lambda z: (0, z, at, 0, 0))


def into_kernel(x_ref, w_ref, out_ref):
    out_ref[0] = dot(x_ref[...], whole_rows(w_ref)).astype(out_ref.dtype)


def into(x, weight, kind):
    count, columns = weight.shape[1], weight.shape[-1]
    tokens = x.shape[0]
    return pl.pallas_call(
        into_kernel,
        grid=(count,),
        in_specs=[
            pl.BlockSpec(x.shape, lambda z: (0, 0)),
            weight_spec(weight),
        ],
        out_specs=pl.BlockSpec((1, tokens, columns), lambda z: (z, 0, 0)),
        out_shape=jax.ShapeDtypeStruct((count, tokens, columns), kind),
        compiler_params=pltpu.CompilerParams(vmem_limit_bytes=VMEM),
        cost_estimate=cost(count * 3 * D * tokens * columns),
    )(x, weight)


def out_of_kernel(y_ref, w_ref, out_ref):
    @pl.when(pl.program_id(0) == 0)
    def _():
        out_ref[...] = jnp.zeros_like(out_ref)

    out_ref[...] += dot_rt(y_ref[0], whole_rows(w_ref))


def out_of(y, weight):
    count, tokens, columns = y.shape
    return pl.pallas_call(
        out_of_kernel,
        grid=(count,),
        in_specs=[
            pl.BlockSpec((1, tokens, columns), lambda z: (z, 0, 0)),
            weight_spec(weight),
        ],
        out_specs=pl.BlockSpec((tokens, D), lambda z: (0, 0)),
        out_shape=jax.ShapeDtypeStruct((tokens, D), f32),
        compiler_params=pltpu.CompilerParams(vmem_limit_bytes=VMEM),
        cost_estimate=cost(count * 3 * D * tokens * columns),
    )(y, weight)


def into_pieces_kernel(weights, offsets, x_ref, *refs):
    refs, (out_ref, weight) = refs[:-2], refs[-2:]
    weights.fill(offsets, refs, weight)
    out_ref[0] = dot(x_ref[...], weight[...]).astype(out_ref.dtype)


def into_pieces(x, weights, kind):
    count, columns = weights.places, weights.columns
    tokens = x.shape[0]
    return pl.pallas_call(
        functools.partial(into_pieces_kernel, weights),
        grid_spec=pltpu.PrefetchScalarGridSpec(
            num_scalar_prefetch=1,
            grid=(count,),
            in_specs=[pl.BlockSpec(x.shape, lambda z, o: (0, 0))] + weights.specs(),
            out_specs=pl.BlockSpec((1, tokens, columns), lambda z, o: (z, 0, 0)),
            scratch_shapes=[pltpu.VMEM((D, columns), bf16)],
        ),
        out_shape=jax.ShapeDtypeStruct((count, tokens, columns), kind),
        compiler_params=pltpu.CompilerParams(vmem_limit_bytes=VMEM),
        cost_estimate=cost(count * 3 * D * tokens * columns),
    )(weights.offsets, x, *[piece for piece, _ in weights.pieces])


def out_of_pieces_kernel(weights, offsets, y_ref, *refs):
    refs, (out_ref, weight) = refs[:-2], refs[-2:]
    weights.fill(offsets, refs, weight)

    @pl.when(pl.program_id(0) == 0)
    def _():
        out_ref[...] = jnp.zeros_like(out_ref)

    out_ref[...] += dot_rt(y_ref[0], weight[...])


def out_of_pieces(y, weights):
    count, tokens, columns = y.shape
    return pl.pallas_call(
        functools.partial(out_of_pieces_kernel, weights),
        grid_spec=pltpu.PrefetchScalarGridSpec(
            num_scalar_prefetch=1,
            grid=(count,),
            in_specs=[pl.BlockSpec((1, tokens, columns), lambda z, o: (z, 0, 0))]
            + weights.specs(),
            out_specs=pl.BlockSpec((tokens, D), lambda z, o: (0, 0)),
            scratch_shapes=[pltpu.VMEM((D, columns), bf16)],
        ),
        out_shape=jax.ShapeDtypeStruct((tokens, D), f32),
        compiler_params=pltpu.CompilerParams(vmem_limit_bytes=VMEM),
        cost_estimate=cost(count * 3 * D * tokens * columns),
    )(weights.offsets, y, *[piece for piece, _ in weights.pieces])


def ffn_kernel(x_ref, gu_ref, d_ref, slope_ref, silu_ref, hidden_ref, out_ref):
    @pl.when(pl.program_id(0) == 0)
    def _():
        out_ref[...] = jnp.zeros_like(out_ref)

    gate = dot(x_ref[...], whole_rows(gu_ref, 0))
    sig = jax.nn.sigmoid(gate)
    silu = gate * sig
    up = dot(x_ref[...], whole_rows(gu_ref, 1))
    hidden = (silu * up).astype(bf16)
    slope_ref[0] = (up * sig * (1.0 + gate * (1.0 - sig))).astype(bf16)
    silu_ref[0] = silu.astype(bf16)
    columns = hidden.shape[1]
    hidden_ref[0, 0, :, :columns] = hidden
    hidden_ref[0, 0, :, columns:] = jnp.zeros_like(hidden_ref[0, 0, :, columns:])
    out_ref[...] += dot_rt(hidden, whole_rows(d_ref))


def ffn(x, weight):
    count, columns = weight.shape[1], weight.shape[-1]
    padded = grouped(columns, LANES)
    tokens = x.shape[0]
    act = pl.BlockSpec((1, tokens, columns), lambda z: (z, 0, 0))
    kept = jax.ShapeDtypeStruct((count, tokens, columns), bf16)
    return pl.pallas_call(
        ffn_kernel,
        grid=(count,),
        in_specs=[
            pl.BlockSpec(x.shape, lambda z: (0, 0)),
            weight_spec(weight, kinds=2),
            weight_spec(weight, at=2),
        ],
        out_specs=[
            act,
            act,
            pl.BlockSpec((1, 1, tokens, padded), lambda z: (z, 0, 0, 0)),
            pl.BlockSpec((tokens, D), lambda z: (0, 0)),
        ],
        out_shape=[
            kept,
            kept,
            jax.ShapeDtypeStruct((count, 1, tokens, padded), bf16),
            jax.ShapeDtypeStruct((tokens, D), f32),
        ],
        compiler_params=pltpu.CompilerParams(vmem_limit_bytes=VMEM),
        cost_estimate=cost(count * 9 * D * tokens * columns),
    )(x, weight, weight)


def ffn_back_kernel(dy_ref, gu_ref, d_ref, slope_ref, silu_ref, grads_ref, out_ref):
    @pl.when(pl.program_id(0) == 0)
    def _():
        out_ref[...] = jnp.zeros_like(out_ref)

    grad_hidden = dot(dy_ref[...], whole_rows(d_ref))
    grad_gate = (grad_hidden * slope_ref[0].astype(f32)).astype(bf16)
    grad_up = (grad_hidden * silu_ref[0].astype(f32)).astype(bf16)
    columns = grad_gate.shape[1]
    grads_ref[0, 0, :, :columns] = grad_gate
    grads_ref[0, 1, :, :columns] = grad_up
    grads_ref[0, :, :, columns:] = jnp.zeros_like(grads_ref[0, :, :, columns:])
    out_ref[...] += dot_rt(grad_gate, whole_rows(gu_ref, 0)) + dot_rt(
        grad_up, whole_rows(gu_ref, 1)
    )


def ffn_back(dy, weight, slope, silu):
    count, columns = weight.shape[1], weight.shape[-1]
    padded = grouped(columns, LANES)
    tokens = dy.shape[0]
    act = pl.BlockSpec((1, tokens, columns), lambda z: (z, 0, 0))
    return pl.pallas_call(
        ffn_back_kernel,
        grid=(count,),
        in_specs=[
            pl.BlockSpec(dy.shape, lambda z: (0, 0)),
            weight_spec(weight, kinds=2),
            weight_spec(weight, at=2),
            act,
            act,
        ],
        out_specs=[
            pl.BlockSpec((1, 2, tokens, padded), lambda z: (z, 0, 0, 0)),
            pl.BlockSpec((tokens, D), lambda z: (0, 0)),
        ],
        out_shape=[
            jax.ShapeDtypeStruct((count, 2, tokens, padded), bf16),
            jax.ShapeDtypeStruct((tokens, D), f32),
        ],
        compiler_params=pltpu.CompilerParams(vmem_limit_bytes=VMEM),
        cost_estimate=cost(count * 9 * D * tokens * columns),
    )(dy, weight, weight, slope, silu)


def inverse_rms(rows):
    return lax.rsqrt(jnp.mean(rows * rows, axis=-1, keepdims=True) + EPSILON)


def norm_back(rows, scale, gain, grad):
    unit = rows * scale
    scaled = gain * grad
    return scale * (scaled - unit * jnp.mean(scaled * unit, axis=-1, keepdims=True))


class Layout:
    def __init__(self, batch, tokens):
        seq, head = lax.axis_size("seq"), lax.axis_size("head")
        self.batch, self.tokens, self.head = batch, tokens, head
        self.splits = min(seq // batch, HEADS // head)
        self.heads = HEADS // (head * self.splits)
        self.parts = seq // (batch * self.splits)
        self.inner = seq // self.parts
        self.v_cols, self.q_cols = self.heads * WIDTH, self.heads * FEAT
        self.width = grouped(self.v_cols + self.q_cols, LANES)
        self.sets = self.width // self.q_cols
        self.key_rows = grouped(tokens // self.sets, 16)
        self.length = tokens * seq * head
        count = self.inner * head
        self.groups = None
        if self.parts > 1:
            self.groups = [list(range(k * count, (k + 1) * count)) for k in range(self.parts)]
            self.mates = [[k * count + i for k in range(self.parts)] for i in range(count)]

    def sequence(self):
        return lax.rem(lax.axis_index("seq"), self.inner) // self.splits

    def pack_keys(self, keys):
        lead, each = keys.shape[:-2], self.tokens // self.sets
        keys = keys.reshape(lead + (self.sets, each, self.q_cols))
        keys = jnp.swapaxes(keys, -3, -2).reshape(lead + (each, self.width))
        return jnp.pad(keys, [(0, 0)] * len(lead) + [(0, self.key_rows - each), (0, 0)])

    def unpack_keys(self, rows):
        lead, each = rows.shape[:-2], self.tokens // self.sets
        rows = rows[..., :each, :].reshape(lead + (each, self.sets, self.q_cols))
        return jnp.swapaxes(rows, -3, -2).reshape(lead + (self.tokens, self.q_cols))

    def exchange(self, blocks):
        return lax.all_to_all(blocks, BOTH, 0, 0, tiled=True, axis_index_groups=self.groups)

    def all_parts(self, rows):
        if self.parts > 1:
            rows = lax.all_gather(rows, BOTH, axis=0, tiled=True, axis_index_groups=self.mates)
        return rows

    def own_part(self, blocks):
        if self.parts > 1:
            count = blocks.shape[0] // self.parts
            part = lax.axis_index("seq") // self.inner
            blocks = lax.dynamic_slice_in_dim(blocks, part * count, count, 0)
        return blocks


def fill_rows(lay, chunk, main, k_ref, values, queries, keys):
    ones = lax.broadcasted_iota(jnp.int32, (chunk, LANES - WIDTH), 1) < 2

    def turn(i, _):
        here = pl.ds(pl.multiple_of(i * chunk, chunk), chunk)
        rows, key_rows = main[here], k_ref[here]
        for h in range(lay.heads):
            values[h, here, :WIDTH] = rows[:, h * WIDTH : (h + 1) * WIDTH]
            values[h, here, WIDTH:] = ones.astype(f32).astype(bf16)
            at = lay.v_cols + h * FEAT
            queries[h, here] = rows[:, at : at + FEAT]
            keys[h, here] = key_rows[:, h * FEAT : (h + 1) * FEAT]
        return 0

    lax.fori_loop(0, lay.length // chunk, turn, 0)


def attend_kernel(
    lay, chunk, main, k_ref, seg_col, seg_row, out_ref, low_ref, values, queries, keys
):
    at = pl.program_id(0)

    @pl.when(at == 0)
    def _():
        fill_rows(lay, chunk, main, k_ref, values, queries, keys)

    mine = seg_col[...]
    rows = pl.ds(pl.multiple_of(at * chunk, chunk), chunk)
    out_ref[...] = jnp.zeros_like(out_ref)
    low_ref[...] = jnp.zeros_like(low_ref)
    for h in range(lay.heads):
        query = queries[h, rows]

        def weighted(j, causal):
            here = pl.ds(pl.multiple_of(j * chunk, chunk), chunk)
            scores = dot_rt(query, keys[h, here])
            allowed = mine == seg_row[j]
            if causal:
                later = lax.broadcasted_iota(jnp.int32, scores.shape, 0)
                allowed &= later >= lax.broadcasted_iota(jnp.int32, scores.shape, 1)
            weights = jnp.where(allowed, 1.0 + scores * (1.0 + 0.5 * scores), 0.0).astype(bf16)
            return dot(weights, values[h, here])

        total = lax.fori_loop(
            0, at, lambda j, acc: acc + weighted(j, False), jnp.zeros((chunk, LANES), f32)
        )
        total = total + weighted(at, True)
        norm = total[:, WIDTH : WIDTH + 1]
        attended = total[:, :WIDTH] / norm
        out_ref[:, h * WIDTH : (h + 1) * WIDTH] = attended
        out_ref[:, lay.v_cols + h : lay.v_cols + h + 1] = norm
        low_ref[:, h * WIDTH : (h + 1) * WIDTH] = attended.astype(bf16)


def attend(lay, main, keys, seg):
    length, width = main.shape
    chunk = min(512, length)
    steps = length // chunk
    part = pl.BlockSpec((chunk, width), lambda i: (i, 0))
    return pl.pallas_call(
        functools.partial(attend_kernel, lay, chunk),
        grid=(steps,),
        in_specs=[
            pl.BlockSpec((length, width), lambda i: (0, 0)),
            pl.BlockSpec((length, lay.q_cols), lambda i: (0, 0)),
            pl.BlockSpec((chunk, 1), lambda i: (i, 0)),
            pl.BlockSpec((steps, 1, chunk), lambda i: (0, 0, 0)),
        ],
        out_specs=[part, part],
        out_shape=[
            jax.ShapeDtypeStruct((length, width), f32),
            jax.ShapeDtypeStruct((length, width), bf16),
        ],
        scratch_shapes=[
            pltpu.VMEM((lay.heads, length, LANES), bf16),
            pltpu.VMEM((lay.heads, length, FEAT), bf16),
            pltpu.VMEM((lay.heads, length, FEAT), bf16),
        ],
        compiler_params=pltpu.CompilerParams(vmem_limit_bytes=VMEM),
        cost_estimate=cost(lay.heads * length * length * 12 * LANES),
    )(main, keys, seg.reshape(length, 1), seg.reshape(steps, 1, chunk))


def attend_back_kernel(
    lay,
    chunk,
    main,
    k_ref,
    kept,
    grad,
    seg_col,
    seg_row,
    out_ref,
    gk_ref,
    values,
    queries,
    keys,
    grad_n,
    grad_q,
):
    at = pl.program_id(0)
    steps = lay.length // chunk

    @pl.when(at == 0)
    def _():
        fill_rows(lay, chunk, main, k_ref, values, queries, keys)
        grad_q[...] = jnp.zeros_like(grad_q)

        def turn(i, _):
            here = pl.ds(pl.multiple_of(i * chunk, chunk), chunk)
            rows, low = kept[here], grad[here].astype(f32)
            for h in range(lay.heads):
                inverse = 1.0 / rows[:, lay.v_cols + h : lay.v_cols + h + 1]
                mine = low[:, h * WIDTH : (h + 1) * WIDTH]
                total = jnp.sum(
                    mine * rows[:, h * WIDTH : (h + 1) * WIDTH], axis=1, keepdims=True
                )
                total = -total * inverse
                high = total.astype(bf16)
                rest = (total - high.astype(f32)).astype(bf16)
                lane = lax.broadcasted_iota(jnp.int32, (chunk, LANES - WIDTH), 1)
                tail = jnp.where(lane == 0, high.astype(f32), 0.0)
                tail = jnp.where(lane == 1, rest.astype(f32), tail)
                grad_n[h, here, :WIDTH] = (mine * inverse).astype(bf16)
                grad_n[h, here, WIDTH:] = tail.astype(bf16)
            return 0

        lax.fori_loop(0, steps, turn, 0)

    mine = seg_col[...]
    rows = pl.ds(pl.multiple_of(at * chunk, chunk), chunk)
    for h in range(lay.heads):
        key, value = keys[h, rows], values[h, rows]
        key_t = key.astype(f32).T.astype(bf16)

        def turn(i, carry, causal):
            grad_k, grad_v = carry
            here = pl.ds(pl.multiple_of(i * chunk, chunk), chunk)
            query, grad_here = queries[h, here], grad_n[h, here]
            scores = dot_rt(key, query)
            allowed = mine == seg_row[i]
            if causal:
                key_at = lax.broadcasted_iota(jnp.int32, scores.shape, 0)
                allowed &= key_at <= lax.broadcasted_iota(jnp.int32, scores.shape, 1)
            weights = jnp.where(allowed, 1.0 + scores * (1.0 + 0.5 * scores), 0.0).astype(bf16)
            grad_s = dot_rt(value, grad_here) * (1.0 + scores)
            grad_s = jnp.where(allowed, grad_s, 0.0).astype(bf16)
            grad_q[h, :, here] += dot(key_t, grad_s)
            return grad_k + dot(grad_s, query), grad_v + dot(weights, grad_here)

        carry = (jnp.zeros((chunk, FEAT), f32), jnp.zeros((chunk, LANES), f32))
        carry = turn(at, carry, True)
        grad_k, grad_v = lax.fori_loop(at + 1, steps, lambda i, c: turn(i, c, False), carry)
        gk_ref[:, h * FEAT : (h + 1) * FEAT] = (0.5 * grad_k).astype(bf16)
        out_ref[rows, h * WIDTH : (h + 1) * WIDTH] = grad_v[:, :WIDTH].astype(bf16)

    @pl.when(at == steps - 1)
    def _():
        def turn(i, _):
            here = pl.ds(pl.multiple_of(i * chunk, chunk), chunk)
            for h in range(lay.heads):
                at = lay.v_cols + h * FEAT
                out_ref[here, at : at + FEAT] = (0.5 * grad_q[h, :, here].T).astype(bf16)
            return 0

        lax.fori_loop(0, steps, turn, 0)


def attend_back(lay, main, keys, kept, grad, seg):
    length, width = main.shape
    chunk = min(512, length)
    steps = length // chunk
    whole = pl.BlockSpec((length, width), lambda i: (0, 0))
    return pl.pallas_call(
        functools.partial(attend_back_kernel, lay, chunk),
        grid=(steps,),
        in_specs=[
            whole,
            pl.BlockSpec((length, lay.q_cols), lambda i: (0, 0)),
            whole,
            whole,
            pl.BlockSpec((chunk, 1), lambda i: (i, 0)),
            pl.BlockSpec((steps, 1, chunk), lambda i: (0, 0, 0)),
        ],
        out_specs=[whole, pl.BlockSpec((chunk, lay.q_cols), lambda i: (i, 0))],
        out_shape=[
            jax.ShapeDtypeStruct((length, width), bf16),
            jax.ShapeDtypeStruct((length, lay.q_cols), bf16),
        ],
        scratch_shapes=[
            pltpu.VMEM((lay.heads, length, LANES), bf16),
            pltpu.VMEM((lay.heads, length, FEAT), bf16),
            pltpu.VMEM((lay.heads, length, FEAT), bf16),
            pltpu.VMEM((lay.heads, length, LANES), bf16),
            pltpu.VMEM((lay.heads, FEAT, length), f32),
        ],
        compiler_params=pltpu.CompilerParams(vmem_limit_bytes=VMEM),
        cost_estimate=cost(lay.heads * length * length * 24 * LANES),
    )(main, keys, kept, grad, seg.reshape(length, 1), seg.reshape(steps, 1, chunk))


def earlier(rows, before, distance):
    moved = pltpu.roll(rows, distance, 0)
    place = lax.broadcasted_iota(jnp.int32, rows.shape, 0)
    for i in range(distance):
        at = 2 - distance + i
        moved = jnp.where(place == i, before[at : at + 1], moved)
    return moved


def later(rows, after, distance):
    count = rows.shape[0]
    moved = pltpu.roll(rows, count - distance, 0)
    place = lax.broadcasted_iota(jnp.int32, rows.shape, 0)
    for i in range(distance):
        moved = jnp.where(place == count - distance + i, after[i : i + 1], moved)
    return moved


def short_filter(taps, same, values, before):
    one_back = earlier(values, before, 1) * same[:, 0:1]
    two_back = earlier(values, before, 2) * same[:, 1:2]
    return taps[0:1] * values + taps[1:2] * one_back + taps[2:3] * two_back, one_back, two_back


def project_kernel(lay, x_ref, side_ref, same_ref, taps_ref, w_ref, main, k_ref, v_ref, f_ref, side_out):
    weight = whole_rows(w_ref)
    q_width = lay.splits * lay.q_cols
    v_at, f_at = 2 * q_width, 2 * q_width + lay.splits * lay.v_cols
    full = dot(x_ref[...], weight)
    side = dot(side_ref[...], weight)
    low = full[:, v_at:f_at].astype(bf16)
    v_ref[0] = low
    f_ref[0] = full[:, f_at:]
    side_v = side[:, v_at:f_at].astype(bf16).astype(f32)
    side_out[0, 0] = side_v
    side_out[0, 1] = side[:, f_at:]
    taps = taps_ref[0]
    for b in range(lay.batch):
        rows = slice(b * lay.tokens, (b + 1) * lay.tokens)
        pre = full[rows, f_at:]
        filtered, _, _ = short_filter(
            taps, same_ref[rows], low[rows].astype(f32), side_v[2 * b : 2 * b + 2]
        )
        mixed = filtered * (pre * jax.nn.sigmoid(pre))
        query = 0.5 * full[rows, :q_width].astype(bf16).astype(f32)
        key = 0.5 * full[rows, q_width:v_at].astype(bf16).astype(f32)
        for i in range(lay.splits):
            v_cols, q_cols = lay.v_cols, lay.q_cols
            main[b, i, 0, :, :v_cols] = mixed[:, i * v_cols : (i + 1) * v_cols].astype(bf16)
            q_here = query[:, i * q_cols : (i + 1) * q_cols].astype(bf16)
            main[b, i, 0, :, v_cols : v_cols + q_cols] = q_here
            k_ref[b, i, 0] = key[:, i * q_cols : (i + 1) * q_cols].astype(bf16)


def project(lay, x, side, same, taps, weight):
    tokens, head = x.shape[0], lay.head
    q_width, v_width = lay.splits * lay.q_cols, lay.splits * lay.v_cols
    columns = 2 * (q_width + v_width)
    beside = side.shape[0]
    to_all = lambda width: pl.BlockSpec(
        (lay.batch, lay.splits, 1, lay.tokens, width), lambda z: (0, 0, z, 0, 0)
    )
    shape = lambda width: jax.ShapeDtypeStruct(
        (lay.batch, lay.splits, head, lay.tokens, width), bf16
    )
    kept = pl.BlockSpec((1, tokens, v_width), lambda z: (z, 0, 0))
    return pl.pallas_call(
        functools.partial(project_kernel, lay),
        grid=(head,),
        in_specs=[
            pl.BlockSpec(x.shape, lambda z: (0, 0)),
            pl.BlockSpec(side.shape, lambda z: (0, 0)),
            pl.BlockSpec(same.shape, lambda z: (0, 0)),
            pl.BlockSpec((1, 3, v_width), lambda z: (z, 0, 0)),
            weight_spec(weight),
        ],
        out_specs=[
            to_all(lay.width),
            to_all(lay.q_cols),
            kept,
            kept,
            pl.BlockSpec((1, 2, beside, v_width), lambda z: (z, 0, 0, 0)),
        ],
        out_shape=[
            shape(lay.width),
            shape(lay.q_cols),
            jax.ShapeDtypeStruct((head, tokens, v_width), bf16),
            jax.ShapeDtypeStruct((head, tokens, v_width), f32),
            jax.ShapeDtypeStruct((head, 2, beside, v_width), f32),
        ],
        compiler_params=pltpu.CompilerParams(vmem_limit_bytes=VMEM),
        cost_estimate=cost(head * 3 * D * tokens * columns),
    )(x, side, same, taps, weight)


def project_back_kernel(
    lay, back_ref, gk_ref, v_ref, f_ref, side_ref, same_ref, taps_ref, out_ref, tap_ref, mixed, after
):
    q_width = lay.splits * lay.q_cols
    v_at, f_at = 2 * q_width, 2 * q_width + lay.splits * lay.v_cols
    v_cols, q_cols = lay.v_cols, lay.q_cols
    taps = taps_ref[0]
    below = lay.tokens + lay.key_rows
    tap_ref[...] = jnp.zeros_like(tap_ref)
    out_ref[0, :, q_width:v_at] = gk_ref[0]
    for b in range(lay.batch):
        rows = slice(b * lay.tokens, (b + 1) * lay.tokens)
        for i in range(lay.splits):
            block = back_ref[b, i, 0, : lay.tokens]
            mixed[:, i * v_cols : (i + 1) * v_cols] = block[:, :v_cols].astype(f32)
            out_ref[0, rows, i * q_cols : (i + 1) * q_cols] = block[:, v_cols : v_cols + q_cols]
            after[:, i * v_cols : (i + 1) * v_cols] = back_ref[
                b, i, 0, below : below + 16, :v_cols
            ].astype(f32)
        grad_mixed = mixed[...]
        pre = f_ref[0, rows]
        sig = jax.nn.sigmoid(pre)
        values = v_ref[0, rows].astype(f32)
        same = same_ref[rows]
        at = 2 * b
        filtered, one_back, two_back = short_filter(
            taps, same, values, side_ref[0, 0, at : at + 2]
        )
        grad = grad_mixed * pre * sig
        at = 2 * (lay.batch + b)
        pre_after = side_ref[0, 1, at : at + 2]
        grad_after = after[0:2] * pre_after * jax.nn.sigmoid(pre_after)
        grad_v = (
            taps[0:1] * grad
            + taps[1:2] * later(grad, grad_after, 1) * same[:, 2:3]
            + taps[2:3] * later(grad, grad_after, 2) * same[:, 3:4]
        )
        out_ref[0, rows, v_at:f_at] = grad_v.astype(bf16)
        grad_f = grad_mixed * filtered * sig * (1.0 + pre * (1.0 - sig))
        out_ref[0, rows, f_at:] = grad_f.astype(bf16)
        for k, term in enumerate((values, one_back, two_back)):
            tap_ref[0, k : k + 1] += jnp.sum(grad * term, axis=0, keepdims=True)


def project_back(lay, back, grad_keys, values, pre, side, same, taps):
    head, tokens, v_width = values.shape
    columns = 2 * (lay.splits * lay.q_cols + v_width)
    kept = pl.BlockSpec((1, tokens, v_width), lambda z: (z, 0, 0))
    return pl.pallas_call(
        functools.partial(project_back_kernel, lay),
        grid=(head,),
        in_specs=[
            pl.BlockSpec(
                (lay.batch, lay.splits, 1) + back.shape[3:], lambda z: (0, 0, z, 0, 0)
            ),
            pl.BlockSpec((1,) + grad_keys.shape[1:], lambda z: (z, 0, 0)),
            kept,
            kept,
            pl.BlockSpec((1,) + side.shape[1:], lambda z: (z, 0, 0, 0)),
            pl.BlockSpec(same.shape, lambda z: (0, 0)),
            pl.BlockSpec((1, 3, v_width), lambda z: (z, 0, 0)),
        ],
        out_specs=[
            pl.BlockSpec((1, tokens, columns), lambda z: (z, 0, 0)),
            pl.BlockSpec((1, 3, v_width), lambda z: (z, 0, 0)),
        ],
        out_shape=[
            jax.ShapeDtypeStruct((head, tokens, columns), bf16),
            jax.ShapeDtypeStruct((head, 3, v_width), f32),
        ],
        scratch_shapes=[
            pltpu.VMEM((lay.tokens, v_width), f32),
            pltpu.VMEM((16, v_width), f32),
        ],
        compiler_params=pltpu.CompilerParams(vmem_limit_bytes=VMEM),
        cost_estimate=cost(head * 2500 * tokens * columns),
    )(back, grad_keys, values, pre, side, same, taps)


def shift(block, distance):
    devices = range(lax.axis_size("seq") * lax.axis_size("head"))
    return lax.ppermute(
        block, BOTH, [(i, i + distance) for i in devices if i + distance in devices]
    )


def local(
    tokens,
    cotangent,
    segment_ids,
    query_weight,
    key_weight,
    value_weight,
    filter_weight,
    out_weight,
    gate_weight,
    up_weight,
    down_weight,
    norm_gain,
    ffn_gain,
    conv_taps,
):
    seq, head = lax.axis_size("seq"), lax.axis_size("head")
    batch, span, _ = tokens.shape
    count = batch * span
    length = segment_ids.shape[1] * seq
    place = lax.axis_index("seq") * head + lax.axis_index("head")
    heads_here = HEADS // head
    qk_width, v_width = heads_here * FEAT, heads_here * WIDTH
    ff_width = gate_weight.shape[1]

    lay = Layout(batch, span)
    out_pad = grouped(v_width, LANES) - v_width
    first = jnp.concatenate([query_weight, key_weight, value_weight, filter_weight], axis=1)
    rows_here, columns = first.shape
    small = [norm_gain, ffn_gain, conv_taps.reshape(-1), segment_ids.astype(bf16).reshape(-1)]
    ends = [0]
    for part in small:
        ends.append(ends[-1] + part.size)
    below = grouped(-(-ends[-1] // columns), 16)
    small = jnp.pad(jnp.concatenate(small), (0, below * columns - ends[-1]))
    first_w = gather(jnp.concatenate([first, small.reshape(below, columns)])[None])
    out_w = Pieces(jnp.pad(out_weight.T, ((0, 0), (0, out_pad))))
    out_w.sides()
    out_w.far()
    ffn_w = gather(jnp.stack([gate_weight, up_weight, down_weight]))
    beside = jnp.concatenate([shift(tokens[:, -2:], 1), shift(tokens[:, :2], -1)], axis=0)

    small = first_w[:, :, 0, rows_here:].reshape(seq, head, -1).astype(f32)
    part = lambda i: small[:, :, ends[i] : ends[i + 1]]
    gain_one, gain_two = part(0)[:, 0].reshape(1, D), part(1)[:, 0].reshape(1, D)
    taps = jnp.transpose(part(2).reshape(seq, head, 3, -1), (1, 2, 0, 3))
    taps = taps.reshape(head, 3, v_width)
    segs = jnp.swapaxes(part(3)[:, 0].reshape(seq, batch, -1), 0, 1).reshape(batch, length)
    x = tokens.reshape(count, D).astype(f32)
    cot_low = cotangent.reshape(count, D)

    def normed_of(rows):
        scale = inverse_rms(rows)
        return scale, (rows * scale * gain_one).astype(bf16)

    scale_one, normed = normed_of(x)
    _, normed_beside = normed_of(beside.reshape(-1, D).astype(f32))
    around = lax.dynamic_slice(
        jnp.pad(segs, ((0, 0), (2, 2)), constant_values=-1.0),
        (0, place * span),
        (batch, span + 4),
    )
    seg_here = around[:, 2:-2]
    others = (around[:, 1:-3], around[:, :-4], around[:, 3:-1], around[:, 4:])
    same = jnp.stack([(seg_here == other).astype(f32) for other in others], axis=-1)
    same = same.reshape(count, 4)
    normed = tie(normed, *[piece for piece, _ in out_w.pieces])
    main, keys, v_low, filter_pre, side = project(lay, normed, normed_beside, same, taps, first_w)
    arrived = jnp.concatenate([main, lay.pack_keys(keys)], axis=3)
    arrived = lay.exchange(arrived.reshape(-1, span + lay.key_rows, lay.width))
    main = lay.all_parts(arrived[:, :span].reshape(-1, lay.width))
    keys = lay.all_parts(lay.unpack_keys(arrived[:, span:]).reshape(-1, lay.q_cols))
    my_seg = lax.dynamic_index_in_dim(segs, lay.sequence(), 0, keepdims=False)
    attended, sent = attend(lay, main, keys, my_seg)
    arrived = lay.exchange(lay.own_part(sent.reshape(-1, span, lay.width)))

    def side_by_side(blocks, width):
        blocks = blocks.reshape(batch, lay.splits, head, span, -1)[..., :width]
        blocks = [blocks[:, i] for i in range(lay.splits)]
        return jnp.swapaxes(jnp.concatenate(blocks, axis=-1), 0, 1).reshape(head, count, -1)

    att_low = side_by_side(arrived, lay.v_cols)
    out_wide = lambda rows: jnp.pad(rows, ((0, 0), (0, 0), (0, out_pad)))
    att_low = out_w.reorder(out_wide(att_low))

    residual = x + out_of_pieces(att_low, out_w)
    scale_two = inverse_rms(residual)
    normed_two = (residual * scale_two * gain_two).astype(bf16)
    slope, silu, hidden, ffn_out = ffn(normed_two, ffn_w)
    layer_output = (residual + ffn_out).astype(bf16).reshape(tokens.shape)

    down_sum = Scatter(cot_low, hidden)
    grads_gu, back_two = ffn_back(cot_low, ffn_w, slope, silu)
    gate_up_sum = Scatter(normed_two, grads_gu)
    down_sends = down_sum.first()
    gain_two_grad = jnp.sum(back_two * residual * scale_two, axis=0)
    grad_residual = cot_low.astype(f32) + norm_back(residual, scale_two, gain_two, back_two)
    grad_res_low = grad_residual.astype(bf16)
    out_sum = Scatter(grad_res_low, att_low[:, None], True)

    grad_att = out_w.reorder(into_pieces(grad_res_low, out_w, bf16))
    sent = jnp.stack(
        [
            grad_att[..., i * lay.v_cols : (i + 1) * lay.v_cols].reshape(head, batch, span, -1)
            for i in range(lay.splits)
        ]
    )
    sent = jnp.pad(sent, [(0, 0)] * 4 + [(0, lay.width - lay.v_cols)])
    sent = jnp.transpose(sent, (2, 0, 1, 3, 4)).reshape(-1, span, lay.width)
    arrived = lay.exchange(tie(sent, *down_sends))
    gate_up_sends = gate_up_sum.first()
    out_sends = out_sum.first()
    grad_rows = lay.all_parts(arrived.reshape(-1, lay.width))
    grad_rows = tie(grad_rows, *gate_up_sends, *out_sends, *down_sum.pending())
    down_sends = down_sum.second()
    grad_rows = tie(grad_rows, *down_sends)
    grad_main, grad_keys = attend_back(lay, main, keys, attended, grad_rows, my_seg)
    grad_main = tie(grad_main, *gate_up_sum.pending(), *out_sum.pending(), *down_sum.pending())
    blocks = grad_main.reshape(-1, span, lay.width)
    ahead = jnp.pad(blocks[1:, :16], ((0, 1), (0, 0), (0, 0)))
    packed = lay.pack_keys(grad_keys.reshape(-1, span, lay.q_cols))
    sent = jnp.concatenate([blocks, packed, ahead], axis=1)
    arrived = lay.exchange(lay.own_part(sent))
    gate_up_sum.second(grad_main)
    out_sum.second(grad_main)
    arrived = tie(arrived, *gate_up_sum.pending(), *out_sum.pending())
    gate_up_sends = gate_up_sum.third(arrived)
    down_sends = down_sum.third(arrived)
    out_sends = out_sum.third(arrived)
    arrived = tie(arrived, *gate_up_sends, *out_sends, *down_sends)

    grad_keys = lay.unpack_keys(arrived[:, span : span + lay.key_rows])
    grad_keys = side_by_side(grad_keys, lay.q_cols)
    arrived = arrived.reshape((batch, lay.splits, head) + arrived.shape[1:])
    grad_first, tap_grads = project_back(
        lay, arrived, grad_keys, v_low, filter_pre, side, same, taps
    )
    tap_grads = jnp.swapaxes(tap_grads, 0, 1).reshape(3, D)
    first_sum = Scatter(normed, grad_first[:, None])
    first_sends = first_sum.first()
    back_one = out_of(tie(grad_first, *first_sends), first_w)
    gain_one_grad = jnp.sum(back_one * x * scale_one, axis=0)
    first_sends = first_sum.second(back_one)
    first_sum.third()
    gate_up_grad = gate_up_sum.finish(*first_sends)
    down_grad = down_sum.finish(*first_sends)
    out_grad = out_sum.finish(*first_sends)
    first_grad = first_sum.finish()[0].astype(f32)
    grad_x = (grad_residual + norm_back(x, scale_one, gain_one, back_one)).astype(bf16)
    tokens_grad = grad_x.reshape(tokens.shape)

    small = jnp.concatenate([jnp.stack([gain_one_grad, gain_two_grad]), tap_grads], axis=0)
    small = jnp.swapaxes(small.reshape(5, head * seq, -1), 0, 1)
    small = lax.all_to_all(small, ("head", "seq"), 0, 0, tiled=True)
    small = jnp.sum(small, axis=0)

    q_end, k_end, v_end = qk_width, 2 * qk_width, 2 * qk_width + v_width
    return (
        layer_output,
        tokens_grad,
        first_grad[:, :q_end],
        first_grad[:, q_end:k_end],
        first_grad[:, k_end:v_end],
        first_grad[:, v_end:],
        out_grad[0][:, :v_width].astype(f32).T,
        gate_up_grad[0][:, :ff_width].astype(f32),
        gate_up_grad[1][:, :ff_width].astype(f32),
        down_grad[0][:, :ff_width].astype(f32),
        small[0],
        small[1],
        small[2:],
    )


def solution(mesh):
    rows = P(None, BOTH, None)
    return jax.shard_map(
        local,
        mesh=mesh,
        in_specs=(
            rows,
            rows,
            P(None, "seq"),
            P("seq", "head"),
            P("seq", "head"),
            P("seq", "head"),
            P("seq", "head"),
            P("head", "seq"),
            P("seq", "head"),
            P("seq", "head"),
            P("seq", "head"),
            P("seq"),
            P("seq"),
            P(None, ("head", "seq")),
        ),
        out_specs=(
            rows,
            rows,
            P("seq", "head"),
            P("seq", "head"),
            P("seq", "head"),
            P("seq", "head"),
            P("head", "seq"),
            P("seq", "head"),
            P("seq", "head"),
            P("seq", "head"),
            P(("head", "seq")),
            P(("head", "seq")),
            P(None, ("head", "seq")),
        ),
        check_vma=False,
    )
```

time: 2650 us -> 1270 us (0.48)
  waiting for transfers between devices: 1630 us -> 648 us
  matrix products: 533 us -> 0 us
  Pallas kernels: 0 us -> 352 us
  blocking collectives: 114 us -> 0 us
  other arithmetic: 176 us -> 93.3 us
  local copies, waits for them, and re-layouts: 142 us -> 71.8 us
  starting transfers between devices: 18.4 us -> 85.4 us
    psum x2 -> x0, waiting for transfers between devices: 709 us -> none  [the longest x1 475 us: local(): mixed_sum = lax.psum(attention_terms, 'head')]
    dot_general x80 -> x0, matrix products: 533 us -> none  [the longest x46 294 us: dot_float(): return jnp.dot(left, right, preferred_element_type=jnp.float32)]
    reduce_scatter x12 -> x0, waiting for transfers between devices: 361 us -> none  [the longest x2 140 us: local(): lax.psum_scatter(back_one_terms.reshape(per_micro, seq_count, D).astype(j...]
    pallas_call x0 -> x17, Pallas kernels: none -> 352 us  [the longest x1 91 us: attend_back(): pl.pallas_call(functools.partial(attend_back_kernel, lay, chunk), grid=(s...]
    ppermute x6 -> x50, waiting for transfers between devices: 0.02 us -> 290 us  [the longest x48 290 us: swap(): return lax.ppermute(block, axis, [(i, i ^ bit) for i in devices])]
    all_to_all x0 -> x5, waiting for transfers between devices: none -> 252 us  [the longest x4 203 us: exchange(): lax.all_to_all(blocks, BOTH, 0, 0, tiled=True, axis_index_groups=self.gro...]
    unnamed x48 -> x2, waiting for transfers between devices: 246 us -> 0.03 us
    all_gather x14 -> x2, waiting for transfers between devices: 318 us -> 106 us  [gather(): whole = lax.all_gather(shard, BOTH)]
  transfers between devices with their start and end apart: 44 -> 57, of which waited for: 26 -> 20; matrix products, arithmetic and copies ran while one was open for 28% -> 11% of each run, Pallas kernels for 0% -> 24%
where the time goes in v1:
time: 1270 us
  waiting for transfers between devices  648 us (51%)
  Pallas kernels  352 us (28%)
  other arithmetic  93.3 us (7%)
  starting transfers between devices  85.4 us (7%)
  local copies, waits for them, and re-layouts  71.8 us (6%)
  between operations  15.3 us (1%)
    ppermute x48, waiting for transfers between devices, swap(): return lax.ppermute(block, axis, [(i, i ^ bit) for i in devices])  290 us
    all_to_all x4, waiting for transfers between devices, exchange(): lax.all_to_all(blocks, BOTH, 0, 0, tiled=True, axis_index_groups=self.gro...  203 us
    all_gather x2, waiting for transfers between devices, gather(): whole = lax.all_gather(shard, BOTH)  106 us
    pallas_call x1, Pallas kernels, attend_back(): pl.pallas_call(functools.partial(attend_back_kernel, lay, chunk), grid=(s...  91 us
    pallas_call x8, Pallas kernels, weight_grads(): pl.pallas_call(functools.partial(grad_kernel, first), grid_spec=pltpu.Pre...  72.2 us
    ppermute x48, starting transfers between devices, swap(): return lax.ppermute(block, axis, [(i, i ^ bit) for i in devices])  53.8 us
    all_to_all x1, waiting for transfers between devices, local(): small = lax.all_to_all(small, ('head', 'seq'), 0, 0, tiled=True)  49 us
    pallas_call x1, Pallas kernels, ffn_back(): pl.pallas_call(ffn_back_kernel, grid=(count,), in_specs=[pl.BlockSpec(dy....  45.5 us
  transfers between devices with their start and end apart: 57, of which 20 were waited for; matrix products, arithmetic and copies ran while one was open for 11% of the time, Pallas kernels for 24%

profile of v1, /device:TPU:0, one launch (start us, length us, event | category | flops | bytes accessed | tf_op | source)
XLA Modules:
  0.0 1266.2 jit_solution(6889905801016510501)
XLA Ops:
  27.4 23.5 %collective-permute-done.1 = bf16[224,512]{1,0:T(8,128)(2,1)S(1)} collective-permute-done((bf16[224,512]{1,0:T(8,128)(2,1)S(1)}, bf16[224,512]{1,0:T(8,128)(2,1)S(1)}, u32[]{:S(2)}, u32[]{:S(2)}) %collective-permute-start.1) | collective-permute-done | bytes 229408 | tf_op jit(solution)/shard_map/ppermute | solution.py:46
  60.5 26.4 %collective-permute-done.3.refs_1_ = bf16[4,224,512]{2,1,0:T(8,128)(2,1)S(1)} collective-permute-done((bf16[4,224,512]{2,1,0:T(8,128)(2,1)S(1)}, bf16[4,224,512]{2,1,0:T(8,128)(2,1)S(1)}, u32[]{:S(2)}, u32[]{:S(2)}) %collective-permute-start.3) | collective-permute-done | bytes 917536 | tf_op jit(solution)/shard_map/ppermute | solution.py:46
  100.0 50.3 %all-gather.5.cloned.1.call-done = bf16[7680,1024]{1,0:T(8,128)(2,1)} async-done(((bf16[240,1024]{1,0:T(8,128)(2,1)}), bf16[7680,1024]{1,0:T(8,128)(2,1)}) %all-gather.5.cloned.1.call-update) | async-done | bytes 15728656 | tf_op jit(solution)/shard_map/all_gather | solution.py:58
  165.2 15.5 %shard_map.246 = (bf16[4,2,4,128,256]{4,3,2,1,0:T(8,128)(2,1)}, bf16[4,2,4,128,32]{4,3,2,1,0:T(8,128)(2,1)}, bf16[4,512,448]{2,1,0:T(8,128)(2,1)}, f32[4,512,448]{2,1,0:T(8,128)}, f32[4,2,16,448]{3,2,1,0:T(8,128)}) custom-call(bf16[512,1792]{1,0:T(8,128)(2,1)} %fusion.8.x_ref, bf16[16,1792]{1,0:T(8,128)(2,1)} %multiply_convert_fusion.1.side_ref, ...), custom_call_target="tpu_custom_call" | custom-call | flops 11274289152 | bytes 1 | tf_op jit(solution)/shard_map/pallas_call | solution.py:774
  192.5 104.5 %all-to-all-done = bf16[32,144,256]{2,1,0:T(8,128)(2,1)} async-done(((bf16[32,144,256]{2,1,0:T(8,128)(2,1)}), bf16[32,144,256]{2,1,0:T(8,128)(2,1)}, u32[]{:S(2)}, u32[]{:S(2)}) %all-to-all-start) | async-done | bytes 2359328 | tf_op jit(solution)/shard_map/all_to_all | solution.py:492
  302.8 43.9 %shard_map.247 = (f32[4096,256]{1,0:T(8,128)}, bf16[4096,256]{1,0:T(8,128)(2,1)}) custom-call(bf16[4096,256]{1,0:T(8,128)(2,1)} %bitcast.326, bf16[4096,32]{1,0:T(8,128)(2,1)} %bitcast.338, f32[4096,1]{1,0:T(8,128)} %copy.237.seg_col, f32[8,1,512]{2,1,0:T(1,128)} %bitcast.364), custom_call_target="tpu_custom_call" | custom-call | flops 51539607552 | bytes 1 | tf_op jit(solution)/shard_map/pallas_call | solution.py:566
  346.7 9.3 all-to-all-start.1
  356.5 98.2 %all-to-all-done.1 = bf16[32,128,256]{2,1,0:T(8,128)(2,1)} async-done(((bf16[32,128,256]{2,1,0:T(8,128)(2,1)}), bf16[32,128,256]{2,1,0:T(8,128)(2,1)}, u32[]{:S(2)}, u32[]{:S(2)}) %all-to-all-start.1) | async-done | bytes 2097184 | tf_op jit(solution)/shard_map/all_to_all | solution.py:492
  460.5 10.2 shard_map.248
  476.7 55.9 %all-gather.7.cloned.1.call-done = bf16[96,224,1216]{2,1,0:T(8,128)(2,1)} async-done(((bf16[3,224,1216]{2,1,0:T(8,128)(2,1)}), bf16[96,224,1216]{2,1,0:T(8,128)(2,1)}) %all-gather.7.cloned.1.call-update) | async-done | bytes 52297744 | tf_op jit(solution)/shard_map/all_gather | solution.py:58
  532.6 38.6 %shard_map.249 = (bf16[4,512,1216]{2,1,0:T(8,128)(2,1)}, bf16[4,512,1216]{2,1,0:T(8,128)(2,1)}, bf16[4,1,512,1280]{3,2,1,0:T(8,128)(2,1)}, f32[512,1792]{1,0:T(8,128)}) custom-call(bf16[512,1792]{1,0:T(8,128)(2,1)} %multiply_convert_fusion.x_ref, bf16[8,4,3,224,1216]{4,3,2,1,0:T(8,128)(2,1)} %bitcast.366, bf16[8,4,3,224,1216]{4,3,2,1,0:T(8,128)(2,1)} %bitcast.367), custom_call_target="tpu_custom_call" | custom-call | flops 40164655104 | bytes 1 | tf_op jit(solution)/shard_map/pallas_call | solution.py:378
  571.6 45.5 %shard_map.250 = (bf16[4,2,512,1280]{3,2,1,0:T(8,128)(2,1)}, f32[512,1792]{1,0:T(8,128)}) custom-call(bf16[512,1792]{1,0:T(8,128)(2,1)} %bitcast.300, bf16[8,4,3,224,1216]{4,3,2,1,0:T(8,128)(2,1)} %bitcast.368, bf16[8,4,3,224,1216]{4,3,2,1,0:T(8,128)(2,1)} %bitcast.369, bf16[4,512,1216]{2,1,0:T(8,128)(2,1)} %get-tuple-element.77.slope_ref, ...), custom_call_target="tpu_custom_call" | custom-call | flops 40164655104 | bytes 1 | tf_op jit(solution)/shard_map/pallas_call | solution.py:425
  636.0 9.1 shard_map.253
  655.7 9.1 shard_map.252
  666.2 9.7 shard_map.251
  684.0 25.3 %collective-permute-done.21 = bf16[2,2,1,224,1280]{4,3,1,2,0:T(8,128)(2,1)} collective-permute-done((bf16[2,2,1,224,1280]{4,3,1,2,0:T(8,128)(2,1)}, bf16[2,2,1,224,1280]{4,3,1,2,0:T(8,128)(2,1)}, u32[]{:S(2)}, u32[]{:S(2)}) %collective-permute-start.21) | collective-permute-done | bytes 2293792 | tf_op jit(solution)/shard_map/ppermute | solution.py:46
  724.6 10.0 collective-permute-done.20
  737.7 27.1 %collective-permute-done.27 = bf16[2,1,224,1280]{3,2,0,1:T(8,128)(2,1)} collective-permute-done((bf16[2,1,224,1280]{3,2,0,1:T(8,128)(2,1)S(1)}, bf16[2,1,224,1280]{3,2,0,1:T(8,128)(2,1)}, u32[]{:S(2)}, u32[]{:S(2)}) %collective-permute-start.27) | collective-permute-done | bytes 1146912 | tf_op jit(solution)/shard_map/ppermute | solution.py:46
  767.4 14.1 %shard_map.254 = (bf16[2,2,2,224,1280]{4,3,2,1,0:T(8,128)(2,1)}, bf16[2,2,2,224,1280]{4,3,2,1,0:T(8,128)(2,1)}) custom-call(s32[1]{0:T(128)} %bitcast.34.plane, bf16[4,224,512]{2,1,0:T(8,128)(2,1)} %get-tuple-element.238.left0, bf16[4,224,512]{2,1,0:T(8,128)(2,1)} %collective-permute-done.16.left1, bf16[4,2,512,1280]{3,2,1,0:T(8,128)(2,1)} %get-tuple-element.85.right0, ...), custom_call_target="tpu_custom_call" | custom-call | flops 11744051200 | bytes 1 | tf_op jit(solution)/shard_map/pallas_call | solution.py:152
  783.0 14.2 %shard_map.255 = (bf16[2,2,2,224,1280]{4,3,2,1,0:T(8,128)(2,1)}, bf16[2,2,2,224,1280]{4,3,2,1,0:T(8,128)(2,1)}) custom-call(s32[1]{0:T(128)} %bitcast.34.plane, bf16[4,224,512]{2,1,0:T(8,128)(2,1)} %get-tuple-element.238.left0, bf16[4,224,512]{2,1,0:T(8,128)(2,1)} %collective-permute-done.16.left1, bf16[4,2,512,1280]{3,2,1,0:T(8,128)(2,1)} %get-tuple-element.85.right0, ...), custom_call_target="tpu_custom_call" | custom-call | flops 11744051200 | bytes 1 | tf_op jit(solution)/shard_map/pallas_call | solution.py:152
  798.7 91.0 %shard_map.258 = (bf16[4096,256]{1,0:T(8,128)(2,1)}, bf16[4096,32]{1,0:T(8,128)(2,1)}) custom-call(bf16[4096,256]{1,0:T(8,128)(2,1)} %bitcast.327, bf16[4096,32]{1,0:T(8,128)(2,1)} %bitcast.339, f32[4096,256]{1,0:T(8,128)} %get-tuple-element.80.kept, bf16[4096,256]{1,0:T(8,128)(2,1)} %bitcast.39.grad, f32[4096,1]{1,0:T(8,128)} %copy.237.seg_col, ...), custom_call_target="tpu_custom_call" | custom-call | flops 103079215104 | bytes 1 | tf_op jit(solution)/shard_map/pallas_call | solution.py:680
  919.0 76.0 %collective-permute-done.31 = bf16[2,1,224,512]{3,2,0,1:T(8,128)(2,1)S(1)} collective-permute-done((bf16[2,1,224,512]{3,2,0,1:T(8,128)(2,1)S(1)}, bf16[2,1,224,512]{3,2,0,1:T(8,128)(2,1)S(1)}, u32[]{:S(2)}, u32[]{:S(2)}) %collective-permute-start.31) | collective-permute-done | bytes 458784 | tf_op jit(solution)/shard_map/ppermute | solution.py:46
  1014.2 11.8 shard_map.259
  1037.1 7.7 shard_map.260
  1044.8 7.8 shard_map.261
  1052.6 13.5 %shard_map.262 = f32[512,1792]{1,0:T(8,128)} custom-call(bf16[4,512,1024]{2,1,0:T(8,128)(2,1)} %get-tuple-element.116.y_ref, bf16[8,4,1,240,1024]{4,3,2,1,0:T(8,128)(2,1)} %bitcast.361), custom_call_target="tpu_custom_call" | custom-call | flops 11274289152 | bytes 1 | tf_op jit(solution)/shard_map/pallas_call | solution.py:287
  1077.5 8.7 fusion.13
  1086.2 49.0 %all-to-all-done.4 = f32[32,1,280]{2,1,0:T(1,128)S(1)} async-done(((f32[32,1,280]{2,1,0:T(1,128)}), f32[32,1,280]{2,1,0:T(1,128)S(1)}, u32[]{:S(2)}, u32[]{:S(2)}) %all-to-all-start.4) | async-done | bytes 35872 | tf_op jit(solution)/shard_map/all_to_all | solution.py:1042
  1159.5 26.2 %collective-permute-done.42 = bf16[1,224,512]{2,1,0:T(8,128)(2,1)S(1)} collective-permute-done((bf16[1,224,512]{2,1,0:T(8,128)(2,1)}, bf16[1,224,512]{2,1,0:T(8,128)(2,1)S(1)}, u32[]{:S(2)}, u32[]{:S(2)}) %collective-permute-start.42) | collective-permute-done | bytes 229408 | tf_op jit(solution)/shard_map/ppermute | solution.py:46
  1188.8 20.7 %collective-permute-done.48 = bf16[1,224,1280]{2,1,0:T(8,128)(2,1)} collective-permute-done((bf16[1,224,1280]{2,1,0:T(8,128)(2,1)}, bf16[1,224,1280]{2,1,0:T(8,128)(2,1)}, u32[]{:S(2)}, u32[]{:S(2)}) %collective-permute-start.48) | collective-permute-done | bytes 573472 | tf_op jit(solution)/shard_map/ppermute | solution.py:46
  1222.9 8.1 collective-permute-done.40
  1231.1 25.0 %collective-permute-done.39 = bf16[1,224,1024]{2,1,0:T(8,128)(2,1)S(1)} collective-permute-done((bf16[1,224,1024]{2,1,0:T(8,128)(2,1)S(1)}, bf16[1,224,1024]{2,1,0:T(8,128)(2,1)S(1)}, u32[]{:S(2)}, u32[]{:S(2)}) %collective-permute-start.39) | collective-permute-done | bytes 458784 | tf_op jit(solution)/shard_map/ppermute | solution.py:46
  (340 shorter events, 265.0 us)
Async XLA Ops:
  7.2 143.1 %all-gather.5.cloned.1.call-start = ((), (), s32[]{:S(2)}) async-start(), calls=%async_computation.5 | async-start | bytes 16220160 | tf_op jit(solution)/shard_map/all_gather | solution.py:58
  14.1 518.6 %all-gather.7.cloned.1.call-start = ((), (), s32[]{:S(2)}) async-start(), calls=%async_computation.6 | async-start | bytes 56770560 | tf_op jit(solution)/shard_map/all_gather | solution.py:58
  91.6 68.8 %collective-permute-start.7 = (bf16[4,224,512]{2,1,0:T(8,128)(2,1)S(1)}, bf16[4,224,512]{2,1,0:T(8,128)(2,1)}, u32[]{:S(2)}, u32[]{:S(2)}) collective-permute-start(bf16[4,224,512]{2,1,0:T(8,128)(2,1)S(1)} %pad_maximum_fusion.6.refs_0_), channel_id=1, source_target_pairs={{0,4},{4,0},{8,12},{12,8},{16,20},{20,16},{24,28},{28,24},{1,5},{5... | collective-permute-start | bytes 2752520 | tf_op jit(solution)/shard_map/ppermute | solution.py:46
  91.7 68.8 %collective-permute-start.8 = (bf16[4,224,512]{2,1,0:T(8,128)(2,1)}, bf16[4,224,512]{2,1,0:T(8,128)(2,1)}, u32[]{:S(2)}, u32[]{:S(2)}) collective-permute-start(bf16[4,224,512]{2,1,0:T(8,128)(2,1)} %copy-done.23), channel_id=1, source_target_pairs={{0,4},{4,0},{8,12},{12,8},{16,20},{20,16},{24,28},{28,24},{1,5},{5... | collective-permute-start | bytes 2752520 | tf_op jit(solution)/shard_map/ppermute | solution.py:46
  92.2 68.3 %collective-permute-start.9 = (bf16[4,224,512]{2,1,0:T(8,128)(2,1)}, bf16[4,224,512]{2,1,0:T(8,128)(2,1)}, u32[]{:S(2)}, u32[]{:S(2)}) collective-permute-start(bf16[4,224,512]{2,1,0:T(8,128)(2,1)} %copy-done.24), channel_id=1, source_target_pairs={{0,4},{4,0},{8,12},{12,8},{16,20},{20,16},{24,28},{28,24},{1,5},{5... | collective-permute-start | bytes 2752520 | tf_op jit(solution)/shard_map/ppermute | solution.py:46
  97.7 62.8 %collective-permute-start.10 = (bf16[2,224,512]{2,1,0:T(8,128)(2,1)}, bf16[2,224,512]{2,1,0:T(8,128)(2,1)S(1)}, u32[]{:S(2)}, u32[]{:S(2)}) collective-permute-start(bf16[2,224,512]{2,1,0:T(8,128)(2,1)} %collective-permute-done.5.refs_3_), channel_id=1, source_target_pairs={{0,4},{4,0},{8,12},{12,8},{16,20},{20,16},{24,28},{28,24},{1,5},{5... | collective-permute-start | bytes 1376264 | tf_op jit(solution)/shard_map/ppermute | solution.py:46
  100.0 61.2 %collective-permute-start.11 = (bf16[2,224,512]{2,1,0:T(8,128)(2,1)}, bf16[2,224,512]{2,1,0:T(8,128)(2,1)}, u32[]{:S(2)}, u32[]{:S(2)}) collective-permute-start(bf16[2,224,512]{2,1,0:T(8,128)(2,1)} %collective-permute-done.6.refs_4_), channel_id=1, source_target_pairs={{0,4},{4,0},{8,12},{12,8},{16,20},{20,16},{24,28},{28,24},{1,5},{5... | collective-permute-start | bytes 1376264 | tf_op jit(solution)/shard_map/ppermute | solution.py:46
  186.1 110.9 %all-to-all-start = ((bf16[32,144,256]{2,1,0:T(8,128)(2,1)}), bf16[32,144,256]{2,1,0:T(8,128)(2,1)}, u32[]{:S(2)}, u32[]{:S(2)}) async-start(bf16[32,144,256]{2,1,0:T(8,128)(2,1)} %pad_maximum_fusion.1), calls=%async_computation | async-start | bytes 4718592 | tf_op jit(solution)/shard_map/all_to_all | solution.py:492
  346.7 108.1 %all-to-all-start.1 = ((bf16[32,128,256]{2,1,0:T(8,128)(2,1)}), bf16[32,128,256]{2,1,0:T(8,128)(2,1)}, u32[]{:S(2)}, u32[]{:S(2)}) async-start(bf16[32,128,256]{2,1,0:T(8,128)(2,1)} %bitcast.328), calls=%async_computation.1 | async-start | bytes 4194304 | tf_op jit(solution)/shard_map/all_to_all | solution.py:492
  571.3 64.8 %collective-permute-start.15 = (bf16[4,1,512,1280]{3,2,1,0:T(8,128)(2,1)}, bf16[4,1,512,1280]{3,2,1,0:T(8,128)(2,1)}, u32[]{:S(2)}, u32[]{:S(2)}) collective-permute-start(bf16[4,1,512,1280]{3,2,1,0:T(8,128)(2,1)} %get-tuple-element.81.right0), channel_id=1, source_target_pairs={{0,4},{4,0},{8,12},{12,8},{16,20},{20,16},{24,28},{28,24},{1,5},{5... | collective-permute-start | bytes 15728648 | tf_op jit(solution)/shard_map/ppermute | solution.py:46
  617.1 150.3 %collective-permute-start.17 = (bf16[4,2,512,1280]{3,2,1,0:T(8,128)(2,1)}, bf16[4,2,512,1280]{3,2,1,0:T(8,128)(2,1)}, u32[]{:S(2)}, u32[]{:S(2)}) collective-permute-start(bf16[4,2,512,1280]{3,2,1,0:T(8,128)(2,1)} %get-tuple-element.85.right0), channel_id=1, source_target_pairs={{0,4},{4,0},{8,12},{12,8},{16,20},{20,16},{24,28},{28,24},{1,5},{5... | collective-permute-start | bytes 31457288 | tf_op jit(solution)/shard_map/ppermute | solution.py:46
  627.3 85.2 %collective-permute-start.19 = (bf16[4,1,512,512]{3,2,1,0:T(8,128)(2,1)}, bf16[4,1,512,512]{3,2,1,0:T(8,128)(2,1)}, u32[]{:S(2)}, u32[]{:S(2)}) collective-permute-start(bf16[4,1,512,512]{3,2,1,0:T(8,128)(2,1)} %get-tuple-element.216.right0), channel_id=1, source_target_pairs={{0,4},{4,0},{8,12},{12,8},{16,20},{20,16},{24,28},{28,24},{1,5},{5... | collective-permute-start | bytes 6291464 | tf_op jit(solution)/shard_map/ppermute | solution.py:46
  645.1 64.2 %collective-permute-start.21 = (bf16[2,2,1,224,1280]{4,3,1,2,0:T(8,128)(2,1)}, bf16[2,2,1,224,1280]{4,3,1,2,0:T(8,128)(2,1)}, u32[]{:S(2)}, u32[]{:S(2)}) collective-permute-start(bf16[2,2,1,224,1280]{4,3,1,2,0:T(8,128)(2,1)} %bitcast.374), channel_id=1, source_target_pairs={{0,16},{4,20},{8,24},{12,28},{16,0},{20,4},{24,8},{28,12},{1,17},{... | collective-permute-start | bytes 6881288 | tf_op jit(solution)/shard_map/ppermute | solution.py:46
  664.8 69.8 %collective-permute-start.20 = (bf16[2,2,1,224,1280]{4,3,1,2,0:T(8,128)(2,1)}, bf16[2,2,1,224,1280]{4,3,1,2,0:T(8,128)(2,1)}, u32[]{:S(2)}, u32[]{:S(2)}) collective-permute-start(bf16[2,2,1,224,1280]{4,3,1,2,0:T(8,128)(2,1)} %bitcast.373), channel_id=1, source_target_pairs={{0,8},{4,12},{8,0},{12,4},{16,24},{20,28},{24,16},{28,20},{1,9},{5... | collective-permute-start | bytes 6881288 | tf_op jit(solution)/shard_map/ppermute | solution.py:46
  680.4 118.3 %all-to-all-start.2 = ((bf16[32,128,256]{2,1,0:T(8,128)(2,1)}), bf16[32,128,256]{2,1,0:T(8,128)(2,1)}, u32[]{:S(2)}, u32[]{:S(2)}) async-start(bf16[32,128,256]{2,1,0:T(8,128)(2,1)} %bitcast.33), calls=%async_computation.2 | async-start | bytes 4194304 | tf_op jit(solution)/shard_map/all_to_all | solution.py:492
  717.6 175.0 %collective-permute-start.24 = (bf16[2,2,1,224,512]{4,3,1,2,0:T(8,128)(2,1)}, bf16[2,2,1,224,512]{4,3,1,2,0:T(8,128)(2,1)}, u32[]{:S(2)}, u32[]{:S(2)}) collective-permute-start(bf16[2,2,1,224,512]{4,3,1,2,0:T(8,128)(2,1)} %bitcast.377), channel_id=1, source_target_pairs={{0,8},{4,12},{8,0},{12,4},{16,24},{20,28},{24,16},{28,20},{1,9},{5... | collective-permute-start | bytes 2752520 | tf_op jit(solution)/shard_map/ppermute | solution.py:46
  734.6 158.0 %collective-permute-start.25 = (bf16[2,2,1,224,512]{4,3,1,2,0:T(8,128)(2,1)}, bf16[2,2,1,224,512]{4,3,1,2,0:T(8,128)(2,1)}, u32[]{:S(2)}, u32[]{:S(2)}) collective-permute-start(bf16[2,2,1,224,512]{4,3,1,2,0:T(8,128)(2,1)} %bitcast.378), channel_id=1, source_target_pairs={{0,16},{4,20},{8,24},{12,28},{16,0},{20,4},{24,8},{28,12},{1,17},{... | collective-permute-start | bytes 2752520 | tf_op jit(solution)/shard_map/ppermute | solution.py:46
  764.8 127.8 %collective-permute-start.26 = (bf16[2,1,224,1280]{3,2,0,1:T(8,128)(2,1)}, bf16[2,1,224,1280]{3,2,0,1:T(8,128)(2,1)S(1)}, u32[]{:S(2)}, u32[]{:S(2)}) collective-permute-start(bf16[2,1,224,1280]{3,2,0,1:T(8,128)(2,1)} %fusion.31), channel_id=1, source_target_pairs={{0,16},{4,20},{8,24},{12,28},{16,0},{20,4},{24,8},{28,12},{1,17},{... | collective-permute-start | bytes 3440648 | tf_op jit(solution)/shard_map/ppermute | solution.py:46
  781.5 111.1 %collective-permute-start.22 = (bf16[2,2,2,224,1280]{4,3,2,1,0:T(8,128)(2,1)}, bf16[2,2,2,224,1280]{4,3,2,1,0:T(8,128)(2,1)}, u32[]{:S(2)}, u32[]{:S(2)}) collective-permute-start(bf16[2,2,2,224,1280]{4,3,2,1,0:T(8,128)(2,1)} %get-tuple-element.86), channel_id=1, source_target_pairs={{0,8},{4,12},{8,0},{12,4},{16,24},{20,28},{24,16},{28,20},{1,9},{5... | collective-permute-start | bytes 13762568 | tf_op jit(solution)/shard_map/ppermute | solution.py:46
  797.3 100.0 %collective-permute-start.23 = (bf16[2,2,2,224,1280]{4,3,2,1,0:T(8,128)(2,1)}, bf16[2,2,2,224,1280]{4,3,2,1,0:T(8,128)(2,1)}, u32[]{:S(2)}, u32[]{:S(2)}) collective-permute-start(bf16[2,2,2,224,1280]{4,3,2,1,0:T(8,128)(2,1)} %get-tuple-element.87), channel_id=1, source_target_pairs={{0,16},{4,20},{8,24},{12,28},{16,0},{20,4},{24,8},{28,12},{1,17},{... | collective-permute-start | bytes 13762568 | tf_op jit(solution)/shard_map/ppermute | solution.py:46
  901.2 104.2 %all-to-all-start.3 = ((bf16[32,160,256]{2,1,0:T(8,128)(2,1)}), bf16[32,160,256]{2,1,0:T(8,128)(2,1)}, u32[]{:S(2)}, u32[]{:S(2)}) async-start(bf16[32,160,256]{2,1,0:T(8,128)(2,1)} %fusion.17), calls=%async_computation.3 | async-start | bytes 5242880 | tf_op jit(solution)/shard_map/all_to_all | solution.py:492
  907.9 89.5 %collective-permute-start.29 = (bf16[2,2,224,1280]{3,2,1,0:T(8,128)(2,1)S(1)}, bf16[2,2,224,1280]{3,2,1,0:T(8,128)(2,1)S(1)}, u32[]{:S(2)}, u32[]{:S(2)}) collective-permute-start(bf16[2,2,224,1280]{3,2,1,0:T(8,128)(2,1)S(1)} %fusion.19), channel_id=1, source_target_pairs={{0,8},{4,12},{8,0},{12,4},{16,24},{20,28},{24,16},{28,20},{1,9},{5... | collective-permute-start | bytes 6881288 | tf_op jit(solution)/shard_map/ppermute | solution.py:46
  913.6 86.6 %collective-permute-start.28 = (bf16[2,2,224,1280]{3,2,1,0:T(8,128)(2,1)S(1)}, bf16[2,2,224,1280]{3,2,1,0:T(8,128)(2,1)S(1)}, u32[]{:S(2)}, u32[]{:S(2)}) collective-permute-start(bf16[2,2,224,1280]{3,2,1,0:T(8,128)(2,1)S(1)} %fusion.18), channel_id=1, source_target_pairs={{0,16},{4,20},{8,24},{12,28},{16,0},{20,4},{24,8},{28,12},{1,17},{... | collective-permute-start | bytes 6881288 | tf_op jit(solution)/shard_map/ppermute | solution.py:46
  916.3 78.6 %collective-permute-start.31 = (bf16[2,1,224,512]{3,2,0,1:T(8,128)(2,1)S(1)}, bf16[2,1,224,512]{3,2,0,1:T(8,128)(2,1)S(1)}, u32[]{:S(2)}, u32[]{:S(2)}) collective-permute-start(bf16[2,1,224,512]{3,2,0,1:T(8,128)(2,1)S(1)} %fusion.46), channel_id=1, source_target_pairs={{0,8},{4,12},{8,0},{12,4},{16,24},{20,28},{24,16},{28,20},{1,9},{5... | collective-permute-start | bytes 1376264 | tf_op jit(solution)/shard_map/ppermute | solution.py:46
  918.3 77.9 %collective-permute-start.30 = (bf16[2,1,224,512]{3,2,0,1:T(8,128)(2,1)S(1)}, bf16[2,1,224,512]{3,2,0,1:T(8,128)(2,1)S(1)}, u32[]{:S(2)}, u32[]{:S(2)}) collective-permute-start(bf16[2,1,224,512]{3,2,0,1:T(8,128)(2,1)S(1)} %fusion.45), channel_id=1, source_target_pairs={{0,16},{4,20},{8,24},{12,28},{16,0},{20,4},{24,8},{28,12},{1,17},{... | collective-permute-start | bytes 1376264 | tf_op jit(solution)/shard_map/ppermute | solution.py:46
  1031.5 114.1 %collective-permute-start.46 = (bf16[2,224,1280]{2,1,0:T(8,128)(2,1)}, bf16[2,224,1280]{2,1,0:T(8,128)(2,1)}, u32[]{:S(2)}, u32[]{:S(2)}) collective-permute-start(bf16[2,224,1280]{2,1,0:T(8,128)(2,1)} %get-tuple-element.206), channel_id=1, source_target_pairs={{0,3},{1,2},{2,1},{3,0},{4,7},{5,6},{6,5},{7,4},{8,11},{9,10},{10,... | collective-permute-start | bytes 3440648 | tf_op jit(solution)/shard_map/ppermute | solution.py:46
  1035.4 111.9 %collective-permute-start.45 = (bf16[2,224,1280]{2,1,0:T(8,128)(2,1)}, bf16[2,224,1280]{2,1,0:T(8,128)(2,1)}, u32[]{:S(2)}, u32[]{:S(2)}) collective-permute-start(bf16[2,224,1280]{2,1,0:T(8,128)(2,1)} %get-tuple-element.207), channel_id=1, source_target_pairs={{0,2},{1,3},{2,0},{3,1},{4,6},{5,7},{6,4},{7,5},{8,10},{9,11},{10,... | collective-permute-start | bytes 3440648 | tf_op jit(solution)/shard_map/ppermute | solution.py:46
  1035.4 114.6 %collective-permute-start.44 = (bf16[2,224,1280]{2,1,0:T(8,128)(2,1)}, bf16[2,224,1280]{2,1,0:T(8,128)(2,1)}, u32[]{:S(2)}, u32[]{:S(2)}) collective-permute-start(bf16[2,224,1280]{2,1,0:T(8,128)(2,1)} %get-tuple-element.208), channel_id=1, source_target_pairs={{0,1},{1,0},{2,3},{3,2},{4,5},{5,4},{6,7},{7,6},{8,9},{9,8},{10,11... | collective-permute-start | bytes 3440648 | tf_op jit(solution)/shard_map/ppermute | solution.py:46
  1066.1 71.6 %collective-permute-start.34 = (bf16[2,2,1,224,1024]{4,3,1,2,0:T(8,128)(2,1)}, bf16[2,2,1,224,1024]{4,3,1,2,0:T(8,128)(2,1)}, u32[]{:S(2)}, u32[]{:S(2)}) collective-permute-start(bf16[2,2,1,224,1024]{4,3,1,2,0:T(8,128)(2,1)} %bitcast.376), channel_id=1, source_target_pairs={{0,8},{4,12},{8,0},{12,4},{16,24},{20,28},{24,16},{28,20},{1,9},{5... | collective-permute-start | bytes 5505032 | tf_op jit(solution)/shard_map/ppermute | solution.py:46
  1066.2 74.3 %collective-permute-start.36 = (bf16[2,2,1,224,1024]{4,3,1,2,0:T(8,128)(2,1)}, bf16[2,2,1,224,1024]{4,3,1,2,0:T(8,128)(2,1)}, u32[]{:S(2)}, u32[]{:S(2)}) collective-permute-start(bf16[2,2,1,224,1024]{4,3,1,2,0:T(8,128)(2,1)} %bitcast.375), channel_id=1, source_target_pairs={{0,16},{4,20},{8,24},{12,28},{16,0},{20,4},{24,8},{28,12},{1,17},{... | collective-permute-start | bytes 5505032 | tf_op jit(solution)/shard_map/ppermute | solution.py:46
  1072.0 63.3 %all-to-all-start.4 = ((f32[32,1,280]{2,1,0:T(1,128)}), f32[32,1,280]{2,1,0:T(1,128)S(1)}, u32[]{:S(2)}, u32[]{:S(2)}) async-start(f32[32,1,280]{2,1,0:T(1,128)} %reshape.718), calls=%async_computation.4 | async-start | bytes 98304 | tf_op jit(solution)/shard_map/all_to_all | solution.py:1042
  1150.0 59.5 %collective-permute-start.48 = (bf16[1,224,1280]{2,1,0:T(8,128)(2,1)}, bf16[1,224,1280]{2,1,0:T(8,128)(2,1)}, u32[]{:S(2)}, u32[]{:S(2)}) collective-permute-start(bf16[1,224,1280]{2,1,0:T(8,128)(2,1)} %get-tuple-element.214), channel_id=1, source_target_pairs={{0,2},{1,3},{2,0},{3,1},{4,6},{5,7},{6,4},{7,5},{8,10},{9,11},{10,... | collective-permute-start | bytes 1720328 | tf_op jit(solution)/shard_map/ppermute | solution.py:46
  (71 other events, 2143.2 us)
Sparse Core Ops, SparseCore 0:
  14.2 136.0 all-gather.4
  153.1 379.4 all-gather.6

commit v2 on v1

v2 whole, which is shorter than its diff:
```python
import functools

import jax
import jax.numpy as jnp
from jax import lax
from jax.experimental import pallas as pl
from jax.experimental.pallas import tpu as pltpu
from jax.sharding import PartitionSpec as P

D = 1792
HEADS = 16
FEAT = 16
WIDTH = D // HEADS
LANES = 128
VMEM = 60 * 2**20
EPSILON = 1e-06
BOTH = ("seq", "head")
CORE, SIDE_X, SIDE_Y = 1, 2, 4

f32 = jnp.float32
bf16 = jnp.bfloat16
MESH = pl.DeviceIdType.MESH


def grouped(value, multiple):
    return -(-value // multiple) * multiple


def cost(flops):
    return pl.CostEstimate(flops=int(flops), bytes_accessed=1, transcendentals=0)


def dot(left, right):
    return jnp.dot(left, right, preferred_element_type=f32)


def dot_rt(left, right):
    return lax.dot_general(left, right, (((1,), (1,)), ((), ())), preferred_element_type=f32)


def dot_lt(left, right):
    return lax.dot_general(left, right, (((0,), (0,)), ((), ())), preferred_element_type=f32)


def swap(block, bit, axis="seq"):
    devices = range(lax.axis_size(axis))
    return lax.ppermute(block, axis, [(i, i ^ bit) for i in devices])


def paired():
    return lax.axis_size("seq") == 8 and lax.axis_size("head") == 4


def tie(value, *others):
    return lax.optimization_barrier((value, others))[0]


def gather(shard):
    whole = lax.all_gather(shard, BOTH)
    return whole.reshape((lax.axis_size("seq"), lax.axis_size("head")) + shard.shape)


def by_place(blocks):
    if not paired():
        return blocks
    here = lax.axis_index("head")
    if blocks.ndim == 1:
        return blocks ^ here
    pick = lambda r: lax.dynamic_index_in_dim(blocks, here ^ r, 0, keepdims=False)
    return jnp.stack([pick(r) for r in range(4)])


def flipped(here, bit):
    return here + bit - 2 * bit * ((here // bit) % 2)


def gather_kernel(shard, edge, *refs):
    count = (len(refs) - 9) // 2
    others, (whole, edges), rest = refs[:count], refs[count : count + 2], refs[count + 2 :]
    lined, (send, recv, local, line_send, line_recv, edge_send, edge_recv) = (
        rest[:count],
        rest[count:],
    )
    place, line = lax.axis_index("seq"), lax.axis_index("head")
    seq, head = lax.axis_size("seq"), lax.axis_size("head")
    lines = [line, flipped(line, 1), flipped(line, 2), 3 - line]
    by_x, by_y, by_core = (flipped(place, bit) for bit in (SIDE_X, SIDE_Y, CORE))
    corner = flipped(by_x, SIDE_Y)
    to = lambda at, z: {"seq": at, "head": z}
    linear = place * head + line
    after, before = (linear + 1) % (seq * head), (linear + seq * head - 1) % (seq * head)
    sides = [to(at // head, at % head) for at in (after, before)]
    partners = [to(place, z) for z in lines[1:]] + [to(at, line) for at in (by_x, by_y, by_core)]
    partners += sides

    barrier = pltpu.get_barrier_semaphore()
    for partner in partners:
        pl.semaphore_signal(barrier, inc=1, device_id=partner, device_id_type=MESH)
    pl.semaphore_wait(barrier, len(partners))

    def remote(source, target, send_sem, recv_sem, partner):
        return pltpu.make_async_remote_copy(
            src_ref=source,
            dst_ref=target,
            send_sem=send_sem,
            recv_sem=recv_sem,
            device_id=partner,
            device_id_type=MESH,
        )

    copies = [pltpu.make_async_copy(shard, whole.at[place, line, 0], local.at[0])]
    copies += [
        pltpu.make_async_copy(other, target.at[0], local.at[1 + i])
        for i, (other, target) in enumerate(zip(others, lined))
    ]
    started = {}

    def start(row, r, source, at, z, partner):
        started[row, r] = remote(
            source, whole.at[at, z, 0], send.at[row, r], recv.at[row, r], partner
        )
        started[row, r].start()

    for r in (1, 2, 3):
        start(0, r, shard, place, line, to(place, lines[r]))
    copies += [
        remote(edge, edges.at[i], edge_send.at[i], edge_recv.at[i], partner)
        for i, partner in enumerate(sides)
    ]
    for each in copies:
        each.start()
    for r in range(4):
        if r > 0:
            started[0, r].wait_recv()
        source = shard if r == 0 else whole.at[place, lines[r], 0]
        start(1, r, source, place, lines[r], to(by_x, line))
        start(2, r, source, place, lines[r], to(by_y, line))
        start(3, r, source, place, lines[r], to(by_core, line))
    more = [
        remote(other, target.at[r], line_send.at[i, r], line_recv.at[i, r], to(place, lines[r]))
        for i, (other, target) in enumerate(zip(others, lined))
        for r in (1, 2, 3)
    ]
    for each in more:
        each.start()
    for r in range(4):
        z = lines[r]
        started[1, r].wait_recv()
        if r < 2:
            start(4, r, whole.at[by_x, z, 0], by_x, z, to(by_y, line))
        start(5, r, whole.at[by_x, z, 0], by_x, z, to(by_core, line))
        started[2, r].wait_recv()
        if r >= 2:
            start(4, r, whole.at[by_y, z, 0], by_y, z, to(by_x, line))
        start(6, r, whole.at[by_y, z, 0], by_y, z, to(by_core, line))
    for r in range(4):
        z = lines[r]
        started[4, r].wait_recv()
        start(7, r, whole.at[corner, z, 0], corner, z, to(by_core, line))
    for (row, r), each in started.items():
        each.wait_send()
        if row in (3, 5, 6, 7):
            each.wait_recv()
    for each in copies + more:
        each.wait()


def gather_first(shard, edge, others):
    seq, head = lax.axis_size("seq"), lax.axis_size("head")
    if not paired():
        return gather(shard[None]), jnp.stack([shift(edge, 1), shift(edge, -1)]), [None] * len(others)
    anywhere = pl.BlockSpec(memory_space=pl.ANY)
    count = len(others)
    dma = pltpu.SemaphoreType.DMA
    whole, edges, *lined = pl.pallas_call(
        gather_kernel,
        in_specs=[anywhere] * (2 + count),
        out_specs=[anywhere] * (2 + count),
        out_shape=[
            jax.ShapeDtypeStruct((seq, head, 1) + shard.shape, bf16),
            jax.ShapeDtypeStruct((2,) + edge.shape, bf16),
        ]
        + [jax.ShapeDtypeStruct((head,) + other.shape, bf16) for other in others],
        scratch_shapes=[
            dma((8, 4)),
            dma((8, 4)),
            dma((1 + count,)),
            dma((count, 4)),
            dma((count, 4)),
            dma((2,)),
            dma((2,)),
        ],
        compiler_params=pltpu.CompilerParams(collective_id=0, has_side_effects=True),
        cost_estimate=cost(100e9),
    )(shard, edge, *others)
    return whole, edges, lined


class Pieces:
    def __init__(self, shard, own=None):
        self.shard = shard
        self.columns = shard.shape[1]
        self.order = by_place(jnp.arange(lax.axis_size("head"), dtype=jnp.int32))
        if paired():
            if own is None:
                own = jnp.stack([shard] + [swap(shard, r, "head") for r in (1, 2, 3)])
            self.own = own
        else:
            own = lax.all_gather(shard, "head")
            self.own = lax.all_gather(own, "seq", axis=1, tiled=True)
            self.pieces, self.offsets = [(self.own, 0)], jnp.zeros((1,), jnp.int32)

    def sides(self, *after):
        if paired():
            own = tie(self.own, *after) if after else self.own
            self.by_x, self.by_y = swap(own, SIDE_X), swap(own, SIDE_Y)
            return self.by_x, self.by_y
        return ()

    def far(self, *after):
        if not paired():
            return
        by_x, by_y = self.by_x[:2], self.by_y[2:]
        if after:
            by_x, by_y = tie(by_x, *after), tie(by_y, *after)
        far_a, far_b = swap(by_x, SIDE_Y), swap(by_y, SIDE_X)
        mine = [(self.own, 0), (self.by_x, 0), (self.by_y, 0), (far_a, 0), (far_b, 2)]
        self.pieces = mine + [(swap(piece, CORE), start) for piece, start in mine]
        sides = (0, SIDE_X, SIDE_Y, SIDE_X | SIDE_Y, SIDE_X | SIDE_Y)
        sides = sides + tuple(side | CORE for side in sides)
        rows = self.shard.shape[0]
        self.offsets = (lax.axis_index("seq") ^ jnp.array(sides, jnp.int32)) * rows

    @property
    def places(self):
        return self.own.shape[0]

    def specs(self):
        def spec(piece, start):
            last = piece.shape[0] - 1
            return pl.BlockSpec(
                (1,) + piece.shape[1:], lambda z, o, p: (jnp.clip(z - start, 0, last), 0, 0)
            )

        return [spec(piece, start) for piece, start in self.pieces]

    def fill(self, offsets, refs, weight):
        z = pl.program_id(0)
        for i, (ref, (piece, start)) in enumerate(zip(refs, self.pieces)):
            count, rows, _ = piece.shape

            def put():
                at = pl.multiple_of(offsets[i], 16)
                weight[pl.ds(at, rows)] = ref[0]

            if count == self.places:
                put()
            else:
                pl.when((z >= start) & (z < start + count))(put)


def grad_kernel(first, plane, left0, left1, right0, right1, send, keep, rows0, rows1):
    _, width, tokens = left0.shape

    @pl.when(pl.program_id(0) == 0)
    def _():
        for i in range(4):
            rows0[i * width : (i + 1) * width] = left0[plane[0] ^ i]
            rows1[i * width : (i + 1) * width] = left1[plane[0] ^ i]

    total = dot(rows0[...], right0[0, 0]) + dot(rows1[...], right1[0, 0])
    total = total.astype(bf16)
    far = first // 2
    near = 3 ^ far
    for i, at in enumerate((0, near)):
        keep[i, 0] = total[at * width : (at + 1) * width]
        at ^= far
        send[i, 0] = total[at * width : (at + 1) * width]


def weight_grads(plane, left0, left1, right0, right1, kind, start, first, light):
    count, _, tokens, columns = right0.shape
    count //= 2
    width = left0.shape[1]
    left = pl.BlockSpec(left0.shape, lambda z, p: (0, 0, 0))
    right = pl.BlockSpec((1, 1, tokens, columns), lambda z, p: (z + start, kind, 0, 0))
    out = pl.BlockSpec((2, 1, width, columns), lambda z, p: (0, z, 0, 0))
    shape = jax.ShapeDtypeStruct((2, count, width, columns), bf16)
    return pl.pallas_call(
        functools.partial(grad_kernel, first),
        grid_spec=pltpu.PrefetchScalarGridSpec(
            num_scalar_prefetch=1,
            grid=(count,),
            in_specs=[left, left, right, right],
            out_specs=[out, out],
            scratch_shapes=[pltpu.VMEM((4 * width, tokens), bf16)] * 2,
        ),
        out_shape=[shape, shape],
        compiler_params=pltpu.CompilerParams(vmem_limit_bytes=VMEM),
        cost_estimate=cost(1 if light else count * 20 * width * tokens * columns),
    )(plane, left0, left1, right0, right1)


class Left:
    def __init__(self, rows):
        self.rows = rows
        if paired():
            blocks = rows.T.reshape(4, 2, D // 8, -1)
            core = lax.axis_index("seq") % 2
            pick = lambda c: lax.dynamic_index_in_dim(blocks, c, 1, keepdims=False)
            self.near, self.far = pick(core), swap(pick(1 - core), CORE)

    def pending(self):
        return (self.far,) if paired() else ()


class Scatter:
    def __init__(self, left, right, relative=False, other=None, kind=0):
        self.right = right
        self.left = left
        self.relative = relative
        self.kind = kind
        if paired():
            self.other = swap(right, CORE) if other is None else other

    def given(self):
        return (self.other,) + self.left.pending() if paired() else ()

    def other_side(self):
        return (self.other,) if paired() else (None,)

    def first(self):
        made = self.products()
        self.go()
        return made

    def products(self, light=False):
        self.made = []
        if not paired():
            return ()
        half = self.right.shape[0] // 2
        plane = (lax.axis_index("seq") // 2).reshape(1)
        self.kept = []
        for start, side in ((0, SIDE_X), (half, SIDE_Y)):
            send, keep = weight_grads(
                plane,
                self.left.near,
                self.left.far,
                self.right,
                self.other,
                self.kind,
                start,
                side,
                light,
            )
            self.made.append(send)
            self.kept.append(keep)
        return tuple(self.made)

    def go(self, *after):
        if paired():
            made = [tie(send, *after) for send in self.made] if after else self.made
            self.arrived = [swap(send, side) for send, side in zip(made, (SIDE_X, SIDE_Y))]
            self.coming = self.arrived

    def second(self, *after):
        if not paired():
            return ()
        self.sums, made = [], []
        for keep, arrived, side in zip(self.kept, self.arrived, (SIDE_Y, SIDE_X)):
            if after:
                arrived = tie(arrived, *after)
            go = (keep[1].astype(f32) + arrived[1].astype(f32)).astype(bf16)
            stay = keep[0].astype(f32) + arrived[0].astype(f32)
            made.append(go)
            self.sums.append((stay, swap(go, side)))
        self.coming = [arrived for _, arrived in self.sums]
        return tuple(made)

    def pending(self):
        return tuple(self.coming) if paired() else ()

    def last(self, *after):
        if not paired():
            whole = jnp.einsum(
                "td,htc->hdc", self.left.rows, self.right[:, self.kind], preferred_element_type=f32
            ).astype(bf16)
            seq = lax.axis_size("seq")
            whole = whole.reshape(whole.shape[:1] + (seq, D // seq, -1))
            return lax.psum_scatter(whole, "seq", scatter_dimension=1)
        sums = []
        for stay, arrived in self.sums:
            if after:
                arrived = tie(arrived, *after)
            sums.append((stay + arrived.astype(f32)).astype(bf16))
        sums = jnp.concatenate(sums, axis=0)
        if self.relative:
            sums = by_place(sums)
        return sums


class Along:
    def __init__(self, blocks, *after):
        if not paired():
            self.mine, self.coming = lax.psum_scatter(blocks, "head", scatter_dimension=0), []
            self.sent = ()
            return
        here = lax.axis_index("head")
        pick = lambda r: lax.dynamic_index_in_dim(blocks, here ^ r, 0, keepdims=False)
        sent = [pick(r) for r in (1, 2, 3)]
        self.sent = tuple(sent)
        if after:
            sent = [tie(block, *after) for block in sent]
        self.mine = pick(0)
        self.coming = [swap(block, r, "head") for r, block in zip((1, 2, 3), sent)]

    def finish(self, *after):
        coming = [tie(block, *after) for block in self.coming] if after else self.coming
        return sum([block.astype(f32) for block in coming], self.mine.astype(f32))


def whole_rows(ref, kind=0):
    block = ref[:, 0, kind]
    return block.reshape(D, block.shape[-1])


def weight_spec(weight, kinds=1, at=0):
    seq, _, _, _, columns = weight.shape
    return pl.BlockSpec((seq, 1, kinds, D // seq, columns), lambda z: (0, z, at, 0, 0))


def into_kernel(x_ref, w_ref, out_ref):
    out_ref[0] = dot(x_ref[...], whole_rows(w_ref)).astype(out_ref.dtype)


def into(x, weight, kind):
    count, columns = weight.shape[1], weight.shape[-1]
    tokens = x.shape[0]
    return pl.pallas_call(
        into_kernel,
        grid=(count,),
        in_specs=[
            pl.BlockSpec(x.shape, lambda z: (0, 0)),
            weight_spec(weight),
        ],
        out_specs=pl.BlockSpec((1, tokens, columns), lambda z: (z, 0, 0)),
        out_shape=jax.ShapeDtypeStruct((count, tokens, columns), kind),
        compiler_params=pltpu.CompilerParams(vmem_limit_bytes=VMEM),
        cost_estimate=cost(count * 3 * D * tokens * columns),
    )(x, weight)


def out_of_kernel(y_ref, w_ref, out_ref):
    @pl.when(pl.program_id(0) == 0)
    def _():
        out_ref[...] = jnp.zeros_like(out_ref)

    out_ref[...] += dot_rt(y_ref[0], whole_rows(w_ref))


def out_of(y, weight):
    count, tokens, columns = y.shape
    return pl.pallas_call(
        out_of_kernel,
        grid=(count,),
        in_specs=[
            pl.BlockSpec((1, tokens, columns), lambda z: (z, 0, 0)),
            weight_spec(weight),
        ],
        out_specs=pl.BlockSpec((tokens, D), lambda z: (0, 0)),
        out_shape=jax.ShapeDtypeStruct((tokens, D), f32),
        compiler_params=pltpu.CompilerParams(vmem_limit_bytes=VMEM),
        cost_estimate=cost(1),
    )(y, weight)


def into_pieces_kernel(lay, weights, offsets, places, x_ref, *refs):
    count = len(weights.pieces)
    refs, outs, weight = refs[:count], refs[count:-1], refs[-1]
    weights.fill(offsets, refs, weight)
    rows = dot(x_ref[...], weight[...])
    for b in range(lay.batch):
        here = slice(b * lay.tokens, (b + 1) * lay.tokens)
        for i in range(lay.splits):
            for j, out in enumerate(outs):
                out[b, i, 0, :, :WIDTH] = rows[here, lay.columns(i, j)[0]].astype(bf16)
                out[b, i, 0, :, WIDTH:] = jnp.zeros_like(out[b, i, 0, :, WIDTH:])


def into_pieces(lay, x, weights):
    count, columns = weights.places, weights.columns
    block = (lay.batch, lay.splits, 1, lay.tokens, LANES)
    return pl.pallas_call(
        functools.partial(into_pieces_kernel, lay, weights),
        grid_spec=pltpu.PrefetchScalarGridSpec(
            num_scalar_prefetch=2,
            grid=(count,),
            in_specs=[pl.BlockSpec(x.shape, lambda z, o, p: (0, 0))] + weights.specs(),
            out_specs=[pl.BlockSpec(block, lambda z, o, p: (0, 0, p[z], 0, 0))] * lay.heads,
            scratch_shapes=[pltpu.VMEM((D, columns), bf16)],
        ),
        out_shape=[jax.ShapeDtypeStruct(block[:2] + (count,) + block[3:], bf16)] * lay.heads,
        compiler_params=pltpu.CompilerParams(vmem_limit_bytes=VMEM),
        cost_estimate=cost(count * 3 * D * x.shape[0] * columns),
    )(weights.offsets, weights.order, x, *[piece for piece, _ in weights.pieces])


def out_of_pieces_kernel(lay, weights, offsets, places, *refs):
    ys, refs, (rows_ref, out_ref, weight) = refs[: lay.heads], refs[lay.heads : -3], refs[-3:]
    weights.fill(offsets, refs, weight)

    @pl.when(pl.program_id(0) == 0)
    def _():
        out_ref[...] = jnp.zeros_like(out_ref)

    end = lay.splits * lay.heads * WIDTH
    rows_ref[0, 0, :, end:] = jnp.zeros_like(rows_ref[0, 0, :, end:])
    for b in range(lay.batch):
        here = slice(b * lay.tokens, (b + 1) * lay.tokens)
        for i in range(lay.splits):
            for j, y_ref in enumerate(ys):
                rows_ref[0, 0, here, lay.columns(i, j)[0]] = y_ref[b, i, 0, :, :WIDTH]
    out_ref[...] += dot_rt(rows_ref[0, 0], weight[...])


def out_of_pieces(lay, ys, weights):
    count, columns = weights.places, weights.columns
    tokens = lay.batch * lay.tokens
    block = (lay.batch, lay.splits, 1, lay.tokens, LANES)
    return pl.pallas_call(
        functools.partial(out_of_pieces_kernel, lay, weights),
        grid_spec=pltpu.PrefetchScalarGridSpec(
            num_scalar_prefetch=2,
            grid=(count,),
            in_specs=[pl.BlockSpec(block, lambda z, o, p: (0, 0, p[z], 0, 0))] * lay.heads
            + weights.specs(),
            out_specs=[
                pl.BlockSpec((1, 1, tokens, columns), lambda z, o, p: (z, 0, 0, 0)),
                pl.BlockSpec((tokens, D), lambda z, o, p: (0, 0)),
            ],
            scratch_shapes=[pltpu.VMEM((D, columns), bf16)],
        ),
        out_shape=[
            jax.ShapeDtypeStruct((count, 1, tokens, columns), bf16),
            jax.ShapeDtypeStruct((tokens, D), f32),
        ],
        compiler_params=pltpu.CompilerParams(vmem_limit_bytes=VMEM),
        cost_estimate=cost(count * 3 * D * tokens * columns),
    )(weights.offsets, weights.order, *ys, *[piece for piece, _ in weights.pieces])


def spread_kernel(weights, offsets, places, x_ref, *refs):
    refs, (out_ref, weight) = refs[:-2], refs[-2:]
    weights.fill(offsets, refs, weight)
    out_ref[0] = dot(x_ref[...], weight[...])


def spread(x, weights):
    count, columns = weights.places, weights.columns
    tokens = x.shape[0]
    return pl.pallas_call(
        functools.partial(spread_kernel, weights),
        grid_spec=pltpu.PrefetchScalarGridSpec(
            num_scalar_prefetch=2,
            grid=(count,),
            in_specs=[pl.BlockSpec(x.shape, lambda z, o, p: (0, 0))] + weights.specs(),
            out_specs=pl.BlockSpec((1, tokens, columns), lambda z, o, p: (p[z], 0, 0)),
            scratch_shapes=[pltpu.VMEM((D, columns), bf16)],
        ),
        out_shape=jax.ShapeDtypeStruct((count, tokens, columns), f32),
        compiler_params=pltpu.CompilerParams(vmem_limit_bytes=VMEM),
        cost_estimate=cost(count * 3 * D * tokens * columns),
    )(weights.offsets, weights.order, x, *[piece for piece, _ in weights.pieces])


def collect_kernel(weights, offsets, places, y_ref, *refs):
    refs, (out_ref, weight) = refs[:-2], refs[-2:]
    weights.fill(offsets, refs, weight)

    @pl.when(pl.program_id(0) == 0)
    def _():
        out_ref[...] = jnp.zeros_like(out_ref)

    out_ref[...] += dot_rt(y_ref[0, 0], weight[...])


def collect(y, weights):
    count, _, tokens, columns = y.shape
    return pl.pallas_call(
        functools.partial(collect_kernel, weights),
        grid_spec=pltpu.PrefetchScalarGridSpec(
            num_scalar_prefetch=2,
            grid=(count,),
            in_specs=[pl.BlockSpec((1,) + y.shape[1:], lambda z, o, p: (p[z], 0, 0, 0))]
            + weights.specs(),
            out_specs=pl.BlockSpec((tokens, D), lambda z, o, p: (0, 0)),
            scratch_shapes=[pltpu.VMEM((D, columns), bf16)],
        ),
        out_shape=jax.ShapeDtypeStruct((tokens, D), f32),
        compiler_params=pltpu.CompilerParams(vmem_limit_bytes=VMEM),
        cost_estimate=cost(count * 3 * D * tokens * columns),
    )(weights.offsets, weights.order, y, *[piece for piece, _ in weights.pieces])


def hidden_kernel(x_ref, gu_ref, slope_ref, silu_ref, hidden_ref):
    gate = dot(x_ref[...], whole_rows(gu_ref, 0))
    sig = jax.nn.sigmoid(gate)
    silu = gate * sig
    up = dot(x_ref[...], whole_rows(gu_ref, 1))
    slope_ref[0] = (up * sig * (1.0 + gate * (1.0 - sig))).astype(bf16)
    silu_ref[0] = silu.astype(bf16)
    columns = gate.shape[1]
    hidden_ref[0, 0, :, :columns] = (silu * up).astype(bf16)
    hidden_ref[0, 0, :, columns:] = jnp.zeros_like(hidden_ref[0, 0, :, columns:])


def hidden_of(x, weight):
    count, columns = weight.shape[1], weight.shape[-1]
    padded = grouped(columns, LANES)
    tokens = x.shape[0]
    act = pl.BlockSpec((1, tokens, columns), lambda z: (z, 0, 0))
    kept = jax.ShapeDtypeStruct((count, tokens, columns), bf16)
    return pl.pallas_call(
        hidden_kernel,
        grid=(count,),
        in_specs=[pl.BlockSpec(x.shape, lambda z: (0, 0)), weight_spec(weight, kinds=2)],
        out_specs=[act, act, pl.BlockSpec((1, 1, tokens, padded), lambda z: (z, 0, 0, 0))],
        out_shape=[kept, kept, jax.ShapeDtypeStruct((count, 1, tokens, padded), bf16)],
        compiler_params=pltpu.CompilerParams(vmem_limit_bytes=VMEM),
        cost_estimate=cost(count * 6 * D * tokens * columns),
    )(x, weight)


def hidden_back_kernel(grad_ref, gu_ref, slope_ref, silu_ref, grads_ref, out_ref):
    @pl.when(pl.program_id(0) == 0)
    def _():
        out_ref[...] = jnp.zeros_like(out_ref)

    columns = slope_ref.shape[-1]
    grad_hidden = grad_ref[0, :, :columns]
    grad_gate = (grad_hidden * slope_ref[0].astype(f32)).astype(bf16)
    grad_up = (grad_hidden * silu_ref[0].astype(f32)).astype(bf16)
    grads_ref[0, 0, :, :columns] = grad_gate
    grads_ref[0, 1, :, :columns] = grad_up
    grads_ref[0, :, :, columns:] = jnp.zeros_like(grads_ref[0, :, :, columns:])
    out_ref[...] += dot_rt(grad_gate, whole_rows(gu_ref, 0)) + dot_rt(
        grad_up, whole_rows(gu_ref, 1)
    )


def hidden_back(grad, weight, slope, silu):
    count, columns = weight.shape[1], weight.shape[-1]
    padded = grouped(columns, LANES)
    tokens = grad.shape[1]
    act = pl.BlockSpec((1, tokens, columns), lambda z: (z, 0, 0))
    return pl.pallas_call(
        hidden_back_kernel,
        grid=(count,),
        in_specs=[
            pl.BlockSpec((1, tokens, padded), lambda z: (z, 0, 0)),
            weight_spec(weight, kinds=2),
            act,
            act,
        ],
        out_specs=[
            pl.BlockSpec((1, 2, tokens, padded), lambda z: (z, 0, 0, 0)),
            pl.BlockSpec((tokens, D), lambda z: (0, 0)),
        ],
        out_shape=[
            jax.ShapeDtypeStruct((count, 2, tokens, padded), bf16),
            jax.ShapeDtypeStruct((tokens, D), f32),
        ],
        compiler_params=pltpu.CompilerParams(vmem_limit_bytes=VMEM),
        cost_estimate=cost(1),
    )(grad, weight, slope, silu)


def inverse_rms(rows):
    return lax.rsqrt(jnp.mean(rows * rows, axis=-1, keepdims=True) + EPSILON)


def norm_back(rows, scale, gain, grad):
    unit = rows * scale
    scaled = gain * grad
    return scale * (scaled - unit * jnp.mean(scaled * unit, axis=-1, keepdims=True))


class Layout:
    def __init__(self, batch, tokens):
        seq, head = lax.axis_size("seq"), lax.axis_size("head")
        self.batch, self.tokens, self.head = batch, tokens, head
        self.splits = min(seq // batch, HEADS // head)
        self.heads = HEADS // (head * self.splits)
        self.parts = seq // (batch * self.splits)
        self.inner = seq // self.parts
        self.sets = LANES // FEAT
        self.key_rows = grouped(tokens // self.sets, 16)
        self.length = tokens * seq * head
        count = self.inner * head
        self.groups = None
        if self.parts > 1:
            self.groups = [list(range(k * count, (k + 1) * count)) for k in range(self.parts)]
            self.mates = [[k * count + i for k in range(self.parts)] for i in range(count)]

    def sequence(self):
        return lax.rem(lax.axis_index("seq"), self.inner) // self.splits

    def pack_keys(self, keys):
        lead, each = keys.shape[:-2], self.tokens // self.sets
        keys = keys.reshape(lead + (self.sets, each, FEAT))
        keys = jnp.swapaxes(keys, -3, -2).reshape(lead + (each, LANES))
        return jnp.pad(keys, [(0, 0)] * len(lead) + [(0, self.key_rows - each), (0, 0)])

    def unpack_keys(self, rows):
        lead, each = rows.shape[:-2], self.tokens // self.sets
        rows = rows[..., :each, :].reshape(lead + (each, self.sets, FEAT))
        return jnp.swapaxes(rows, -3, -2).reshape(lead + (self.tokens, FEAT))

    def columns(self, i, j):
        at = i * self.heads + j
        return slice(at * WIDTH, (at + 1) * WIDTH), slice(at * FEAT, (at + 1) * FEAT)

    def by_place(self, blocks):
        return blocks.reshape((self.batch, self.splits, self.head) + blocks.shape[1:])

    def exchange(self, blocks):
        return lax.all_to_all(blocks, BOTH, 0, 0, tiled=True, axis_index_groups=self.groups)

    def all_parts(self, rows):
        if self.parts > 1:
            rows = lax.all_gather(rows, BOTH, axis=0, tiled=True, axis_index_groups=self.mates)
        return rows

    def own_part(self, blocks):
        if self.parts > 1:
            count = blocks.shape[0] // self.parts
            part = lax.axis_index("seq") // self.inner
            blocks = lax.dynamic_slice_in_dim(blocks, part * count, count, 0)
        return blocks


def fill_values(chunk, main, values, queries):
    lane = lax.broadcasted_iota(jnp.int32, (chunk, LANES), 1)
    ones = jnp.where(lane < WIDTH + 2, 1.0, 0.0)

    def turn(i, _):
        here = pl.ds(pl.multiple_of(i * chunk, chunk), chunk)
        rows = main[here]
        values[here] = jnp.where(lane < WIDTH, rows.astype(f32), ones).astype(bf16)
        queries[here] = rows[:, WIDTH:]
        return 0

    lax.fori_loop(0, main.shape[0] // chunk, turn, 0)


def attend_kernel(chunk, main, keys, seg_col, seg_row, out_ref, low_ref, values, queries):
    at = pl.program_id(0)

    @pl.when(at == 0)
    def _():
        fill_values(chunk, main, values, queries)

    mine = seg_col[...]
    query = queries[pl.ds(pl.multiple_of(at * chunk, chunk), chunk)]

    def weighted(j, causal):
        here = pl.ds(pl.multiple_of(j * chunk, chunk), chunk)
        scores = dot_rt(query, keys[here])
        allowed = mine == seg_row[j]
        if causal:
            later = lax.broadcasted_iota(jnp.int32, scores.shape, 0)
            allowed &= later >= lax.broadcasted_iota(jnp.int32, scores.shape, 1)
        weights = jnp.where(allowed, 1.0 + scores * (1.0 + 0.5 * scores), 0.0).astype(bf16)
        return dot(weights, values[here])

    total = lax.fori_loop(
        0, at, lambda j, acc: acc + weighted(j, False), jnp.zeros((chunk, LANES), f32)
    )
    total = total + weighted(at, True)
    norm = total[:, WIDTH : WIDTH + 1]
    lane = lax.broadcasted_iota(jnp.int32, total.shape, 1)
    total = jnp.where(lane < WIDTH, total / norm, norm)
    out_ref[...] = total
    low_ref[...] = total.astype(bf16)


def attend(main, keys, seg):
    length = main.shape[0]
    chunk = min(512, length)
    steps = length // chunk
    part = pl.BlockSpec((chunk, LANES), lambda i: (i, 0))
    return pl.pallas_call(
        functools.partial(attend_kernel, chunk),
        grid=(steps,),
        in_specs=[
            pl.BlockSpec((length, LANES), lambda i: (0, 0)),
            pl.BlockSpec((length, FEAT), lambda i: (0, 0)),
            pl.BlockSpec((chunk, 1), lambda i: (i, 0)),
            pl.BlockSpec((steps, 1, chunk), lambda i: (0, 0, 0)),
        ],
        out_specs=[part, part],
        out_shape=[
            jax.ShapeDtypeStruct((length, LANES), f32),
            jax.ShapeDtypeStruct((length, LANES), bf16),
        ],
        scratch_shapes=[pltpu.VMEM((length, LANES), bf16), pltpu.VMEM((length, FEAT), bf16)],
        compiler_params=pltpu.CompilerParams(vmem_limit_bytes=VMEM),
        cost_estimate=cost(length * length * 12 * LANES),
    )(main, keys, seg.reshape(length, 1), seg.reshape(steps, 1, chunk))


def attend_back_kernel(
    chunk,
    main,
    keys,
    kept,
    grad,
    seg_col,
    seg_row,
    out_ref,
    gk_ref,
    values,
    queries,
    grad_n,
    grad_q,
):
    at = pl.program_id(0)
    steps = main.shape[0] // chunk

    @pl.when(at == 0)
    def _():
        fill_values(chunk, main, values, queries)
        grad_q[...] = jnp.zeros_like(grad_q)
        lane = lax.broadcasted_iota(jnp.int32, (chunk, LANES), 1)

        def turn(i, _):
            here = pl.ds(pl.multiple_of(i * chunk, chunk), chunk)
            rows = kept[here]
            low = jnp.where(lane < WIDTH, grad[here].astype(f32), 0.0)
            inverse = 1.0 / rows[:, WIDTH : WIDTH + 1]
            total = -jnp.sum(low * rows, axis=1, keepdims=True) * inverse
            high = total.astype(bf16).astype(f32)
            low = low * inverse
            low = jnp.where(lane == WIDTH, high, low)
            grad_n[here] = jnp.where(lane == WIDTH + 1, total - high, low).astype(bf16)
            return 0

        lax.fori_loop(0, steps, turn, 0)

    mine = seg_col[...]
    rows = pl.ds(pl.multiple_of(at * chunk, chunk), chunk)
    key, value = keys[rows], values[rows]
    key_t = key.astype(f32).T.astype(bf16)

    def turn(i, carry, causal):
        grad_k, grad_v = carry
        here = pl.ds(pl.multiple_of(i * chunk, chunk), chunk)
        query, grad_here = queries[here], grad_n[here]
        scores = dot_rt(key, query)
        allowed = mine == seg_row[i]
        if causal:
            key_at = lax.broadcasted_iota(jnp.int32, scores.shape, 0)
            allowed &= key_at <= lax.broadcasted_iota(jnp.int32, scores.shape, 1)
        weights = jnp.where(allowed, 1.0 + scores * (1.0 + 0.5 * scores), 0.0).astype(bf16)
        grad_s = dot_rt(value, grad_here) * (1.0 + scores)
        grad_s = jnp.where(allowed, grad_s, 0.0).astype(bf16)
        grad_q[:, here] += dot(key_t, grad_s)
        return grad_k + dot(grad_s, query), grad_v + dot(weights, grad_here)

    carry = (jnp.zeros((chunk, FEAT), f32), jnp.zeros((chunk, LANES), f32))
    carry = turn(at, carry, True)
    grad_k, grad_v = lax.fori_loop(at + 1, steps, lambda i, c: turn(i, c, False), carry)
    gk_ref[...] = (0.5 * grad_k).astype(bf16)
    out_ref[rows] = grad_v.astype(bf16)

    @pl.when(at == steps - 1)
    def _():
        def turn(i, _):
            here = pl.ds(pl.multiple_of(i * chunk, chunk), chunk)
            out_ref[here, WIDTH:] = (0.5 * grad_q[:, here].T).astype(bf16)
            return 0

        lax.fori_loop(0, steps, turn, 0)


def attend_back(main, keys, kept, grad, seg):
    length = main.shape[0]
    chunk = min(512, length)
    steps = length // chunk
    whole = pl.BlockSpec((length, LANES), lambda i: (0, 0))
    return pl.pallas_call(
        functools.partial(attend_back_kernel, chunk),
        grid=(steps,),
        in_specs=[
            whole,
            pl.BlockSpec((length, FEAT), lambda i: (0, 0)),
            whole,
            whole,
            pl.BlockSpec((chunk, 1), lambda i: (i, 0)),
            pl.BlockSpec((steps, 1, chunk), lambda i: (0, 0, 0)),
        ],
        out_specs=[whole, pl.BlockSpec((chunk, FEAT), lambda i: (i, 0))],
        out_shape=[
            jax.ShapeDtypeStruct((length, LANES), bf16),
            jax.ShapeDtypeStruct((length, FEAT), bf16),
        ],
        scratch_shapes=[
            pltpu.VMEM((length, LANES), bf16),
            pltpu.VMEM((length, FEAT), bf16),
            pltpu.VMEM((length, LANES), bf16),
            pltpu.VMEM((FEAT, length), f32),
        ],
        compiler_params=pltpu.CompilerParams(vmem_limit_bytes=VMEM),
        cost_estimate=cost(length * length * 24 * LANES),
    )(main, keys, kept, grad, seg.reshape(length, 1), seg.reshape(steps, 1, chunk))


def earlier(rows, before, distance):
    moved = pltpu.roll(rows, distance, 0)
    place = lax.broadcasted_iota(jnp.int32, rows.shape, 0)
    for i in range(distance):
        at = 2 - distance + i
        moved = jnp.where(place == i, before[at : at + 1], moved)
    return moved


def later(rows, after, distance):
    count = rows.shape[0]
    moved = pltpu.roll(rows, count - distance, 0)
    place = lax.broadcasted_iota(jnp.int32, rows.shape, 0)
    for i in range(distance):
        moved = jnp.where(place == count - distance + i, after[i : i + 1], moved)
    return moved


def short_filter(taps, same, values, before):
    one_back = earlier(values, before, 1) * same[:, 0:1]
    two_back = earlier(values, before, 2) * same[:, 1:2]
    return taps[0:1] * values + taps[1:2] * one_back + taps[2:3] * two_back, one_back, two_back


def project_kernel(lay, x_ref, side_ref, same_ref, taps_ref, w_ref, v_ref, f_ref, side_out, *outs):
    weight = whole_rows(w_ref)
    q_width, v_width = lay.splits * lay.heads * FEAT, v_ref.shape[-1]
    v_at, f_at = 2 * q_width, 2 * q_width + v_width
    full = dot(x_ref[...], weight)
    side = dot(side_ref[...], weight)
    low = full[:, v_at:f_at].astype(bf16)
    v_ref[0] = low
    f_ref[0] = full[:, f_at:]
    side_v = side[:, v_at:f_at].astype(bf16).astype(f32)
    side_out[0, 0] = side_v
    side_out[0, 1] = side[:, f_at:]
    taps = taps_ref[0]
    for b in range(lay.batch):
        rows = slice(b * lay.tokens, (b + 1) * lay.tokens)
        pre = full[rows, f_at:]
        filtered, _, _ = short_filter(
            taps, same_ref[rows], low[rows].astype(f32), side_v[2 * b : 2 * b + 2]
        )
        mixed = filtered * (pre * jax.nn.sigmoid(pre))
        query = 0.5 * full[rows, :q_width].astype(bf16).astype(f32)
        key = 0.5 * full[rows, q_width:v_at].astype(bf16).astype(f32)
        for i in range(lay.splits):
            for j in range(lay.heads):
                main, k_ref = outs[2 * j : 2 * j + 2]
                v_cols, q_cols = lay.columns(i, j)
                main[b, i, 0, :, :WIDTH] = mixed[:, v_cols].astype(bf16)
                main[b, i, 0, :, WIDTH:] = query[:, q_cols].astype(bf16)
                k_ref[b, i, 0] = key[:, q_cols].astype(bf16)


def project(lay, x, side, same, taps, weight):
    tokens, head = x.shape[0], lay.head
    v_width = taps.shape[-1]
    beside = side.shape[0]
    to_all = lambda width: pl.BlockSpec(
        (lay.batch, lay.splits, 1, lay.tokens, width), lambda z: (0, 0, z, 0, 0)
    )
    shape = lambda width: jax.ShapeDtypeStruct(
        (lay.batch, lay.splits, head, lay.tokens, width), bf16
    )
    kept = pl.BlockSpec((1, tokens, v_width), lambda z: (z, 0, 0))
    return pl.pallas_call(
        functools.partial(project_kernel, lay),
        grid=(head,),
        in_specs=[
            pl.BlockSpec(x.shape, lambda z: (0, 0)),
            pl.BlockSpec(side.shape, lambda z: (0, 0)),
            pl.BlockSpec(same.shape, lambda z: (0, 0)),
            pl.BlockSpec((1, 3, v_width), lambda z: (z, 0, 0)),
            weight_spec(weight),
        ],
        out_specs=[
            kept,
            kept,
            pl.BlockSpec((1, 2, beside, v_width), lambda z: (z, 0, 0, 0)),
        ]
        + [to_all(LANES), to_all(FEAT)] * lay.heads,
        out_shape=[
            jax.ShapeDtypeStruct((head, tokens, v_width), bf16),
            jax.ShapeDtypeStruct((head, tokens, v_width), f32),
            jax.ShapeDtypeStruct((head, 2, beside, v_width), f32),
        ]
        + [shape(LANES), shape(FEAT)] * lay.heads,
        compiler_params=pltpu.CompilerParams(vmem_limit_bytes=VMEM),
        cost_estimate=cost(head * 3 * D * tokens * weight.shape[-1]),
    )(x, side, same, taps, weight)


def project_back_kernel(
    lay, v_ref, f_ref, side_ref, same_ref, taps_ref, gk_ref, *refs
):
    backs, (out_ref, tap_ref, mixed, after) = refs[:-4], refs[-4:]
    q_width, v_width = gk_ref.shape[-1], v_ref.shape[-1]
    v_at, f_at = 2 * q_width, 2 * q_width + v_width
    taps = taps_ref[0]
    below = lay.tokens + lay.key_rows
    tap_ref[...] = jnp.zeros_like(tap_ref)
    out_ref[0, :, q_width:v_at] = gk_ref[0]
    for b in range(lay.batch):
        rows = slice(b * lay.tokens, (b + 1) * lay.tokens)
        for i in range(lay.splits):
            for j, back in enumerate(backs):
                v_cols, q_cols = lay.columns(i, j)
                block = back[b, i, 0, : lay.tokens]
                mixed[:, v_cols] = block[:, :WIDTH].astype(f32)
                out_ref[0, rows, q_cols] = block[:, WIDTH:]
                after[:, v_cols] = back[b, i, 0, below : below + 16, :WIDTH].astype(f32)
        grad_mixed = mixed[...]
        pre = f_ref[0, rows]
        sig = jax.nn.sigmoid(pre)
        values = v_ref[0, rows].astype(f32)
        same = same_ref[rows]
        at = 2 * b
        filtered, one_back, two_back = short_filter(
            taps, same, values, side_ref[0, 0, at : at + 2]
        )
        grad = grad_mixed * pre * sig
        at = 2 * (lay.batch + b)
        pre_after = side_ref[0, 1, at : at + 2]
        grad_after = after[0:2] * pre_after * jax.nn.sigmoid(pre_after)
        grad_v = (
            taps[0:1] * grad
            + taps[1:2] * later(grad, grad_after, 1) * same[:, 2:3]
            + taps[2:3] * later(grad, grad_after, 2) * same[:, 3:4]
        )
        out_ref[0, rows, v_at:f_at] = grad_v.astype(bf16)
        grad_f = grad_mixed * filtered * sig * (1.0 + pre * (1.0 - sig))
        out_ref[0, rows, f_at:] = grad_f.astype(bf16)
        for k, term in enumerate((values, one_back, two_back)):
            tap_ref[0, k : k + 1] += jnp.sum(grad * term, axis=0, keepdims=True)


def project_back(lay, backs, grad_keys, values, pre, side, same, taps):
    head, tokens, v_width = values.shape
    columns = 2 * (grad_keys.shape[-1] + v_width)
    kept = pl.BlockSpec((1, tokens, v_width), lambda z: (z, 0, 0))
    return pl.pallas_call(
        functools.partial(project_back_kernel, lay),
        grid=(head,),
        in_specs=[
            kept,
            kept,
            pl.BlockSpec((1,) + side.shape[1:], lambda z: (z, 0, 0, 0)),
            pl.BlockSpec(same.shape, lambda z: (0, 0)),
            pl.BlockSpec((1, 3, v_width), lambda z: (z, 0, 0)),
            pl.BlockSpec((1,) + grad_keys.shape[1:], lambda z: (z, 0, 0)),
        ]
        + [
            pl.BlockSpec(
                (lay.batch, lay.splits, 1) + back.shape[3:], lambda z: (0, 0, z, 0, 0)
            )
            for back in backs
        ],
        out_specs=[
            pl.BlockSpec((1, tokens, columns), lambda z: (z, 0, 0)),
            pl.BlockSpec((1, 3, v_width), lambda z: (z, 0, 0)),
        ],
        out_shape=[
            jax.ShapeDtypeStruct((head, tokens, columns), bf16),
            jax.ShapeDtypeStruct((head, 3, v_width), f32),
        ],
        scratch_shapes=[
            pltpu.VMEM((lay.tokens, v_width), f32),
            pltpu.VMEM((16, v_width), f32),
        ],
        compiler_params=pltpu.CompilerParams(vmem_limit_bytes=VMEM),
        cost_estimate=cost(1),
    )(values, pre, side, same, taps, grad_keys, *backs)


def shift(block, distance):
    devices = range(lax.axis_size("seq") * lax.axis_size("head"))
    return lax.ppermute(
        block, BOTH, [(i, i + distance) for i in devices if i + distance in devices]
    )


def local(
    tokens,
    cotangent,
    segment_ids,
    query_weight,
    key_weight,
    value_weight,
    filter_weight,
    out_weight,
    gate_weight,
    up_weight,
    down_weight,
    norm_gain,
    ffn_gain,
    conv_taps,
):
    seq, head = lax.axis_size("seq"), lax.axis_size("head")
    batch, span, _ = tokens.shape
    count = batch * span
    length = segment_ids.shape[1] * seq
    place = lax.axis_index("seq") * head + lax.axis_index("head")
    heads_here = HEADS // head
    qk_width, v_width = heads_here * FEAT, heads_here * WIDTH
    ff_width = gate_weight.shape[1]

    lay = Layout(batch, span)
    out_pad = grouped(v_width, LANES) - v_width
    first = jnp.concatenate([query_weight, key_weight, value_weight, filter_weight], axis=1)
    rows_here, columns = first.shape
    small = [norm_gain, ffn_gain, conv_taps.reshape(-1), segment_ids.astype(bf16).reshape(-1)]
    ends = [0]
    for part in small:
        ends.append(ends[-1] + part.size)
    below = grouped(-(-ends[-1] // columns), 16)
    small = jnp.pad(jnp.concatenate(small), (0, below * columns - ends[-1]))
    ff_pad = grouped(ff_width, LANES) - ff_width
    down_shard = jnp.pad(down_weight, ((0, 0), (0, ff_pad)))
    out_shard = jnp.pad(out_weight.T, ((0, 0), (0, out_pad)))
    edge = jnp.stack([tokens[:, -2:], tokens[:, :2]]).reshape(-1, D)
    edge = jnp.pad(edge, ((0, grouped(edge.shape[0], 16) - edge.shape[0]), (0, 0)))
    first_w, edges, lined = gather_first(
        jnp.concatenate([first, small.reshape(below, columns)]), edge, [down_shard]
    )
    beside = jnp.concatenate([edges[0, : 2 * batch], edges[1, 2 * batch : 4 * batch]])
    gate_up_w = gather(jnp.stack([gate_weight, up_weight]))
    down_w = Pieces(down_shard, lined[0])

    small = first_w[:, :, 0, rows_here:].reshape(seq, head, -1).astype(f32)
    part = lambda i: small[:, :, ends[i] : ends[i + 1]]
    gain_one, gain_two = part(0)[:, 0].reshape(1, D), part(1)[:, 0].reshape(1, D)
    taps = jnp.transpose(part(2).reshape(seq, head, 3, -1), (1, 2, 0, 3))
    taps = taps.reshape(head, 3, v_width)
    segs = jnp.swapaxes(part(3)[:, 0].reshape(seq, batch, -1), 0, 1).reshape(batch, length)
    x = tokens.reshape(count, D).astype(f32)
    cot_low = cotangent.reshape(count, D)

    def normed_of(rows):
        scale = inverse_rms(rows)
        return scale, (rows * scale * gain_one).astype(bf16)

    scale_one, normed = normed_of(x)
    _, normed_beside = normed_of(beside.astype(f32))
    around = lax.dynamic_slice(
        jnp.pad(segs, ((0, 0), (2, 2)), constant_values=-1.0),
        (0, place * span),
        (batch, span + 4),
    )
    seg_here = around[:, 2:-2]
    others = (around[:, 1:-3], around[:, :-4], around[:, 3:-1], around[:, 4:])
    same = jnp.stack([(seg_here == other).astype(f32) for other in others], axis=-1)
    same = same.reshape(count, 4)
    cot_left = Left(cot_low)
    normed = tie(normed, down_w.own, *cot_left.pending())
    down_sides = down_w.sides(first_w)
    v_low, filter_pre, side, *sent = project(lay, normed, normed_beside, same, taps, first_w)
    my_seg = lax.dynamic_index_in_dim(segs, lay.sequence(), 0, keepdims=False)
    heads = range(lay.heads)
    mains, all_keys, kept, low = [], [], [], []
    for j in heads:
        blocks = jnp.concatenate([sent[2 * j], lay.pack_keys(sent[2 * j + 1])], axis=3)
        if j > 0:
            blocks = tie(blocks, mains[-1])
        blocks = lay.exchange(blocks.reshape(-1, span + lay.key_rows, LANES))
        mains.append(lay.all_parts(blocks[:, :span].reshape(-1, LANES)))
        all_keys.append(lay.all_parts(lay.unpack_keys(blocks[:, span:]).reshape(-1, FEAT)))
    mains[0] = tie(mains[0], *down_sides)
    down_w.far(mains[0])
    for j in heads:
        attended, sent = attend(mains[j], all_keys[j], my_seg)
        kept.append(attended)
        blocks = lay.own_part(sent.reshape(-1, span, LANES))
        if j == 0:
            out_w = Pieces(tie(out_shard, blocks))
        if j == lay.heads - 1:
            blocks = tie(blocks, out_w.own, *[piece for piece, _ in down_w.pieces])
            out_sides = out_w.sides(blocks)
        if j > 0:
            blocks = tie(blocks, low[-1])
        low.append(lay.exchange(blocks))
    grad_hidden = spread(tie(cot_low, blocks), down_w)
    low[-1] = tie(low[-1], grad_hidden, *out_sides)
    out_w.far(grad_hidden)
    att_low, projected = out_of_pieces(lay, [lay.by_place(blocks) for blocks in low], out_w)

    residual = x + projected
    scale_two = inverse_rms(residual)
    normed_two = (residual * scale_two * gain_two).astype(bf16)
    out_sum = Scatter(None, att_low, True)
    normed_two = tie(normed_two, out_sum.other_side())
    slope, silu, hidden = hidden_of(normed_two, gate_up_w)
    down_sum = Scatter(cot_left, hidden)
    ffn_out = collect(hidden, down_w)
    layer_output = (residual + ffn_out).astype(bf16).reshape(tokens.shape)

    down_sum.right = tie(down_sum.right, ffn_out)
    down_sends = down_sum.first()
    grads_gu, back_two = hidden_back(tie(grad_hidden, *down_sends), gate_up_w, slope, silu)
    two_left = Left(normed_two)
    gate_sum = Scatter(two_left, grads_gu)
    up_sum = Scatter(two_left, grads_gu, False, *gate_sum.other_side(), kind=1)
    gain_two_grad = jnp.sum(back_two * residual * scale_two, axis=0)
    grad_residual = cot_low.astype(f32) + norm_back(residual, scale_two, gain_two, back_two)
    grad_res_low = grad_residual.astype(bf16)

    sent = [rows.reshape(-1, span, LANES) for rows in into_pieces(lay, grad_res_low, out_w)]
    arrived = [lay.exchange(blocks) for blocks in sent]
    down_sends = down_sum.second(*sent)
    out_sum.left = Left(tie(grad_res_low, *sent))
    for terms in (gate_sum, up_sum, out_sum):
        terms.right = tie(terms.right, *down_sends)
    up_sum.right = tie(up_sum.right, *arrived[1:])
    made = gate_sum.products() + up_sum.products() + out_sum.products()
    down_sum = Along(down_sum.last(*made))
    gate_sum.go(*down_sum.sent)
    arrived[0] = tie(arrived[0], *made, *down_sum.sent)
    backs, grad_keys = [], []
    for j in heads:
        grad_rows = lay.all_parts(arrived[j].reshape(-1, LANES))
        if j == lay.heads - 1:
            if j > 0:
                grad_rows = tie(grad_rows, sent)
            up_sum.go(grad_rows, *gate_sum.pending())
            grad_rows = tie(grad_rows, *gate_sum.pending(), *down_sum.coming)
        grad_main, grad_key = attend_back(mains[j], all_keys[j], kept[j], grad_rows, my_seg)
        if j == lay.heads - 1:
            grad_main = tie(grad_main, *up_sum.pending())
        blocks = grad_main.reshape(-1, span, LANES)
        ahead = jnp.pad(blocks[1:, :16], ((0, 1), (0, 0), (0, 0)))
        packed = lay.pack_keys(grad_key.reshape(-1, span, FEAT))
        sent = lay.own_part(jnp.concatenate([blocks, packed, ahead], axis=1))
        if j > 0:
            sent = tie(sent, backs[-1])
        blocks = lay.exchange(sent)
        grad_keys.append(lay.unpack_keys(blocks[:, span : span + lay.key_rows]))
        backs.append(lay.by_place(blocks))
    gate_sum.second(sent)
    up_sum.second(sent)
    backs[-1] = tie(backs[-1], *gate_sum.pending(), *up_sum.pending())
    gate_up_sum = Along(jnp.stack([gate_sum.last(backs[-1]), up_sum.last(backs[-1])], axis=1))
    backs[-1] = tie(backs[-1], *gate_up_sum.sent)
    out_sum.go(backs[-1])

    grad_keys = jnp.stack([lay.by_place(rows) for rows in grad_keys])
    grad_keys = jnp.transpose(grad_keys, (3, 1, 4, 2, 0, 5)).reshape(head, count, -1)
    grad_first, tap_grads = project_back(
        lay, backs, grad_keys, v_low, filter_pre, side, same, taps
    )
    tap_grads = jnp.swapaxes(tap_grads, 0, 1).reshape(3, D)
    grad_first = tie(grad_first, *out_sum.pending(), *gate_up_sum.coming[:1])
    first_sum = Scatter(Left(tie(normed, grad_first)), grad_first[:, None])
    out_sends = out_sum.second(*first_sum.given())
    first_sum.right = tie(first_sum.right, *out_sends)
    first_sum.products(True)
    first_sum.go(*out_sum.pending())
    out_grad = lax.psum_scatter(out_sum.last(*first_sum.made), "head", scatter_dimension=0)
    back_one = out_of(tie(grad_first, *first_sum.made), first_w)
    gain_one_grad = jnp.sum(back_one * x * scale_one, axis=0)
    first_sends = first_sum.second(back_one, *gate_up_sum.coming[1:])
    gate_up_grad = gate_up_sum.finish(*first_sends)
    down_grad = down_sum.finish(*first_sends)
    first_sum = Along(first_sum.last(*first_sends))
    out_grad = tie(out_grad, *first_sum.sent)
    first_grad = first_sum.finish()
    grad_x = (grad_residual + norm_back(x, scale_one, gain_one, back_one)).astype(bf16)
    tokens_grad = grad_x.reshape(tokens.shape)

    small = jnp.concatenate([jnp.stack([gain_one_grad, gain_two_grad]), tap_grads], axis=0)
    small = tie(small, *first_sum.sent)
    small = jnp.swapaxes(small.reshape(5, head * seq, -1), 0, 1)
    small = lax.all_to_all(small, ("head", "seq"), 0, 0, tiled=True)
    small = jnp.sum(small, axis=0)

    q_end, k_end, v_end = qk_width, 2 * qk_width, 2 * qk_width + v_width
    return (
        layer_output,
        tokens_grad,
        first_grad[:, :q_end],
        first_grad[:, q_end:k_end],
        first_grad[:, k_end:v_end],
        first_grad[:, v_end:],
        out_grad[:, :v_width].astype(f32).T,
        gate_up_grad[0][:, :ff_width].astype(f32),
        gate_up_grad[1][:, :ff_width].astype(f32),
        down_grad[:, :ff_width].astype(f32),
        small[0],
        small[1],
        small[2:],
    )


def solution(mesh):
    rows = P(None, BOTH, None)
    return jax.shard_map(
        local,
        mesh=mesh,
        in_specs=(
            rows,
            rows,
            P(None, "seq"),
            P("seq", "head"),
            P("seq", "head"),
            P("seq", "head"),
            P("seq", "head"),
            P("head", "seq"),
            P("seq", "head"),
            P("seq", "head"),
            P("seq", "head"),
            P("seq"),
            P("seq"),
            P(None, ("head", "seq")),
        ),
        out_specs=(
            rows,
            rows,
            P("seq", "head"),
            P("seq", "head"),
            P("seq", "head"),
            P("seq", "head"),
            P("head", "seq"),
            P("seq", "head"),
            P("seq", "head"),
            P("seq", "head"),
            P(("head", "seq")),
            P(("head", "seq")),
            P(None, ("head", "seq")),
        ),
        check_vma=False,
    )
```

time: 1270 us -> 1150 us (0.906)
  waiting for transfers between devices: 648 us -> 256 us
  Pallas kernels: 352 us -> 513 us
  starting transfers between devices: 85.4 us -> 161 us
  local copies, waits for them, and re-layouts: 71.8 us -> 94.7 us
    all_to_all x4 -> x8, waiting for transfers between devices: 203 us -> 29.5 us  [exchange(): lax.all_to_all(blocks, BOTH, 0, 0, tiled=True, axis_index_groups=self.gro...]
    pallas_call x6 -> x11, Pallas kernels: 239 us -> 391 us  [the longest x1 146 us: gather_first(): pl.pallas_call(gather_kernel, in_specs=[anywhere] * (2 + count), out_spec...]
    all_gather x2 -> x1, waiting for transfers between devices: 106 us -> 0.01 us  [gather(): whole = lax.all_gather(shard, BOTH)]
    ppermute x48 -> x58, waiting for transfers between devices: 290 us -> 202 us  [swap(): return lax.ppermute(block, axis, [(i, i ^ bit) for i in devices])]
    all_to_all x4 -> x8, starting transfers between devices: 20.2 us -> 76 us  [exchange(): lax.all_to_all(blocks, BOTH, 0, 0, tiled=True, axis_index_groups=self.gro...]
    ppermute x48 -> x58, starting transfers between devices: 53.8 us -> 81.6 us  [swap(): return lax.ppermute(block, axis, [(i, i ^ bit) for i in devices])]
    all_to_all x1, waiting for transfers between devices: 49 us -> 24.7 us  [local(): small = lax.all_to_all(small, ('head', 'seq'), 0, 0, tiled=True)]
    transpose x13 -> x10, local copies, waits for them, and re-layouts: 16.7 us -> 26.5 us  [the longest x4 12.8 us: __init__(): blocks = rows.T.reshape(4, 2, D // 8, -1)]
  transfers between devices with their start and end apart: 57 -> 69, of which waited for: 20 -> 18; matrix products, arithmetic and copies ran while one was open for 11% -> 15% of each run, Pallas kernels for 24% -> 39%
where the time goes in v2:
time: 1150 us; the launch traced here: 1140 us
  Pallas kernels  513 us (45%)
  waiting for transfers between devices  256 us (22%)
  starting transfers between devices  161 us (14%)
  other arithmetic  94.9 us (8%)
  local copies, waits for them, and re-layouts  94.7 us (8%)
  between operations  15.8 us (1%)
    ppermute x58, waiting for transfers between devices, swap(): return lax.ppermute(block, axis, [(i, i ^ bit) for i in devices])  202 us
    pallas_call x1, Pallas kernels, gather_first(): pl.pallas_call(gather_kernel, in_specs=[anywhere] * (2 + count), out_spec...  146 us
    pallas_call x2, Pallas kernels, attend_back(): pl.pallas_call(functools.partial(attend_back_kernel, chunk), grid=(steps,...  89.9 us
    ppermute x58, starting transfers between devices, swap(): return lax.ppermute(block, axis, [(i, i ^ bit) for i in devices])  81.6 us
    pallas_call x10, Pallas kernels, weight_grads(): pl.pallas_call(functools.partial(grad_kernel, first), grid_spec=pltpu.Pre...  79.2 us
    all_to_all x8, starting transfers between devices, exchange(): lax.all_to_all(blocks, BOTH, 0, 0, tiled=True, axis_index_groups=self.gro...  76 us
    pallas_call x2, Pallas kernels, attend(): pl.pallas_call(functools.partial(attend_kernel, chunk), grid=(steps,), in...  43.6 us
    all_to_all x8, waiting for transfers between devices, exchange(): lax.all_to_all(blocks, BOTH, 0, 0, tiled=True, axis_index_groups=self.gro...  29.5 us
  transfers between devices with their start and end apart: 69, of which 18 were waited for; matrix products, arithmetic and copies ran while one was open for 15% of the time, Pallas kernels for 39%

profile of v2, /device:TPU:0, one launch (start us, length us, event | category | flops | bytes accessed | tf_op | source)
XLA Modules:
  0.0 1135.7 jit_solution(15492696886714744576)
XLA Ops:
  13.0 145.8 %shard_map.255 = (bf16[8,4,1,240,1024]{4,3,2,1,0:T(8,128)(2,1)}, bf16[2,16,1792]{2,1,0:T(8,128)(2,1)}, bf16[4,224,1280]{2,1,0:T(8,128)(2,1)}) custom-call(bf16[240,1024]{1,0:T(8,128)(2,1)} %pad_maximum_fusion.5.shard, bf16[16,1792]{1,0:T(8,128)(2,1)} %reshape.318.edge, bf16[224,1280]{1,0:T(8,128)(2,1)} %pad.24.refs_0_), custom_call_target="tpu_custom_call" | custom-call | flops 99999997952 | bytes 1 | tf_op jit(solution)/shard_map/pallas_call | solution.py:175
  183.4 16.7 %shard_map.256 = (bf16[4,512,448]{2,1,0:T(8,128)(2,1)}, f32[4,512,448]{2,1,0:T(8,128)}, f32[4,2,16,448]{3,2,1,0:T(8,128)}, bf16[4,2,4,128,128]{4,3,2,1,0:T(8,128...) custom-call(bf16[512,1792]{1,0:T(8,128)(2,1)} %fusion.3.x_ref, ...), custom_call_target="tpu_custom_call" | custom-call | flops 11274289152 | bytes 1 | tf_op jit(solution)/shard_map/pallas_call | solution.py:984
  204.6 29.9 %all-to-all-start = ((bf16[32,144,128]{2,1,0:T(8,128)(2,1)}), bf16[32,144,128]{2,1,0:T(8,128)(2,1)S(1)}, u32[]{:S(2)}, u32[]{:S(2)}) async-start(bf16[32,144,128]{2,1,0:T(8,128)(2,1)} %pad_maximum_fusion), calls=%async_computation | async-start | bytes 2359296 | tf_op jit(solution)/shard_map/all_to_all | solution.py:727
  249.5 29.4 %all-to-all-done = bf16[32,144,128]{2,1,0:T(8,128)(2,1)S(1)} async-done(((bf16[32,144,128]{2,1,0:T(8,128)(2,1)}), bf16[32,144,128]{2,1,0:T(8,128)(2,1)S(1)}, u32[]{:S(2)}, u32[]{:S(2)}) %all-to-all-start) | async-done | bytes 1179680 | tf_op jit(solution)/shard_map/all_to_all | solution.py:727
  280.4 21.2 %all-to-all-start.2 = ((bf16[32,144,128]{2,1,0:T(8,128)(2,1)}), bf16[32,144,128]{2,1,0:T(8,128)(2,1)S(1)}, u32[]{:S(2)}, u32[]{:S(2)}) async-start(bf16[32,144,128]{2,1,0:T(8,128)(2,1)} %bitcast.25), calls=%async_computation.2 | async-start | bytes 2359296 | tf_op jit(solution)/shard_map/all_to_all | solution.py:727
  310.3 21.9 %shard_map.257 = (f32[4096,128]{1,0:T(8,128)}, bf16[4096,128]{1,0:T(8,128)(2,1)}) custom-call(bf16[4096,128]{1,0:T(8,128)(2,1)} %bitcast.332, bf16[4096,16]{1,0:T(8,128)(2,1)} %bitcast.326, f32[4096,1]{1,0:T(8,128)} %copy.148.seg_col, f32[8,1,512]{2,1,0:T(1,128)} %bitcast.361), custom_call_target="tpu_custom_call" | custom-call | flops 25769803776 | bytes 1 | tf_op jit(solution)/shard_map/pallas_call | solution.py:792
  342.6 27.6 %collective-permute-done.4 = bf16[224,512]{1,0:T(8,128)(2,1)S(1)} collective-permute-done((bf16[224,512]{1,0:T(8,128)(2,1)S(1)}, bf16[224,512]{1,0:T(8,128)(2,1)S(1)}, u32[]{:S(2)}, u32[]{:S(2)}) %collective-permute-start.4) | collective-permute-done | bytes 229408 | tf_op jit(solution)/shard_map/ppermute | solution.py:47
  381.2 21.7 %shard_map.258 = (f32[4096,128]{1,0:T(8,128)}, bf16[4096,128]{1,0:T(8,128)(2,1)}) custom-call(bf16[4096,128]{1,0:T(8,128)(2,1)} %bitcast.334, bf16[4096,16]{1,0:T(8,128)(2,1)} %bitcast.328, f32[4096,1]{1,0:T(8,128)} %copy.148.seg_col, f32[8,1,512]{2,1,0:T(1,128)} %bitcast.362), custom_call_target="tpu_custom_call" | custom-call | flops 25769803776 | bytes 1 | tf_op jit(solution)/shard_map/pallas_call | solution.py:792
  410.4 18.0 %shard_map.259.grad_ref = f32[4,512,1280]{2,1,0:T(8,128)} custom-call(s32[10]{0:T(128)} %xor_multiply_fusion.offsets, s32[4]{0:T(128)} %iota_xor_fusion.places, bf16[512,1792]{1,0:T(8,128)(2,1)} %bitcast.301, bf16[4,224,1280]{2,1,0:T(8,128)(2,1)} %get-tuple-element.136.refs_0_, bf16[4,224,1280]{2,1,0:T(8,128)(2,1)} %collective-permute-done.1.refs_1_, ...), custom_call_target="tpu_custom_call" | custom-call | flops 14092861440 | bytes 1 | tf_op jit(solution)/shard_map/pallas_call | solution.py:561
  454.4 10.7 shard_map.260
  470.4 26.5 %shard_map.261 = (bf16[4,512,1216]{2,1,0:T(8,128)(2,1)}, bf16[4,512,1216]{2,1,0:T(8,128)(2,1)}, bf16[4,1,512,1280]{3,2,1,0:T(8,128)(2,1)}) custom-call(bf16[512,1792]{1,0:T(8,128)(2,1)} %multiply_convert_fusion.x_ref, bf16[8,4,2,224,1216]{4,3,2,1,0:T(8,128)(2,1)} %bitcast.298), custom_call_target="tpu_custom_call" | custom-call | flops 26776436736 | bytes 1 | tf_op jit(solution)/shard_map/pallas_call | solution.py:623
  497.3 17.7 %shard_map.262 = f32[512,1792]{1,0:T(8,128)} custom-call(s32[10]{0:T(128)} %xor_multiply_fusion.offsets, s32[4]{0:T(128)} %iota_xor_fusion.places, bf16[4,1,512,1280]{3,2,1,0:T(8,128)(2,1)} %get-tuple-element.157.y_ref.right0, bf16[4,224,1280]{2,1,0:T(8,128)(2,1)} %get-tuple-element.136.refs_0_, bf16[4,224,1280]{2,1,0:T(8,128)(2,1)} %collective-permute-done.1.refs_1_, ...), custom_call_target="tpu_custom_call" | custom-call | flops 14092861440 | bytes 1 | tf_op jit(solution)/shard_map/pallas_call | solution.py:589
  515.0 9.1 shard_map.263
  524.1 8.9 shard_map.264
  533.0 28.5 %shard_map.265 = (bf16[4,2,512,1280]{3,2,1,0:T(8,128)(2,1)}, f32[512,1792]{1,0:T(8,128)}) custom-call(f32[4,512,1280]{2,1,0:T(8,128)} %shard_map.259.grad_ref, bf16[8,4,2,224,1216]{4,3,2,1,0:T(8,128)(2,1)} %bitcast.299, bf16[4,512,1216]{2,1,0:T(8,128)(2,1)} %get-tuple-element.161.slope_ref, bf16[4,512,1216]{2,1,0:T(8,128)(2,1)} %get-tuple-element.162.silu_ref), custom_call_target="tpu_custom_call" | custom-call | flops 1 | bytes 1 | tf_op jit(solution)/shard_map/pallas_call | solution.py:656
  570.4 10.2 shard_map.266
  595.9 27.2 %collective-permute-done.25 = bf16[2,2,224,1280]{3,2,1,0:T(8,128)(2,1)} collective-permute-done((bf16[2,2,224,1280]{3,2,1,0:T(8,128)(2,1)}, bf16[2,2,224,1280]{3,2,1,0:T(8,128)(2,1)}, u32[]{:S(2)}, u32[]{:S(2)}) %collective-permute-start.25) | collective-permute-done | bytes 2293792 | tf_op jit(solution)/shard_map/ppermute | solution.py:47
  648.2 8.9 shard_map.267
  657.1 8.9 shard_map.268
  666.0 8.9 shard_map.269
  674.9 8.9 shard_map.270
  697.8 45.1 %shard_map.273 = (bf16[4096,128]{1,0:T(8,128)(2,1)}, bf16[4096,16]{1,0:T(8,128)(2,1)}) custom-call(bf16[4096,128]{1,0:T(8,128)(2,1)} %bitcast.333, bf16[4096,16]{1,0:T(8,128)(2,1)} %bitcast.327, f32[4096,128]{1,0:T(8,128)} %get-tuple-element.167.kept, bf16[4096,128]{1,0:T(8,128)(2,1)} %bitcast.60.grad, f32[4096,1]{1,0:T(8,128)} %copy.148.seg_col, ...), custom_call_target="tpu_custom_call" | custom-call | flops 51539607552 | bytes 1 | tf_op jit(solution)/shard_map/pallas_call | solution.py:891
  755.0 44.7 %shard_map.274 = (bf16[4096,128]{1,0:T(8,128)(2,1)}, bf16[4096,16]{1,0:T(8,128)(2,1)}) custom-call(bf16[4096,128]{1,0:T(8,128)(2,1)} %bitcast.335, bf16[4096,16]{1,0:T(8,128)(2,1)} %bitcast.329, f32[4096,128]{1,0:T(8,128)} %get-tuple-element.190.kept, bf16[4096,128]{1,0:T(8,128)(2,1)} %bitcast.67.grad, f32[4096,1]{1,0:T(8,128)} %copy.148.seg_col, ...), custom_call_target="tpu_custom_call" | custom-call | flops 51539607552 | bytes 1 | tf_op jit(solution)/shard_map/pallas_call | solution.py:891
  802.5 15.2 %collective-permute-done.36 = bf16[2,2,224,1280]{3,2,1,0:T(8,128)(2,1)} collective-permute-done((bf16[2,2,224,1280]{3,2,1,0:T(8,128)(2,1)}, bf16[2,2,224,1280]{3,2,1,0:T(8,128)(2,1)}, u32[]{:S(2)}, u32[]{:S(2)}) %collective-permute-start.36) | collective-permute-done | bytes 2293792 | tf_op jit(solution)/shard_map/ppermute | solution.py:47
  835.2 30.1 %collective-permute-done.38 = bf16[2,224,1280]{2,1,0:T(8,128)(2,1)S(1)} collective-permute-done((bf16[2,224,1280]{2,1,0:T(8,128)(2,1)S(1)}, bf16[2,224,1280]{2,1,0:T(8,128)(2,1)S(1)}, u32[]{:S(2)}, u32[]{:S(2)}) %collective-permute-start.38) | collective-permute-done | bytes 1146912 | tf_op jit(solution)/shard_map/ppermute | solution.py:47
  865.4 24.2 %collective-permute-done.40 = bf16[2,224,1280]{2,1,0:T(8,128)(2,1)S(1)} collective-permute-done((bf16[2,224,1280]{2,1,0:T(8,128)(2,1)S(1)}, bf16[2,224,1280]{2,1,0:T(8,128)(2,1)S(1)}, u32[]{:S(2)}, u32[]{:S(2)}) %collective-permute-start.40) | collective-permute-done | bytes 1146912 | tf_op jit(solution)/shard_map/ppermute | solution.py:47
  919.8 12.3 %shard_map.275 = (bf16[4,512,1024]{2,1,0:T(8,128)(2,1)}, f32[4,3,448]{2,1,0:T(4,128)}) custom-call(bf16[4,512,448]{2,1,0:T(8,128)(2,1)} %get-tuple-element.164.v_ref, f32[4,512,448]{2,1,0:T(8,128)} %get-tuple-element.165.f_ref, f32[4,2,16,448]{3,2,1,0:T(8,128)} %get-tuple-element.166.side_ref, f32[512,4]{1,0:T(8,128)} %stack.83.same_ref, ...), custom_call_target="tpu_custom_call" | custom-call | flops 1 | bytes 1 | tf_op jit(solution)/shard_map/pallas_call | solution.py:1059
  965.4 13.3 %shard_map.278 = f32[512,1792]{1,0:T(8,128)} custom-call(bf16[4,512,1024]{2,1,0:T(8,128)(2,1)} %get-tuple-element.227.y_ref, bf16[8,4,1,240,1024]{4,3,2,1,0:T(8,128)(2,1)} %get-tuple-element.130.w_ref), custom_call_target="tpu_custom_call" | custom-call | flops 1 | bytes 1 | tf_op jit(solution)/shard_map/pallas_call | solution.py:463
  996.1 36.3 %collective-permute-done.50 = bf16[2,224,1280]{2,1,0:T(8,128)(2,1)} collective-permute-done((bf16[2,224,1280]{2,1,0:T(8,128)(2,1)}, bf16[2,224,1280]{2,1,0:T(8,128)(2,1)}, u32[]{:S(2)}, u32[]{:S(2)}) %collective-permute-start.50) | collective-permute-done | bytes 1146912 | tf_op jit(solution)/shard_map/ppermute | solution.py:47
  1044.2 12.4 %collective-permute-done.52 = bf16[2,224,1024]{2,1,0:T(8,128)(2,1)S(1)} collective-permute-done((bf16[2,224,1024]{2,1,0:T(8,128)(2,1)S(1)}, bf16[2,224,1024]{2,1,0:T(8,128)(2,1)S(1)}, u32[]{:S(2)}, u32[]{:S(2)}) %collective-permute-start.52) | collective-permute-done | bytes 917536 | tf_op jit(solution)/shard_map/ppermute | solution.py:47
  1065.7 25.1 %collective-permute-start.56 = (bf16[224,1024]{1,0:T(8,128)(2,1)}, bf16[224,1024]{1,0:T(8,128)(2,1)S(1)}, u32[]{:S(2)}, u32[]{:S(2)}) collective-permute-start(bf16[224,1024]{1,0:T(8,128)(2,1)} %get-tuple-element.321), channel_id=1, source_target_pairs={{0,2},{1,3},{2,0},{3,1},{4,6},{5,7},{6,4},{7,5},{8,10},{9,11},{10,... | collective-permute-start | bytes 1376264 | tf_op jit(solution)/shard_map/ppermute | solution.py:47
  1097.1 24.7 %all-to-all-done.8 = f32[32,1,280]{2,1,0:T(1,128)S(1)} async-done(((f32[32,1,280]{2,1,0:T(1,128)}), f32[32,1,280]{2,1,0:T(1,128)S(1)}, u32[]{:S(2)}, u32[]{:S(2)}) %all-to-all-start.8) | async-done | bytes 35872 | tf_op jit(solution)/shard_map/all_to_all | solution.py:1289
  (426 shorter events, 329.7 us)
Async XLA Ops:
  7.3 463.1 %all-gather.3.cloned.1.call-start = ((), (), s32[]{:S(2)}) async-start(), calls=%async_computation.11 | async-start | bytes 37847040 | tf_op jit(solution)/shard_map/all_gather | solution.py:59
  158.8 86.1 %collective-permute-start.1 = (bf16[4,224,1280]{2,1,0:T(8,128)(2,1)}, bf16[4,224,1280]{2,1,0:T(8,128)(2,1)}, u32[]{:S(2)}, u32[]{:S(2)}) collective-permute-start(bf16[4,224,1280]{2,1,0:T(8,128)(2,1)} %get-tuple-element.136.refs_0_), channel_id=1, source_target_pairs={{0,8},{4,12},{8,0},{12,4},{16,24},{20,28},{24,16},{28,20},{1,9},{5... | collective-permute-start | bytes 6881288 | tf_op jit(solution)/shard_map/ppermute | solution.py:47
  161.1 86.1 %collective-permute-start.2 = (bf16[4,224,1280]{2,1,0:T(8,128)(2,1)}, bf16[4,224,1280]{2,1,0:T(8,128)(2,1)}, u32[]{:S(2)}, u32[]{:S(2)}) collective-permute-start(bf16[4,224,1280]{2,1,0:T(8,128)(2,1)} %get-tuple-element.136.refs_0_), channel_id=1, source_target_pairs={{0,16},{4,20},{8,24},{12,28},{16,0},{20,4},{24,8},{28,12},{1,17},{... | collective-permute-start | bytes 6881288 | tf_op jit(solution)/shard_map/ppermute | solution.py:47
  204.6 74.4 %all-to-all-start = ((bf16[32,144,128]{2,1,0:T(8,128)(2,1)}), bf16[32,144,128]{2,1,0:T(8,128)(2,1)S(1)}, u32[]{:S(2)}, u32[]{:S(2)}) async-start(bf16[32,144,128]{2,1,0:T(8,128)(2,1)} %pad_maximum_fusion), calls=%async_computation | async-start | bytes 2359296 | tf_op jit(solution)/shard_map/all_to_all | solution.py:727
  280.4 91.8 %all-to-all-start.2 = ((bf16[32,144,128]{2,1,0:T(8,128)(2,1)}), bf16[32,144,128]{2,1,0:T(8,128)(2,1)S(1)}, u32[]{:S(2)}, u32[]{:S(2)}) async-start(bf16[32,144,128]{2,1,0:T(8,128)(2,1)} %bitcast.25), calls=%async_computation.2 | async-start | bytes 2359296 | tf_op jit(solution)/shard_map/all_to_all | solution.py:727
  306.9 64.7 %collective-permute-start.6 = (bf16[2,224,1280]{2,1,0:T(8,128)(2,1)}, bf16[2,224,1280]{2,1,0:T(8,128)(2,1)}, u32[]{:S(2)}, u32[]{:S(2)}) collective-permute-start(bf16[2,224,1280]{2,1,0:T(8,128)(2,1)} %slice.329), channel_id=1, source_target_pairs={{0,16},{4,20},{8,24},{12,28},{16,0},{20,4},{24,8},{28,12},{1,17},{... | collective-permute-start | bytes 3440648 | tf_op jit(solution)/shard_map/ppermute | solution.py:47
  308.8 62.9 %collective-permute-start.7 = (bf16[2,224,1280]{2,1,0:T(8,128)(2,1)}, bf16[2,224,1280]{2,1,0:T(8,128)(2,1)}, u32[]{:S(2)}, u32[]{:S(2)}) collective-permute-start(bf16[2,224,1280]{2,1,0:T(8,128)(2,1)} %slice.330), channel_id=1, source_target_pairs={{0,8},{4,12},{8,0},{12,4},{16,24},{20,28},{24,16},{28,20},{1,9},{5... | collective-permute-start | bytes 3440648 | tf_op jit(solution)/shard_map/ppermute | solution.py:47
  342.5 60.3 %collective-permute-start.8 = (bf16[4,224,1280]{2,1,0:T(8,128)(2,1)}, bf16[4,224,1280]{2,1,0:T(8,128)(2,1)}, u32[]{:S(2)}, u32[]{:S(2)}) collective-permute-start(bf16[4,224,1280]{2,1,0:T(8,128)(2,1)} %get-tuple-element.136.refs_0_), channel_id=1, source_target_pairs={{0,4},{4,0},{8,12},{12,8},{16,20},{20,16},{24,28},{28,24},{1,5},{5... | collective-permute-start | bytes 6881288 | tf_op jit(solution)/shard_map/ppermute | solution.py:47
  561.5 85.8 %collective-permute-start.27 = (bf16[4,2,512,1280]{3,2,1,0:T(8,128)(2,1)}, bf16[4,2,512,1280]{3,2,1,0:T(8,128)(2,1)}, u32[]{:S(2)}, u32[]{:S(2)}) collective-permute-start(bf16[4,2,512,1280]{3,2,1,0:T(8,128)(2,1)} %get-tuple-element.178.right0), channel_id=1, source_target_pairs={{0,4},{4,0},{8,12},{12,8},{16,20},{20,16},{24,28},{28,24},{1,5},{5... | collective-permute-start | bytes 31457288 | tf_op jit(solution)/shard_map/ppermute | solution.py:47
  561.7 61.4 %collective-permute-start.25 = (bf16[2,2,224,1280]{3,2,1,0:T(8,128)(2,1)}, bf16[2,2,224,1280]{3,2,1,0:T(8,128)(2,1)}, u32[]{:S(2)}, u32[]{:S(2)}) collective-permute-start(bf16[2,2,224,1280]{3,2,1,0:T(8,128)(2,1)} %get-tuple-element.158), channel_id=1, source_target_pairs={{0,8},{4,12},{8,0},{12,4},{16,24},{20,28},{24,16},{28,20},{1,9},{5... | collective-permute-start | bytes 6881288 | tf_op jit(solution)/shard_map/ppermute | solution.py:47
  562.7 61.4 %collective-permute-start.26 = (bf16[2,2,224,1280]{3,2,1,0:T(8,128)(2,1)}, bf16[2,2,224,1280]{3,2,1,0:T(8,128)(2,1)}, u32[]{:S(2)}, u32[]{:S(2)}) collective-permute-start(bf16[2,2,224,1280]{3,2,1,0:T(8,128)(2,1)} %get-tuple-element.159), channel_id=1, source_target_pairs={{0,16},{4,20},{8,24},{12,28},{16,0},{20,4},{24,8},{28,12},{1,17},{... | collective-permute-start | bytes 6881288 | tf_op jit(solution)/shard_map/ppermute | solution.py:47
  580.7 52.5 %all-to-all-start.5 = ((bf16[32,128,128]{2,1,0:T(8,128)(2,1)}), bf16[32,128,128]{2,1,0:T(8,128)(2,1)}, u32[]{:S(2)}, u32[]{:S(2)}) async-start(bf16[32,128,128]{2,1,0:T(8,128)(2,1)} %bitcast.338), calls=%async_computation.5 | async-start | bytes 2097152 | tf_op jit(solution)/shard_map/all_to_all | solution.py:727
  591.1 56.2 %collective-permute-start.24 = (bf16[4,224,512]{2,1,0:T(8,128)(2,1)}, bf16[4,224,512]{2,1,0:T(8,128)(2,1)S(1)}, u32[]{:S(2)}, u32[]{:S(2)}) collective-permute-start(bf16[4,224,512]{2,1,0:T(8,128)(2,1)} %get-tuple-element.327), channel_id=1, source_target_pairs={{0,4},{4,0},{8,12},{12,8},{16,20},{20,16},{24,28},{28,24},{1,5},{5... | collective-permute-start | bytes 2752520 | tf_op jit(solution)/shard_map/ppermute | solution.py:47
  629.2 54.7 %collective-permute-start.29 = (bf16[2,224,1280]{2,1,0:T(8,128)(2,1)}, bf16[2,224,1280]{2,1,0:T(8,128)(2,1)}, u32[]{:S(2)}, u32[]{:S(2)}) collective-permute-start(bf16[2,224,1280]{2,1,0:T(8,128)(2,1)} %fusion.26), channel_id=1, source_target_pairs={{0,16},{4,20},{8,24},{12,28},{16,0},{20,4},{24,8},{28,12},{1,17},{... | collective-permute-start | bytes 3440648 | tf_op jit(solution)/shard_map/ppermute | solution.py:47
  630.3 53.5 %collective-permute-start.30 = (bf16[2,224,1280]{2,1,0:T(8,128)(2,1)}, bf16[2,224,1280]{2,1,0:T(8,128)(2,1)}, u32[]{:S(2)}, u32[]{:S(2)}) collective-permute-start(bf16[2,224,1280]{2,1,0:T(8,128)(2,1)} %fusion.27), channel_id=1, source_target_pairs={{0,8},{4,12},{8,0},{12,4},{16,24},{20,28},{24,16},{28,20},{1,9},{5... | collective-permute-start | bytes 3440648 | tf_op jit(solution)/shard_map/ppermute | solution.py:47
  633.1 61.5 %all-to-all-start.4 = ((bf16[32,128,128]{2,1,0:T(8,128)(2,1)}), bf16[32,128,128]{2,1,0:T(8,128)(2,1)}, u32[]{:S(2)}, u32[]{:S(2)}) async-start(bf16[32,128,128]{2,1,0:T(8,128)(2,1)} %bitcast.336), calls=%async_computation.4 | async-start | bytes 2097152 | tf_op jit(solution)/shard_map/all_to_all | solution.py:727
  690.3 61.3 %collective-permute-start.33 = (bf16[224,1280]{1,0:T(8,128)(2,1)}, bf16[224,1280]{1,0:T(8,128)(2,1)S(1)}, u32[]{:S(2)}, u32[]{:S(2)}) collective-permute-start(bf16[224,1280]{1,0:T(8,128)(2,1)} %get-tuple-element.315), channel_id=1, source_target_pairs={{0,1},{1,0},{2,3},{3,2},{4,5},{5,4},{6,7},{7,6},{8,9},{9,8},{10,11... | collective-permute-start | bytes 1720328 | tf_op jit(solution)/shard_map/ppermute | solution.py:47
  692.0 59.6 %collective-permute-start.34 = (bf16[224,1280]{1,0:T(8,128)(2,1)}, bf16[224,1280]{1,0:T(8,128)(2,1)S(1)}, u32[]{:S(2)}, u32[]{:S(2)}) collective-permute-start(bf16[224,1280]{1,0:T(8,128)(2,1)} %get-tuple-element.316), channel_id=1, source_target_pairs={{0,2},{1,3},{2,0},{3,1},{4,6},{5,7},{6,4},{7,5},{8,10},{9,11},{10,... | collective-permute-start | bytes 1720328 | tf_op jit(solution)/shard_map/ppermute | solution.py:47
  694.4 57.2 %collective-permute-start.35 = (bf16[224,1280]{1,0:T(8,128)(2,1)}, bf16[224,1280]{1,0:T(8,128)(2,1)S(1)}, u32[]{:S(2)}, u32[]{:S(2)}) collective-permute-start(bf16[224,1280]{1,0:T(8,128)(2,1)} %get-tuple-element.317), channel_id=1, source_target_pairs={{0,3},{1,2},{2,1},{3,0},{4,7},{5,6},{6,5},{7,4},{8,11},{9,10},{10,... | collective-permute-start | bytes 1720328 | tf_op jit(solution)/shard_map/ppermute | solution.py:47
  694.7 57.0 %collective-permute-start.31 = (bf16[2,2,224,1280]{3,2,1,0:T(8,128)(2,1)}, bf16[2,2,224,1280]{3,2,1,0:T(8,128)(2,1)}, u32[]{:S(2)}, u32[]{:S(2)}) collective-permute-start(bf16[2,2,224,1280]{3,2,1,0:T(8,128)(2,1)} %get-tuple-element.192), channel_id=1, source_target_pairs={{0,8},{4,12},{8,0},{12,4},{16,24},{20,28},{24,16},{28,20},{1,9},{5... | collective-permute-start | bytes 6881288 | tf_op jit(solution)/shard_map/ppermute | solution.py:47
  696.4 55.3 %collective-permute-start.32 = (bf16[2,2,224,1280]{3,2,1,0:T(8,128)(2,1)}, bf16[2,2,224,1280]{3,2,1,0:T(8,128)(2,1)}, u32[]{:S(2)}, u32[]{:S(2)}) collective-permute-start(bf16[2,2,224,1280]{3,2,1,0:T(8,128)(2,1)} %get-tuple-element.193), channel_id=1, source_target_pairs={{0,16},{4,20},{8,24},{12,28},{16,0},{20,4},{24,8},{28,12},{1,17},{... | collective-permute-start | bytes 6881288 | tf_op jit(solution)/shard_map/ppermute | solution.py:47
  747.8 71.1 %all-to-all-start.6 = ((bf16[32,160,128]{2,1,0:T(8,128)(2,1)}), bf16[32,160,128]{2,1,0:T(8,128)(2,1)S(1)}, u32[]{:S(2)}, u32[]{:S(2)}) async-start(bf16[32,160,128]{2,1,0:T(8,128)(2,1)} %fusion.24), calls=%async_computation.6 | async-start | bytes 2621440 | tf_op jit(solution)/shard_map/all_to_all | solution.py:727
  751.7 66.1 %collective-permute-start.36 = (bf16[2,2,224,1280]{3,2,1,0:T(8,128)(2,1)}, bf16[2,2,224,1280]{3,2,1,0:T(8,128)(2,1)}, u32[]{:S(2)}, u32[]{:S(2)}) collective-permute-start(bf16[2,2,224,1280]{3,2,1,0:T(8,128)(2,1)} %get-tuple-element.196), channel_id=1, source_target_pairs={{0,8},{4,12},{8,0},{12,4},{16,24},{20,28},{24,16},{28,20},{1,9},{5... | collective-permute-start | bytes 6881288 | tf_op jit(solution)/shard_map/ppermute | solution.py:47
  753.5 64.3 %collective-permute-start.37 = (bf16[2,2,224,1280]{3,2,1,0:T(8,128)(2,1)}, bf16[2,2,224,1280]{3,2,1,0:T(8,128)(2,1)}, u32[]{:S(2)}, u32[]{:S(2)}) collective-permute-start(bf16[2,2,224,1280]{3,2,1,0:T(8,128)(2,1)} %get-tuple-element.197), channel_id=1, source_target_pairs={{0,16},{4,20},{8,24},{12,28},{16,0},{20,4},{24,8},{28,12},{1,17},{... | collective-permute-start | bytes 6881288 | tf_op jit(solution)/shard_map/ppermute | solution.py:47
  818.9 70.8 %all-to-all-start.7 = ((bf16[32,160,128]{2,1,0:T(8,128)(2,1)}), bf16[32,160,128]{2,1,0:T(8,128)(2,1)S(1)}, u32[]{:S(2)}, u32[]{:S(2)}) async-start(bf16[32,160,128]{2,1,0:T(8,128)(2,1)} %fusion.25), calls=%async_computation.7 | async-start | bytes 2621440 | tf_op jit(solution)/shard_map/all_to_all | solution.py:727
  823.6 267.2 %reduce-scatter.2.cloned.1.call-start = ((), (), s32[]{:S(2)}) async-start(), calls=%async_computation.10 | async-start | bytes 1146880 | tf_op jit(solution)/shard_map/reduce_scatter | solution.py:1274
  832.3 57.3 %collective-permute-start.40 = (bf16[2,224,1280]{2,1,0:T(8,128)(2,1)S(1)}, bf16[2,224,1280]{2,1,0:T(8,128)(2,1)S(1)}, u32[]{:S(2)}, u32[]{:S(2)}) collective-permute-start(bf16[2,224,1280]{2,1,0:T(8,128)(2,1)S(1)} %fusion.30), channel_id=1, source_target_pairs={{0,16},{4,20},{8,24},{12,28},{16,0},{20,4},{24,8},{28,12},{1,17},{... | collective-permute-start | bytes 3440648 | tf_op jit(solution)/shard_map/ppermute | solution.py:47
  834.6 55.2 %collective-permute-start.41 = (bf16[2,224,1280]{2,1,0:T(8,128)(2,1)S(1)}, bf16[2,224,1280]{2,1,0:T(8,128)(2,1)}, u32[]{:S(2)}, u32[]{:S(2)}) collective-permute-start(bf16[2,224,1280]{2,1,0:T(8,128)(2,1)S(1)} %fusion.31), channel_id=1, source_target_pairs={{0,8},{4,12},{8,0},{12,4},{16,24},{20,28},{24,16},{28,20},{1,9},{5... | collective-permute-start | bytes 3440648 | tf_op jit(solution)/shard_map/ppermute | solution.py:47
  940.0 92.4 %collective-permute-start.50 = (bf16[2,224,1280]{2,1,0:T(8,128)(2,1)}, bf16[2,224,1280]{2,1,0:T(8,128)(2,1)}, u32[]{:S(2)}, u32[]{:S(2)}) collective-permute-start(bf16[2,224,1280]{2,1,0:T(8,128)(2,1)} %get-tuple-element.311), channel_id=1, source_target_pairs={{0,2},{1,3},{2,0},{3,1},{4,6},{5,7},{6,4},{7,5},{8,10},{9,11},{10,... | collective-permute-start | bytes 3440648 | tf_op jit(solution)/shard_map/ppermute | solution.py:47
  942.4 90.0 %collective-permute-start.51 = (bf16[2,224,1280]{2,1,0:T(8,128)(2,1)}, bf16[2,224,1280]{2,1,0:T(8,128)(2,1)}, u32[]{:S(2)}, u32[]{:S(2)}) collective-permute-start(bf16[2,224,1280]{2,1,0:T(8,128)(2,1)} %get-tuple-element.309), channel_id=1, source_target_pairs={{0,3},{1,2},{2,1},{3,0},{4,7},{5,6},{6,5},{7,4},{8,11},{9,10},{10,... | collective-permute-start | bytes 3440648 | tf_op jit(solution)/shard_map/ppermute | solution.py:47
  1064.2 60.2 %collective-permute-start.57 = (bf16[224,1024]{1,0:T(8,128)(2,1)}, bf16[224,1024]{1,0:T(8,128)(2,1)S(1)}, u32[]{:S(2)}, u32[]{:S(2)}) collective-permute-start(bf16[224,1024]{1,0:T(8,128)(2,1)} %get-tuple-element.322), channel_id=1, source_target_pairs={{0,3},{1,2},{2,1},{3,0},{4,7},{5,6},{6,5},{7,4},{8,11},{9,10},{10,... | collective-permute-start | bytes 1376264 | tf_op jit(solution)/shard_map/ppermute | solution.py:47
  1065.7 58.7 %collective-permute-start.56 = (bf16[224,1024]{1,0:T(8,128)(2,1)}, bf16[224,1024]{1,0:T(8,128)(2,1)S(1)}, u32[]{:S(2)}, u32[]{:S(2)}) collective-permute-start(bf16[224,1024]{1,0:T(8,128)(2,1)} %get-tuple-element.321), channel_id=1, source_target_pairs={{0,2},{1,3},{2,0},{3,1},{4,6},{5,7},{6,4},{7,5},{8,10},{9,11},{10,... | collective-permute-start | bytes 1376264 | tf_op jit(solution)/shard_map/ppermute | solution.py:47
  (107 other events, 1787.2 us)
Sparse Core Ops, SparseCore 0:
  11.5 380.6 all-gather.2
  996.2 32.0 reduce-scatter.1

commit v3 on v2

--- a/solution.py
+++ b/solution.py
@@ -121,7 +121,7 @@
         )
         started[row, r].start()
 
-    for r in (1, 2, 3):
+    for r in (2, 1):
         start(0, r, shard, place, line, to(place, lines[r]))
     copies += [
         remote(edge, edges.at[i], edge_send.at[i], edge_recv.at[i], partner)
@@ -129,21 +129,30 @@
     ]
     for each in copies:
         each.start()
-    for r in range(4):
+    for r in (0, 2, 1, 3):
         if r > 0:
             started[0, r].wait_recv()
         source = shard if r == 0 else whole.at[place, lines[r], 0]
+        if r == 2:
+            start(0, 3, source, place, lines[r], to(place, lines[1]))
         start(1, r, source, place, lines[r], to(by_x, line))
         start(2, r, source, place, lines[r], to(by_y, line))
         start(3, r, source, place, lines[r], to(by_core, line))
-    more = [
-        remote(other, target.at[r], line_send.at[i, r], line_recv.at[i, r], to(place, lines[r]))
+    more = {
+        (i, r): remote(
+            target.at[2] if r == 3 else other,
+            target.at[r],
+            line_send.at[i, r],
+            line_recv.at[i, r],
+            to(place, lines[2 if r == 2 else 1]),
+        )
         for i, (other, target) in enumerate(zip(others, lined))
-        for r in (1, 2, 3)
-    ]
-    for each in more:
-        each.start()
-    for r in range(4):
+        for r in (2, 1, 3)
+    }
+    for (i, r), each in more.items():
+        if r < 3:
+            each.start()
+    for r in (0, 2, 1, 3):
         z = lines[r]
         started[1, r].wait_recv()
         if r < 2:
@@ -153,7 +162,10 @@
         if r >= 2:
             start(4, r, whole.at[by_y, z, 0], by_y, z, to(by_x, line))
         start(6, r, whole.at[by_y, z, 0], by_y, z, to(by_core, line))
-    for r in range(4):
+    for i in range(count):
+        more[i, 2].wait_recv()
+        more[i, 3].start()
+    for r in (0, 2, 1, 3):
         z = lines[r]
         started[4, r].wait_recv()
         start(7, r, whole.at[corner, z, 0], corner, z, to(by_core, line))
@@ -161,7 +173,11 @@
         each.wait_send()
         if row in (3, 5, 6, 7):
             each.wait_recv()
-    for each in copies + more:
+    for (i, r), each in more.items():
+        each.wait_send()
+        if r != 2:
+            each.wait_recv()
+    for each in copies:
         each.wait()
 
 
@@ -203,7 +219,9 @@
         self.order = by_place(jnp.arange(lax.axis_size("head"), dtype=jnp.int32))
         if paired():
             if own is None:
-                own = jnp.stack([shard] + [swap(shard, r, "head") for r in (1, 2, 3)])
+                two = swap(shard, 2, "head")
+                one = swap(jnp.stack([shard, two]), 1, "head")
+                own = jnp.stack([shard, one[0], two, one[1]])
             self.own = own
         else:
             own = lax.all_gather(shard, "head")
@@ -400,23 +418,36 @@
 
 
 class Along:
-    def __init__(self, blocks, *after):
+    def __init__(self, blocks):
         if not paired():
-            self.mine, self.coming = lax.psum_scatter(blocks, "head", scatter_dimension=0), []
-            self.sent = ()
+            self.total = lax.psum_scatter(blocks, "head", scatter_dimension=0).astype(f32)
+            self.coming, self.sent = (), ()
             return
         here = lax.axis_index("head")
         pick = lambda r: lax.dynamic_index_in_dim(blocks, here ^ r, 0, keepdims=False)
-        sent = [pick(r) for r in (1, 2, 3)]
-        self.sent = tuple(sent)
+        self.kept = (pick(0), pick(2))
+        sent = jnp.stack([pick(1), pick(3)])
+        self.sent = (sent,)
+        self.coming = (swap(sent, 1, "head"),)
+
+    def go(self, *after):
+        if not paired():
+            return
+        (arrived,) = self.coming
         if after:
-            sent = [tie(block, *after) for block in sent]
-        self.mine = pick(0)
-        self.coming = [swap(block, r, "head") for r, block in zip((1, 2, 3), sent)]
+            arrived = tie(arrived, *after)
+        self.stay = self.kept[0].astype(f32) + arrived[0].astype(f32)
+        sent = (self.kept[1].astype(f32) + arrived[1].astype(f32)).astype(bf16)
+        self.sent = (sent,)
+        self.coming = (swap(sent, 2, "head"),)
 
     def finish(self, *after):
-        coming = [tie(block, *after) for block in self.coming] if after else self.coming
-        return sum([block.astype(f32) for block in coming], self.mine.astype(f32))
+        if not paired():
+            return self.total
+        (arrived,) = self.coming
+        if after:
+            arrived = tie(arrived, *after)
+        return self.stay + arrived.astype(f32)
 
 
 def whole_rows(ref, kind=0):
@@ -1138,10 +1169,10 @@
     edge = jnp.stack([tokens[:, -2:], tokens[:, :2]]).reshape(-1, D)
     edge = jnp.pad(edge, ((0, grouped(edge.shape[0], 16) - edge.shape[0]), (0, 0)))
     first_w, edges, lined = gather_first(
-        jnp.concatenate([first, small.reshape(below, columns)]), edge, [down_shard]
+        jnp.concatenate([first, small.reshape(below, columns)]), edge, [down_shard, out_shard]
     )
     beside = jnp.concatenate([edges[0, : 2 * batch], edges[1, 2 * batch : 4 * batch]])
-    gate_up_w = gather(jnp.stack([gate_weight, up_weight]))
+    gate_up_w = gather(tie(jnp.stack([gate_weight, up_weight]), first_w))
     down_w = Pieces(down_shard, lined[0])
 
     small = first_w[:, :, 0, rows_here:].reshape(seq, head, -1).astype(f32)
@@ -1170,6 +1201,8 @@
     same = same.reshape(count, 4)
     cot_left = Left(cot_low)
     normed = tie(normed, down_w.own, *cot_left.pending())
+    out_w = Pieces(out_shard, lined[1])
+    out_sides = out_w.sides(first_w)
     down_sides = down_w.sides(first_w)
     v_low, filter_pre, side, *sent = project(lay, normed, normed_beside, same, taps, first_w)
     my_seg = lax.dynamic_index_in_dim(segs, lay.sequence(), 0, keepdims=False)
@@ -1182,30 +1215,24 @@
         blocks = lay.exchange(blocks.reshape(-1, span + lay.key_rows, LANES))
         mains.append(lay.all_parts(blocks[:, :span].reshape(-1, LANES)))
         all_keys.append(lay.all_parts(lay.unpack_keys(blocks[:, span:]).reshape(-1, FEAT)))
-    mains[0] = tie(mains[0], *down_sides)
-    down_w.far(mains[0])
+    mains[-1] = tie(mains[-1], *out_sides, *down_sides)
+    out_w.far(mains[-1])
+    down_w.far(mains[-1])
     for j in heads:
         attended, sent = attend(mains[j], all_keys[j], my_seg)
         kept.append(attended)
         blocks = lay.own_part(sent.reshape(-1, span, LANES))
-        if j == 0:
-            out_w = Pieces(tie(out_shard, blocks))
-        if j == lay.heads - 1:
-            blocks = tie(blocks, out_w.own, *[piece for piece, _ in down_w.pieces])
-            out_sides = out_w.sides(blocks)
         if j > 0:
             blocks = tie(blocks, low[-1])
         low.append(lay.exchange(blocks))
-    grad_hidden = spread(tie(cot_low, blocks), down_w)
-    low[-1] = tie(low[-1], grad_hidden, *out_sides)
-    out_w.far(grad_hidden)
     att_low, projected = out_of_pieces(lay, [lay.by_place(blocks) for blocks in low], out_w)
 
     residual = x + projected
     scale_two = inverse_rms(residual)
     normed_two = (residual * scale_two * gain_two).astype(bf16)
     out_sum = Scatter(None, att_low, True)
-    normed_two = tie(normed_two, out_sum.other_side())
+    grad_hidden = spread(tie(cot_low, att_low), down_w)
+    normed_two = tie(normed_two, out_sum.other_side(), grad_hidden)
     slope, silu, hidden = hidden_of(normed_two, gate_up_w)
     down_sum = Scatter(cot_left, hidden)
     ffn_out = collect(hidden, down_w)
@@ -1239,10 +1266,11 @@
             if j > 0:
                 grad_rows = tie(grad_rows, sent)
             up_sum.go(grad_rows, *gate_sum.pending())
-            grad_rows = tie(grad_rows, *gate_sum.pending(), *down_sum.coming)
+            down_sum.go(grad_rows)
+            grad_rows = tie(grad_rows, *gate_sum.pending(), *down_sum.sent)
         grad_main, grad_key = attend_back(mains[j], all_keys[j], kept[j], grad_rows, my_seg)
         if j == lay.heads - 1:
-            grad_main = tie(grad_main, *up_sum.pending())
+            grad_main = tie(grad_main, *up_sum.pending(), *down_sum.coming)
         blocks = grad_main.reshape(-1, span, LANES)
         ahead = jnp.pad(blocks[1:, :16], ((0, 1), (0, 0), (0, 0)))
         packed = lay.pack_keys(grad_key.reshape(-1, span, FEAT))
@@ -1265,20 +1293,23 @@
         lay, backs, grad_keys, v_low, filter_pre, side, same, taps
     )
     tap_grads = jnp.swapaxes(tap_grads, 0, 1).reshape(3, D)
-    grad_first = tie(grad_first, *out_sum.pending(), *gate_up_sum.coming[:1])
+    grad_first = tie(grad_first, *out_sum.pending())
     first_sum = Scatter(Left(tie(normed, grad_first)), grad_first[:, None])
     out_sends = out_sum.second(*first_sum.given())
     first_sum.right = tie(first_sum.right, *out_sends)
     first_sum.products(True)
-    first_sum.go(*out_sum.pending())
-    out_grad = lax.psum_scatter(out_sum.last(*first_sum.made), "head", scatter_dimension=0)
+    first_sum.go()
     back_one = out_of(tie(grad_first, *first_sum.made), first_w)
+    gate_up_sum.go(back_one)
     gain_one_grad = jnp.sum(back_one * x * scale_one, axis=0)
-    first_sends = first_sum.second(back_one, *gate_up_sum.coming[1:])
-    gate_up_grad = gate_up_sum.finish(*first_sends)
-    down_grad = down_sum.finish(*first_sends)
-    first_sum = Along(first_sum.last(*first_sends))
-    out_grad = tie(out_grad, *first_sum.sent)
+    first_sends = first_sum.second(back_one)
+    out_sum = Along(out_sum.last(*first_sends))
+    first_sum = Along(first_sum.last(*out_sum.sent))
+    gate_up_grad = gate_up_sum.finish(*first_sum.sent)
+    down_grad = down_sum.finish(*first_sum.sent)
+    out_sum.go(*first_sum.sent)
+    first_sum.go(*out_sum.sent)
+    out_grad = out_sum.finish(*first_sum.sent)
     first_grad = first_sum.finish()
     grad_x = (grad_residual + norm_back(x, scale_one, gain_one, back_one)).astype(bf16)
     tokens_grad = grad_x.reshape(tokens.shape)

time: 1150 us -> 1100 us (0.957)
  waiting for transfers between devices: 256 us -> 328 us
  starting transfers between devices: 161 us -> 89.2 us
  Pallas kernels: 513 us -> 460 us
    pallas_call x1, Pallas kernels: 146 us -> 94.3 us  [gather_first(): pl.pallas_call(gather_kernel, in_specs=[anywhere] * (2 + count), out_spec...]
    all_to_all x8, waiting for transfers between devices: 29.5 us -> 71.7 us  [exchange(): lax.all_to_all(blocks, BOTH, 0, 0, tiled=True, axis_index_groups=self.gro...]
    all_to_all x8, starting transfers between devices: 76 us -> 36.6 us  [exchange(): lax.all_to_all(blocks, BOTH, 0, 0, tiled=True, axis_index_groups=self.gro...]
    ppermute x58 -> x54, waiting for transfers between devices: 202 us -> 240 us  [swap(): return lax.ppermute(block, axis, [(i, i ^ bit) for i in devices])]
    ppermute x58 -> x54, starting transfers between devices: 81.6 us -> 49.7 us  [swap(): return lax.ppermute(block, axis, [(i, i ^ bit) for i in devices])]
  transfers between devices with their start and end apart: 69 -> 64, of which waited for: 18 -> 25; matrix products, arithmetic and copies ran while one was open for 15% -> 15% of each run, Pallas kernels for 39% -> 27%
where the time goes in v3:
time: 1100 us; the launch traced here: 1090 us
  Pallas kernels  460 us (42%)
  waiting for transfers between devices  328 us (30%)
  local copies, waits for them, and re-layouts  100 us (9%)
  other arithmetic  93.1 us (8%)
  starting transfers between devices  89.2 us (8%)
  between operations  15.7 us (1%)
    ppermute x54, waiting for transfers between devices, swap(): return lax.ppermute(block, axis, [(i, i ^ bit) for i in devices])  240 us
    pallas_call x1, Pallas kernels, gather_first(): pl.pallas_call(gather_kernel, in_specs=[anywhere] * (2 + count), out_spec...  94.3 us
    pallas_call x2, Pallas kernels, attend_back(): pl.pallas_call(functools.partial(attend_back_kernel, chunk), grid=(steps,...  89.9 us
    pallas_call x10, Pallas kernels, weight_grads(): pl.pallas_call(functools.partial(grad_kernel, first), grid_spec=pltpu.Pre...  79.5 us
    all_to_all x8, waiting for transfers between devices, exchange(): lax.all_to_all(blocks, BOTH, 0, 0, tiled=True, axis_index_groups=self.gro...  71.7 us
    ppermute x54, starting transfers between devices, swap(): return lax.ppermute(block, axis, [(i, i ^ bit) for i in devices])  49.7 us
    pallas_call x2, Pallas kernels, attend(): pl.pallas_call(functools.partial(attend_kernel, chunk), grid=(steps,), in...  43.4 us
    all_to_all x8, starting transfers between devices, exchange(): lax.all_to_all(blocks, BOTH, 0, 0, tiled=True, axis_index_groups=self.gro...  36.6 us
  transfers between devices with their start and end apart: 64, of which 25 were waited for; matrix products, arithmetic and copies ran while one was open for 15% of the time, Pallas kernels for 27%

profile of v3, /device:TPU:0, one launch (start us, length us, event | category | flops | bytes accessed | tf_op | source)
XLA Modules:
  0.0 1085.9 jit_solution(16832515878613080389)
XLA Ops:
  19.6 94.3 %shard_map.255 = (bf16[8,4,1,240,1024]{4,3,2,1,0:T(8,128)(2,1)}, bf16[2,16,1792]{2,1,0:T(8,128)(2,1)}, bf16[4,224,1280]{2,1,0:T(8,128)(2,1)}, bf16[4,224,512]{2,1,0:T(8,128)(2,1)}) custom-call(bf16[240,1024]{1,0:T(8,128)(2,1)} %pad_maximum_fusion.7.shard, bf16[16,1792]{1,0:T(8,128)(2,1)} %reshape.340.edge, bf16[224,1280]{1,0:T(8,128)(2,1)} %pad.24.refs_0_, ...), custom_call_target="tpu_custom_call" | custom-call | flops 99999997952 | bytes 1 | tf_op jit(solution)/shard_map/pallas_call | solution.py:191
  133.8 15.9 %shard_map.256 = (bf16[4,512,448]{2,1,0:T(8,128)(2,1)}, f32[4,512,448]{2,1,0:T(8,128)}, f32[4,2,16,448]{3,2,1,0:T(8,128)}, bf16[4,2,4,128,128]{4,3,2,1,0:T(8,128...) custom-call(bf16[512,1792]{1,0:T(8,128)(2,1)} %fusion.3.x_ref, ...), custom_call_target="tpu_custom_call" | custom-call | flops 11274289152 | bytes 1 | tf_op jit(solution)/shard_map/pallas_call | solution.py:1015
  169.6 47.3 %collective-permute-done.1.refs_3_.refs_1_ = bf16[4,224,512]{2,1,0:T(8,128)(2,1)} collective-permute-done((bf16[4,224,512]{2,1,0:T(8,128)(2,1)}, bf16[4,224,512]{2,1,0:T(8,128)(2,1)}, u32[]{:S(2)}, u32[]{:S(2)}) %collective-permute-start.1) | collective-permute-done | bytes 917536 | tf_op jit(solution)/shard_map/ppermute | solution.py:47
  228.9 21.7 %shard_map.257 = (f32[4096,128]{1,0:T(8,128)}, bf16[4096,128]{1,0:T(8,128)(2,1)}) custom-call(bf16[4096,128]{1,0:T(8,128)(2,1)} %bitcast.325, bf16[4096,16]{1,0:T(8,128)(2,1)} %bitcast.319, f32[4096,1]{1,0:T(8,128)} %copy.161.seg_col, f32[8,1,512]{2,1,0:T(1,128)} %bitcast.346), custom_call_target="tpu_custom_call" | custom-call | flops 25769803776 | bytes 1 | tf_op jit(solution)/shard_map/pallas_call | solution.py:823
  250.6 45.5 %all-to-all-done.2 = bf16[32,144,128]{2,1,0:T(8,128)(2,1)} async-done(((bf16[32,144,128]{2,1,0:T(8,128)(2,1)}), bf16[32,144,128]{2,1,0:T(8,128)(2,1)}, u32[]{:S(2)}, u32[]{:S(2)}) %all-to-all-start.2) | async-done | bytes 1179680 | tf_op jit(solution)/shard_map/all_to_all | solution.py:758
  305.9 21.7 %shard_map.258 = (f32[4096,128]{1,0:T(8,128)}, bf16[4096,128]{1,0:T(8,128)(2,1)}) custom-call(bf16[4096,128]{1,0:T(8,128)(2,1)} %bitcast.323, bf16[4096,16]{1,0:T(8,128)(2,1)} %bitcast.317, f32[4096,1]{1,0:T(8,128)} %copy.161.seg_col, f32[8,1,512]{2,1,0:T(1,128)} %bitcast.347), custom_call_target="tpu_custom_call" | custom-call | flops 25769803776 | bytes 1 | tf_op jit(solution)/shard_map/pallas_call | solution.py:823
  327.6 23.3 %all-to-all-done.1 = bf16[32,128,128]{2,1,0:T(8,128)(2,1)S(1)} async-done(((bf16[32,128,128]{2,1,0:T(8,128)(2,1)}), bf16[32,128,128]{2,1,0:T(8,128)(2,1)S(1)}, u32[]{:S(2)}, u32[]{:S(2)}) %all-to-all-start.1) | async-done | bytes 1048608 | tf_op jit(solution)/shard_map/all_to_all | solution.py:758
  369.2 10.8 collective-permute-done.5.refs_5_.refs_3_
  384.4 23.5 %collective-permute-done.13.refs_3_ = bf16[2,224,1280]{2,1,0:T(8,128)(2,1)} collective-permute-done((bf16[2,224,1280]{2,1,0:T(8,128)(2,1)}, bf16[2,224,1280]{2,1,0:T(8,128)(2,1)}, u32[]{:S(2)}, u32[]{:S(2)}) %collective-permute-start.13) | collective-permute-done | bytes 1146912 | tf_op jit(solution)/shard_map/ppermute | solution.py:47
  411.4 10.8 shard_map.259
  428.9 18.0 %shard_map.260.grad_ref = f32[4,512,1280]{2,1,0:T(8,128)} custom-call(s32[10]{0:T(128)} %xor_multiply_fusion.offsets, s32[4]{0:T(128)} %iota_xor_fusion.places, bf16[512,1792]{1,0:T(8,128)(2,1)} %bitcast.291, bf16[4,224,1280]{2,1,0:T(8,128)(2,1)} %get-tuple-element.139.refs_0_, bf16[4,224,1280]{2,1,0:T(8,128)(2,1)} %collective-permute-done.3.refs_1_, ...), custom_call_target="tpu_custom_call" | custom-call | flops 14092861440 | bytes 1 | tf_op jit(solution)/shard_map/pallas_call | solution.py:592
  446.9 26.5 %shard_map.261 = (bf16[4,512,1216]{2,1,0:T(8,128)(2,1)}, bf16[4,512,1216]{2,1,0:T(8,128)(2,1)}, bf16[4,1,512,1280]{3,2,1,0:T(8,128)(2,1)}) custom-call(bf16[512,1792]{1,0:T(8,128)(2,1)} %multiply_convert_fusion.x_ref, bf16[8,4,2,224,1216]{4,3,2,1,0:T(8,128)(2,1)} %bitcast.289), custom_call_target="tpu_custom_call" | custom-call | flops 26776436736 | bytes 1 | tf_op jit(solution)/shard_map/pallas_call | solution.py:654
  474.2 17.7 %shard_map.262 = f32[512,1792]{1,0:T(8,128)} custom-call(s32[10]{0:T(128)} %xor_multiply_fusion.offsets, s32[4]{0:T(128)} %iota_xor_fusion.places, bf16[4,1,512,1280]{3,2,1,0:T(8,128)(2,1)} %get-tuple-element.153.y_ref.right0, bf16[4,224,1280]{2,1,0:T(8,128)(2,1)} %get-tuple-element.139.refs_0_, bf16[4,224,1280]{2,1,0:T(8,128)(2,1)} %collective-permute-done.3.refs_1_, ...), custom_call_target="tpu_custom_call" | custom-call | flops 14092861440 | bytes 1 | tf_op jit(solution)/shard_map/pallas_call | solution.py:620
  491.9 9.1 shard_map.263
  501.0 8.9 shard_map.264
  509.9 28.5 %shard_map.265 = (bf16[4,2,512,1280]{3,2,1,0:T(8,128)(2,1)}, f32[512,1792]{1,0:T(8,128)}) custom-call(f32[4,512,1280]{2,1,0:T(8,128)} %shard_map.260.grad_ref, bf16[8,4,2,224,1216]{4,3,2,1,0:T(8,128)(2,1)} %bitcast.290, bf16[4,512,1216]{2,1,0:T(8,128)(2,1)} %get-tuple-element.157.slope_ref, bf16[4,512,1216]{2,1,0:T(8,128)(2,1)} %get-tuple-element.158.silu_ref), custom_call_target="tpu_custom_call" | custom-call | flops 1 | bytes 1 | tf_op jit(solution)/shard_map/pallas_call | solution.py:687
  547.6 10.2 shard_map.266
  572.0 27.9 %collective-permute-done.22 = bf16[2,2,224,1280]{3,2,1,0:T(8,128)(2,1)} collective-permute-done((bf16[2,2,224,1280]{3,2,1,0:T(8,128)(2,1)}, bf16[2,2,224,1280]{3,2,1,0:T(8,128)(2,1)}, u32[]{:S(2)}, u32[]{:S(2)}) %collective-permute-start.22) | collective-permute-done | bytes 2293792 | tf_op jit(solution)/shard_map/ppermute | solution.py:47
  634.1 9.0 shard_map.268
  643.1 9.0 shard_map.269
  652.1 9.1 shard_map.270
  671.7 45.1 %shard_map.273 = (bf16[4096,128]{1,0:T(8,128)(2,1)}, bf16[4096,16]{1,0:T(8,128)(2,1)}) custom-call(bf16[4096,128]{1,0:T(8,128)(2,1)} %bitcast.326, bf16[4096,16]{1,0:T(8,128)(2,1)} %bitcast.320, f32[4096,128]{1,0:T(8,128)} %get-tuple-element.163.kept, bf16[4096,128]{1,0:T(8,128)(2,1)} %bitcast.53.grad, f32[4096,1]{1,0:T(8,128)} %copy.161.seg_col, ...), custom_call_target="tpu_custom_call" | custom-call | flops 51539607552 | bytes 1 | tf_op jit(solution)/shard_map/pallas_call | solution.py:922
  734.8 44.7 %shard_map.274 = (bf16[4096,128]{1,0:T(8,128)(2,1)}, bf16[4096,16]{1,0:T(8,128)(2,1)}) custom-call(bf16[4096,128]{1,0:T(8,128)(2,1)} %bitcast.324, bf16[4096,16]{1,0:T(8,128)(2,1)} %bitcast.318, f32[4096,128]{1,0:T(8,128)} %get-tuple-element.186.kept, bf16[4096,128]{1,0:T(8,128)(2,1)} %bitcast.60.grad, f32[4096,1]{1,0:T(8,128)} %copy.161.seg_col, ...), custom_call_target="tpu_custom_call" | custom-call | flops 51539607552 | bytes 1 | tf_op jit(solution)/shard_map/pallas_call | solution.py:922
  782.5 9.5 collective-permute-done.31
  810.9 31.8 %collective-permute-done.34 = bf16[2,224,1280]{2,1,0:T(8,128)(2,1)S(1)} collective-permute-done((bf16[2,224,1280]{2,1,0:T(8,128)(2,1)S(1)}, bf16[2,224,1280]{2,1,0:T(8,128)(2,1)S(1)}, u32[]{:S(2)}, u32[]{:S(2)}) %collective-permute-start.34) | collective-permute-done | bytes 1146912 | tf_op jit(solution)/shard_map/ppermute | solution.py:47
  842.7 24.1 %collective-permute-done.36 = bf16[2,224,1280]{2,1,0:T(8,128)(2,1)S(1)} collective-permute-done((bf16[2,224,1280]{2,1,0:T(8,128)(2,1)S(1)}, bf16[2,224,1280]{2,1,0:T(8,128)(2,1)S(1)}, u32[]{:S(2)}, u32[]{:S(2)}) %collective-permute-start.36) | collective-permute-done | bytes 1146912 | tf_op jit(solution)/shard_map/ppermute | solution.py:47
  896.0 12.3 %shard_map.275 = (bf16[4,512,1024]{2,1,0:T(8,128)(2,1)}, f32[4,3,448]{2,1,0:T(4,128)}) custom-call(bf16[4,512,448]{2,1,0:T(8,128)(2,1)} %get-tuple-element.160.v_ref, f32[4,512,448]{2,1,0:T(8,128)} %get-tuple-element.161.f_ref, f32[4,2,16,448]{3,2,1,0:T(8,128)} %get-tuple-element.162.side_ref, f32[512,4]{1,0:T(8,128)} %stack.88.same_ref, ...), custom_call_target="tpu_custom_call" | custom-call | flops 1 | bytes 1 | tf_op jit(solution)/shard_map/pallas_call | solution.py:1090
  943.2 13.2 %shard_map.278 = f32[512,1792]{1,0:T(8,128)} custom-call(bf16[4,512,1024]{2,1,0:T(8,128)(2,1)} %get-tuple-element.224.y_ref, bf16[8,4,1,240,1024]{4,3,2,1,0:T(8,128)(2,1)} %get-tuple-element.127.w_ref), custom_call_target="tpu_custom_call" | custom-call | flops 1 | bytes 1 | tf_op jit(solution)/shard_map/pallas_call | solution.py:494
  991.3 11.4 %collective-permute-done.43 = bf16[2,224,1024]{2,1,0:T(8,128)(2,1)S(1)} collective-permute-done((bf16[2,224,1024]{2,1,0:T(8,128)(2,1)S(1)}, bf16[2,224,1024]{2,1,0:T(8,128)(2,1)S(1)}, u32[]{:S(2)}, u32[]{:S(2)}) %collective-permute-start.43) | collective-permute-done | bytes 917536 | tf_op jit(solution)/shard_map/ppermute | solution.py:47
  1010.3 14.9 %collective-permute-done.49 = bf16[2,224,512]{2,1,0:T(8,128)(2,1)S(1)} collective-permute-done((bf16[2,224,512]{2,1,0:T(8,128)(2,1)S(1)}, bf16[2,224,512]{2,1,0:T(8,128)(2,1)S(1)}, u32[]{:S(2)}, u32[]{:S(2)}) %collective-permute-start.49) | collective-permute-done | bytes 458784 | tf_op jit(solution)/shard_map/ppermute | solution.py:47
  1032.0 16.1 %collective-permute-done.48 = bf16[2,224,1024]{2,1,0:T(8,128)(2,1)S(1)} collective-permute-done((bf16[2,224,1024]{2,1,0:T(8,128)(2,1)S(1)}, bf16[2,224,1024]{2,1,0:T(8,128)(2,1)S(1)}, u32[]{:S(2)}, u32[]{:S(2)}) %collective-permute-start.48) | collective-permute-done | bytes 917536 | tf_op jit(solution)/shard_map/ppermute | solution.py:47
  1055.7 16.4 %all-to-all-done.8 = f32[32,1,280]{2,1,0:T(1,128)S(1)} async-done(((f32[32,1,280]{2,1,0:T(1,128)}), f32[32,1,280]{2,1,0:T(1,128)S(1)}, u32[]{:S(2)}, u32[]{:S(2)}) %all-to-all-start.8) | async-done | bytes 35872 | tf_op jit(solution)/shard_map/all_to_all | solution.py:1320
  (421 shorter events, 342.0 us)
Async XLA Ops:
  7.2 439.7 %all-gather.3.cloned.1.call-start = ((), (), s32[]{:S(2)}) async-start(), calls=%async_computation.9 | async-start | bytes 37847040 | tf_op jit(solution)/shard_map/all_gather | solution.py:59
  154.2 65.6 %all-to-all-start = ((bf16[32,144,128]{2,1,0:T(8,128)(2,1)}), bf16[32,144,128]{2,1,0:T(8,128)(2,1)S(1)}, u32[]{:S(2)}, u32[]{:S(2)}) async-start(bf16[32,144,128]{2,1,0:T(8,128)(2,1)} %pad_maximum_fusion.1), calls=%async_computation | async-start | bytes 2359296 | tf_op jit(solution)/shard_map/all_to_all | solution.py:758
  158.3 58.6 %collective-permute-start.1 = (bf16[4,224,512]{2,1,0:T(8,128)(2,1)}, bf16[4,224,512]{2,1,0:T(8,128)(2,1)}, u32[]{:S(2)}, u32[]{:S(2)}) collective-permute-start(bf16[4,224,512]{2,1,0:T(8,128)(2,1)} %get-tuple-element.138.refs_2_.refs_0_), channel_id=1, source_target_pairs={{0,8},{4,12},{8,0},{12,4},{16,24},{20,28},{24,16},{28,20},{1,9},{5... | collective-permute-start | bytes 2752520 | tf_op jit(solution)/shard_map/ppermute | solution.py:47
  160.2 56.8 %collective-permute-start.2 = (bf16[4,224,512]{2,1,0:T(8,128)(2,1)}, bf16[4,224,512]{2,1,0:T(8,128)(2,1)}, u32[]{:S(2)}, u32[]{:S(2)}) collective-permute-start(bf16[4,224,512]{2,1,0:T(8,128)(2,1)} %get-tuple-element.138.refs_2_.refs_0_), channel_id=1, source_target_pairs={{0,16},{4,20},{8,24},{12,28},{16,0},{20,4},{24,8},{28,12},{1,17},{... | collective-permute-start | bytes 2752520 | tf_op jit(solution)/shard_map/ppermute | solution.py:47
  161.6 140.4 %collective-permute-start.3 = (bf16[4,224,1280]{2,1,0:T(8,128)(2,1)}, bf16[4,224,1280]{2,1,0:T(8,128)(2,1)}, u32[]{:S(2)}, u32[]{:S(2)}) collective-permute-start(bf16[4,224,1280]{2,1,0:T(8,128)(2,1)} %get-tuple-element.139.refs_0_), channel_id=1, source_target_pairs={{0,8},{4,12},{8,0},{12,4},{16,24},{20,28},{24,16},{28,20},{1,9},{5... | collective-permute-start | bytes 6881288 | tf_op jit(solution)/shard_map/ppermute | solution.py:47
  162.2 139.9 %collective-permute-start.4 = (bf16[4,224,1280]{2,1,0:T(8,128)(2,1)}, bf16[4,224,1280]{2,1,0:T(8,128)(2,1)}, u32[]{:S(2)}, u32[]{:S(2)}) collective-permute-start(bf16[4,224,1280]{2,1,0:T(8,128)(2,1)} %get-tuple-element.139.refs_0_), channel_id=1, source_target_pairs={{0,16},{4,20},{8,24},{12,28},{16,0},{20,4},{24,8},{28,12},{1,17},{... | collective-permute-start | bytes 6881288 | tf_op jit(solution)/shard_map/ppermute | solution.py:47
  162.4 202.0 %collective-permute-start.7 = (bf16[4,224,512]{2,1,0:T(8,128)(2,1)}, bf16[4,224,512]{2,1,0:T(8,128)(2,1)}, u32[]{:S(2)}, u32[]{:S(2)}) collective-permute-start(bf16[4,224,512]{2,1,0:T(8,128)(2,1)} %get-tuple-element.138.refs_2_.refs_0_), channel_id=1, source_target_pairs={{0,4},{4,0},{8,12},{12,8},{16,20},{20,16},{24,28},{28,24},{1,5},{5... | collective-permute-start | bytes 2752520 | tf_op jit(solution)/shard_map/ppermute | solution.py:47
  216.9 151.3 %collective-permute-start.8 = (bf16[4,224,512]{2,1,0:T(8,128)(2,1)}, bf16[4,224,512]{2,1,0:T(8,128)(2,1)}, u32[]{:S(2)}, u32[]{:S(2)}) collective-permute-start(bf16[4,224,512]{2,1,0:T(8,128)(2,1)} %collective-permute-done.1.refs_3_.refs_1_), channel_id=1, source_target_pairs={{0,4},{4,0},{8,12},{12,8},{16,20},{20,16},{24,28},{28,24},{1,5},{5... | collective-permute-start | bytes 2752520 | tf_op jit(solution)/shard_map/ppermute | solution.py:47
  216.9 152.0 %collective-permute-start.9 = (bf16[4,224,512]{2,1,0:T(8,128)(2,1)}, bf16[4,224,512]{2,1,0:T(8,128)(2,1)}, u32[]{:S(2)}, u32[]{:S(2)}) collective-permute-start(bf16[4,224,512]{2,1,0:T(8,128)(2,1)} %collective-permute-done.2.refs_4_.refs_2_), channel_id=1, source_target_pairs={{0,4},{4,0},{8,12},{12,8},{16,20},{20,16},{24,28},{28,24},{1,5},{5... | collective-permute-start | bytes 2752520 | tf_op jit(solution)/shard_map/ppermute | solution.py:47
  220.9 75.2 %all-to-all-start.2 = ((bf16[32,144,128]{2,1,0:T(8,128)(2,1)}), bf16[32,144,128]{2,1,0:T(8,128)(2,1)}, u32[]{:S(2)}, u32[]{:S(2)}) async-start(bf16[32,144,128]{2,1,0:T(8,128)(2,1)} %bitcast.301), calls=%async_computation.2 | async-start | bytes 2359296 | tf_op jit(solution)/shard_map/all_to_all | solution.py:758
  296.0 54.8 %all-to-all-start.1 = ((bf16[32,128,128]{2,1,0:T(8,128)(2,1)}), bf16[32,128,128]{2,1,0:T(8,128)(2,1)S(1)}, u32[]{:S(2)}, u32[]{:S(2)}) async-start(bf16[32,128,128]{2,1,0:T(8,128)(2,1)} %bitcast.331), calls=%async_computation.1 | async-start | bytes 2097152 | tf_op jit(solution)/shard_map/all_to_all | solution.py:758
  350.8 60.6 %all-to-all-start.3 = ((bf16[32,128,128]{2,1,0:T(8,128)(2,1)}), bf16[32,128,128]{2,1,0:T(8,128)(2,1)}, u32[]{:S(2)}, u32[]{:S(2)}) async-start(bf16[32,128,128]{2,1,0:T(8,128)(2,1)} %bitcast.328), calls=%async_computation.3 | async-start | bytes 2097152 | tf_op jit(solution)/shard_map/all_to_all | solution.py:758
  364.5 60.3 %collective-permute-start.15 = (bf16[4,224,1280]{2,1,0:T(8,128)(2,1)}, bf16[4,224,1280]{2,1,0:T(8,128)(2,1)}, u32[]{:S(2)}, u32[]{:S(2)}) collective-permute-start(bf16[4,224,1280]{2,1,0:T(8,128)(2,1)} %get-tuple-element.139.refs_0_), channel_id=1, source_target_pairs={{0,4},{4,0},{8,12},{12,8},{16,20},{20,16},{24,28},{28,24},{1,5},{5... | collective-permute-start | bytes 6881288 | tf_op jit(solution)/shard_map/ppermute | solution.py:47
  538.5 85.9 %collective-permute-start.24 = (bf16[4,2,512,1280]{3,2,1,0:T(8,128)(2,1)}, bf16[4,2,512,1280]{3,2,1,0:T(8,128)(2,1)}, u32[]{:S(2)}, u32[]{:S(2)}) collective-permute-start(bf16[4,2,512,1280]{3,2,1,0:T(8,128)(2,1)} %get-tuple-element.174.right0), channel_id=1, source_target_pairs={{0,4},{4,0},{8,12},{12,8},{16,20},{20,16},{24,28},{28,24},{1,5},{5... | collective-permute-start | bytes 31457288 | tf_op jit(solution)/shard_map/ppermute | solution.py:47
  538.5 61.4 %collective-permute-start.22 = (bf16[2,2,224,1280]{3,2,1,0:T(8,128)(2,1)}, bf16[2,2,224,1280]{3,2,1,0:T(8,128)(2,1)}, u32[]{:S(2)}, u32[]{:S(2)}) collective-permute-start(bf16[2,2,224,1280]{3,2,1,0:T(8,128)(2,1)} %get-tuple-element.154), channel_id=1, source_target_pairs={{0,8},{4,12},{8,0},{12,4},{16,24},{20,28},{24,16},{28,20},{1,9},{5... | collective-permute-start | bytes 6881288 | tf_op jit(solution)/shard_map/ppermute | solution.py:47
  540.0 61.8 %collective-permute-start.23 = (bf16[2,2,224,1280]{3,2,1,0:T(8,128)(2,1)}, bf16[2,2,224,1280]{3,2,1,0:T(8,128)(2,1)}, u32[]{:S(2)}, u32[]{:S(2)}) collective-permute-start(bf16[2,2,224,1280]{3,2,1,0:T(8,128)(2,1)} %get-tuple-element.155), channel_id=1, source_target_pairs={{0,16},{4,20},{8,24},{12,28},{16,0},{20,4},{24,8},{28,12},{1,17},{... | collective-permute-start | bytes 6881288 | tf_op jit(solution)/shard_map/ppermute | solution.py:47
  567.2 57.1 %collective-permute-start.21 = (bf16[4,224,512]{2,1,0:T(8,128)(2,1)}, bf16[4,224,512]{2,1,0:T(8,128)(2,1)S(1)}, u32[]{:S(2)}, u32[]{:S(2)}) collective-permute-start(bf16[4,224,512]{2,1,0:T(8,128)(2,1)} %get-tuple-element.319), channel_id=1, source_target_pairs={{0,4},{4,0},{8,12},{12,8},{16,20},{20,16},{24,28},{28,24},{1,5},{5... | collective-permute-start | bytes 2752520 | tf_op jit(solution)/shard_map/ppermute | solution.py:47
  607.0 54.2 %collective-permute-start.26 = (bf16[2,224,1280]{2,1,0:T(8,128)(2,1)}, bf16[2,224,1280]{2,1,0:T(8,128)(2,1)}, u32[]{:S(2)}, u32[]{:S(2)}) collective-permute-start(bf16[2,224,1280]{2,1,0:T(8,128)(2,1)} %fusion.25), channel_id=1, source_target_pairs={{0,16},{4,20},{8,24},{12,28},{16,0},{20,4},{24,8},{28,12},{1,17},{... | collective-permute-start | bytes 3440648 | tf_op jit(solution)/shard_map/ppermute | solution.py:47
  608.4 52.8 %collective-permute-start.27 = (bf16[2,224,1280]{2,1,0:T(8,128)(2,1)}, bf16[2,224,1280]{2,1,0:T(8,128)(2,1)}, u32[]{:S(2)}, u32[]{:S(2)}) collective-permute-start(bf16[2,224,1280]{2,1,0:T(8,128)(2,1)} %fusion.26), channel_id=1, source_target_pairs={{0,8},{4,12},{8,0},{12,4},{16,24},{20,28},{24,16},{28,20},{1,9},{5... | collective-permute-start | bytes 3440648 | tf_op jit(solution)/shard_map/ppermute | solution.py:47
  609.7 58.9 %all-to-all-start.4 = ((bf16[32,128,128]{2,1,0:T(8,128)(2,1)}), bf16[32,128,128]{2,1,0:T(8,128)(2,1)}, u32[]{:S(2)}, u32[]{:S(2)}) async-start(bf16[32,128,128]{2,1,0:T(8,128)(2,1)} %bitcast.39), calls=%async_computation.4 | async-start | bytes 2097152 | tf_op jit(solution)/shard_map/all_to_all | solution.py:758
  667.1 59.1 %collective-permute-start.30 = (bf16[2,224,1280]{2,1,0:T(8,128)(2,1)}, bf16[2,224,1280]{2,1,0:T(8,128)(2,1)}, u32[]{:S(2)}, u32[]{:S(2)}) collective-permute-start(bf16[2,224,1280]{2,1,0:T(8,128)(2,1)} %pad_maximum_fusion.4), channel_id=1, source_target_pairs={{0,1},{1,0},{2,3},{3,2},{4,5},{5,4},{6,7},{7,6},{8,9},{9,8},{10,11... | collective-permute-start | bytes 3440648 | tf_op jit(solution)/shard_map/ppermute | solution.py:47
  668.7 63.1 %collective-permute-start.28 = (bf16[2,2,224,1280]{3,2,1,0:T(8,128)(2,1)}, bf16[2,2,224,1280]{3,2,1,0:T(8,128)(2,1)}, u32[]{:S(2)}, u32[]{:S(2)}) collective-permute-start(bf16[2,2,224,1280]{3,2,1,0:T(8,128)(2,1)} %get-tuple-element.188), channel_id=1, source_target_pairs={{0,8},{4,12},{8,0},{12,4},{16,24},{20,28},{24,16},{28,20},{1,9},{5... | collective-permute-start | bytes 6881288 | tf_op jit(solution)/shard_map/ppermute | solution.py:47
  670.2 61.6 %collective-permute-start.29 = (bf16[2,2,224,1280]{3,2,1,0:T(8,128)(2,1)}, bf16[2,2,224,1280]{3,2,1,0:T(8,128)(2,1)}, u32[]{:S(2)}, u32[]{:S(2)}) collective-permute-start(bf16[2,2,224,1280]{3,2,1,0:T(8,128)(2,1)} %get-tuple-element.189), channel_id=1, source_target_pairs={{0,16},{4,20},{8,24},{12,28},{16,0},{20,4},{24,8},{28,12},{1,17},{... | collective-permute-start | bytes 6881288 | tf_op jit(solution)/shard_map/ppermute | solution.py:47
  722.8 73.3 %all-to-all-start.6 = ((bf16[32,160,128]{2,1,0:T(8,128)(2,1)}), bf16[32,160,128]{2,1,0:T(8,128)(2,1)}, u32[]{:S(2)}, u32[]{:S(2)}) async-start(bf16[32,160,128]{2,1,0:T(8,128)(2,1)} %fusion.23), calls=%async_computation.6 | async-start | bytes 2621440 | tf_op jit(solution)/shard_map/all_to_all | solution.py:758
  729.2 53.3 %collective-permute-start.33 = (bf16[224,1280]{1,0:T(8,128)(2,1)}, bf16[224,1280]{1,0:T(8,128)(2,1)S(1)}, u32[]{:S(2)}, u32[]{:S(2)}) collective-permute-start(bf16[224,1280]{1,0:T(8,128)(2,1)} %get-tuple-element.308), channel_id=1, source_target_pairs={{0,2},{1,3},{2,0},{3,1},{4,6},{5,7},{6,4},{7,5},{8,10},{9,11},{10,... | collective-permute-start | bytes 1720328 | tf_op jit(solution)/shard_map/ppermute | solution.py:47
  731.8 60.2 %collective-permute-start.31 = (bf16[2,2,224,1280]{3,2,1,0:T(8,128)(2,1)}, bf16[2,2,224,1280]{3,2,1,0:T(8,128)(2,1)S(1)}, u32[]{:S(2)}, u32[]{:S(2)}) collective-permute-start(bf16[2,2,224,1280]{3,2,1,0:T(8,128)(2,1)} %get-tuple-element.193), channel_id=1, source_target_pairs={{0,8},{4,12},{8,0},{12,4},{16,24},{20,28},{24,16},{28,20},{1,9},{5... | collective-permute-start | bytes 6881288 | tf_op jit(solution)/shard_map/ppermute | solution.py:47
  733.3 59.4 %collective-permute-start.32 = (bf16[2,2,224,1280]{3,2,1,0:T(8,128)(2,1)}, bf16[2,2,224,1280]{3,2,1,0:T(8,128)(2,1)}, u32[]{:S(2)}, u32[]{:S(2)}) collective-permute-start(bf16[2,2,224,1280]{3,2,1,0:T(8,128)(2,1)} %get-tuple-element.194), channel_id=1, source_target_pairs={{0,16},{4,20},{8,24},{12,28},{16,0},{20,4},{24,8},{28,12},{1,17},{... | collective-permute-start | bytes 6881288 | tf_op jit(solution)/shard_map/ppermute | solution.py:47
  796.1 71.7 %all-to-all-start.7 = ((bf16[32,160,128]{2,1,0:T(8,128)(2,1)}), bf16[32,160,128]{2,1,0:T(8,128)(2,1)S(1)}, u32[]{:S(2)}, u32[]{:S(2)}) async-start(bf16[32,160,128]{2,1,0:T(8,128)(2,1)} %fusion.24), calls=%async_computation.7 | async-start | bytes 2621440 | tf_op jit(solution)/shard_map/all_to_all | solution.py:758
  808.0 58.8 %collective-permute-start.36 = (bf16[2,224,1280]{2,1,0:T(8,128)(2,1)S(1)}, bf16[2,224,1280]{2,1,0:T(8,128)(2,1)S(1)}, u32[]{:S(2)}, u32[]{:S(2)}) collective-permute-start(bf16[2,224,1280]{2,1,0:T(8,128)(2,1)S(1)} %fusion.29), channel_id=1, source_target_pairs={{0,16},{4,20},{8,24},{12,28},{16,0},{20,4},{24,8},{28,12},{1,17},{... | collective-permute-start | bytes 3440648 | tf_op jit(solution)/shard_map/ppermute | solution.py:47
  810.2 57.6 %collective-permute-start.37 = (bf16[2,224,1280]{2,1,0:T(8,128)(2,1)S(1)}, bf16[2,224,1280]{2,1,0:T(8,128)(2,1)}, u32[]{:S(2)}, u32[]{:S(2)}) collective-permute-start(bf16[2,224,1280]{2,1,0:T(8,128)(2,1)S(1)} %fusion.30), channel_id=1, source_target_pairs={{0,8},{4,12},{8,0},{12,4},{16,24},{20,28},{24,16},{28,20},{1,9},{5... | collective-permute-start | bytes 3440648 | tf_op jit(solution)/shard_map/ppermute | solution.py:47
  921.8 65.8 %collective-permute-start.44 = (bf16[2,224,512]{2,1,0:T(8,128)(2,1)}, bf16[2,224,512]{2,1,0:T(8,128)(2,1)S(1)}, u32[]{:S(2)}, u32[]{:S(2)}) collective-permute-start(bf16[2,224,512]{2,1,0:T(8,128)(2,1)} %fusion.48), channel_id=1, source_target_pairs={{0,16},{4,20},{8,24},{12,28},{16,0},{20,4},{24,8},{28,12},{1,17},{... | collective-permute-start | bytes 1376264 | tf_op jit(solution)/shard_map/ppermute | solution.py:47
  962.8 64.8 %collective-permute-start.53 = (bf16[2,224,1280]{2,1,0:T(8,128)(2,1)S(1)}, bf16[2,224,1280]{2,1,0:T(8,128)(2,1)S(1)}, u32[]{:S(2)}, u32[]{:S(2)}) collective-permute-start(bf16[2,224,1280]{2,1,0:T(8,128)(2,1)S(1)} %fusion.31), channel_id=1, source_target_pairs={{0,2},{1,3},{2,0},{3,1},{4,6},{5,7},{6,4},{7,5},{8,10},{9,11},{10,... | collective-permute-start | bytes 3440648 | tf_op jit(solution)/shard_map/ppermute | solution.py:47
  (101 other events, 1847.3 us)
Sparse Core Ops, SparseCore 0:
  114.0 309.7 all-gather.2

commit v4 on v3

--- a/solution.py
+++ b/solution.py
@@ -1225,20 +1225,21 @@
         if j > 0:
             blocks = tie(blocks, low[-1])
         low.append(lay.exchange(blocks))
+    low[-1] = tie(low[-1], *[piece for piece, _ in down_w.pieces[3:5]])
     att_low, projected = out_of_pieces(lay, [lay.by_place(blocks) for blocks in low], out_w)
 
     residual = x + projected
     scale_two = inverse_rms(residual)
     normed_two = (residual * scale_two * gain_two).astype(bf16)
     out_sum = Scatter(None, att_low, True)
-    grad_hidden = spread(tie(cot_low, att_low), down_w)
-    normed_two = tie(normed_two, out_sum.other_side(), grad_hidden)
+    normed_two = tie(
+        normed_two, out_sum.other_side(), *[piece for piece, _ in down_w.pieces]
+    )
     slope, silu, hidden = hidden_of(normed_two, gate_up_w)
     down_sum = Scatter(cot_left, hidden)
-    ffn_out = collect(hidden, down_w)
-    layer_output = (residual + ffn_out).astype(bf16).reshape(tokens.shape)
-
-    down_sum.right = tie(down_sum.right, ffn_out)
+
+    grad_hidden = spread(tie(cot_low, hidden), down_w)
+    down_sum.right = tie(down_sum.right, grad_hidden)
     down_sends = down_sum.first()
     grads_gu, back_two = hidden_back(tie(grad_hidden, *down_sends), gate_up_w, slope, silu)
     two_left = Left(normed_two)
@@ -1250,15 +1251,16 @@
 
     sent = [rows.reshape(-1, span, LANES) for rows in into_pieces(lay, grad_res_low, out_w)]
     arrived = [lay.exchange(blocks) for blocks in sent]
-    down_sends = down_sum.second(*sent)
     out_sum.left = Left(tie(grad_res_low, *sent))
-    for terms in (gate_sum, up_sum, out_sum):
+    gate_sum.right = tie(gate_sum.right, *sent)
+    made = gate_sum.products()
+    down_sends = down_sum.second(*made)
+    for terms in (up_sum, out_sum):
         terms.right = tie(terms.right, *down_sends)
     up_sum.right = tie(up_sum.right, *arrived[1:])
-    made = gate_sum.products() + up_sum.products() + out_sum.products()
-    down_sum = Along(down_sum.last(*made))
-    gate_sum.go(*down_sum.sent)
-    arrived[0] = tie(arrived[0], *made, *down_sum.sent)
+    made += up_sum.products() + out_sum.products()
+    gate_sum.go(*down_sends)
+    arrived[0] = tie(arrived[0], *made)
     backs, grad_keys = [], []
     for j in heads:
         grad_rows = lay.all_parts(arrived[j].reshape(-1, LANES))
@@ -1266,7 +1268,7 @@
             if j > 0:
                 grad_rows = tie(grad_rows, sent)
             up_sum.go(grad_rows, *gate_sum.pending())
-            down_sum.go(grad_rows)
+            down_sum = Along(down_sum.last(grad_rows))
             grad_rows = tie(grad_rows, *gate_sum.pending(), *down_sum.sent)
         grad_main, grad_key = attend_back(mains[j], all_keys[j], kept[j], grad_rows, my_seg)
         if j == lay.heads - 1:
@@ -1282,9 +1284,8 @@
         backs.append(lay.by_place(blocks))
     gate_sum.second(sent)
     up_sum.second(sent)
-    backs[-1] = tie(backs[-1], *gate_sum.pending(), *up_sum.pending())
-    gate_up_sum = Along(jnp.stack([gate_sum.last(backs[-1]), up_sum.last(backs[-1])], axis=1))
-    backs[-1] = tie(backs[-1], *gate_up_sum.sent)
+    down_sum.go(sent)
+    backs[-1] = tie(backs[-1], *gate_sum.pending(), *up_sum.pending(), *down_sum.coming)
     out_sum.go(backs[-1])
 
     grad_keys = jnp.stack([lay.by_place(rows) for rows in grad_keys])
@@ -1293,6 +1294,7 @@
         lay, backs, grad_keys, v_low, filter_pre, side, same, taps
     )
     tap_grads = jnp.swapaxes(tap_grads, 0, 1).reshape(3, D)
+    gate_up_sum = Along(jnp.stack([gate_sum.last(grad_first), up_sum.last(grad_first)], axis=1))
     grad_first = tie(grad_first, *out_sum.pending())
     first_sum = Scatter(Left(tie(normed, grad_first)), grad_first[:, None])
     out_sends = out_sum.second(*first_sum.given())
@@ -1307,6 +1309,8 @@
     first_sum = Along(first_sum.last(*out_sum.sent))
     gate_up_grad = gate_up_sum.finish(*first_sum.sent)
     down_grad = down_sum.finish(*first_sum.sent)
+    ffn_out = collect(tie(hidden, *first_sum.sent), down_w)
+    layer_output = (residual + ffn_out).astype(bf16).reshape(tokens.shape)
     out_sum.go(*first_sum.sent)
     first_sum.go(*out_sum.sent)
     out_grad = out_sum.finish(*first_sum.sent)

time: 1100 us -> 1070 us (0.973)
  waiting for transfers between devices: 328 us -> 300 us
    ppermute x54, waiting for transfers between devices: 240 us -> 164 us  [swap(): return lax.ppermute(block, axis, [(i, i ^ bit) for i in devices])]
    all_to_all x8, waiting for transfers between devices: 71.7 us -> 120 us  [exchange(): lax.all_to_all(blocks, BOTH, 0, 0, tiled=True, axis_index_groups=self.gro...]
  transfers between devices with their start and end apart: 64 -> 64, of which waited for: 25 -> 21; matrix products, arithmetic and copies ran while one was open for 15% -> 16% of each run, Pallas kernels for 27% -> 28%
where the time goes in v4:
time: 1070 us; the launch traced here: 1060 us
  Pallas kernels  461 us (43%)
  waiting for transfers between devices  300 us (28%)
  other arithmetic  102 us (10%)
  local copies, waits for them, and re-layouts  93.9 us (9%)
  starting transfers between devices  91.5 us (9%)
  between operations  15.7 us (1%)
    ppermute x54, waiting for transfers between devices, swap(): return lax.ppermute(block, axis, [(i, i ^ bit) for i in devices])  164 us
    all_to_all x8, waiting for transfers between devices, exchange(): lax.all_to_all(blocks, BOTH, 0, 0, tiled=True, axis_index_groups=self.gro...  120 us
    pallas_call x1, Pallas kernels, gather_first(): pl.pallas_call(gather_kernel, in_specs=[anywhere] * (2 + count), out_spec...  94.3 us
    pallas_call x2, Pallas kernels, attend_back(): pl.pallas_call(functools.partial(attend_back_kernel, chunk), grid=(steps,...  89.5 us
    pallas_call x10, Pallas kernels, weight_grads(): pl.pallas_call(functools.partial(grad_kernel, first), grid_spec=pltpu.Pre...  79.2 us
    ppermute x54, starting transfers between devices, swap(): return lax.ppermute(block, axis, [(i, i ^ bit) for i in devices])  47.4 us
    pallas_call x2, Pallas kernels, attend(): pl.pallas_call(functools.partial(attend_kernel, chunk), grid=(steps,), in...  43.4 us
    all_to_all x8, starting transfers between devices, exchange(): lax.all_to_all(blocks, BOTH, 0, 0, tiled=True, axis_index_groups=self.gro...  40 us
  transfers between devices with their start and end apart: 64, of which 21 were waited for; matrix products, arithmetic and copies ran while one was open for 16% of the time, Pallas kernels for 28%

profile of v4, /device:TPU:0, one launch (start us, length us, event | category | flops | bytes accessed | tf_op | source)
XLA Modules:
  0.0 1063.7 jit_solution(2273459187366733751)
XLA Ops:
  19.6 94.3 %shard_map.255 = (bf16[8,4,1,240,1024]{4,3,2,1,0:T(8,128)(2,1)}, bf16[2,16,1792]{2,1,0:T(8,128)(2,1)}, bf16[4,224,1280]{2,1,0:T(8,128)(2,1)}, bf16[4,224,512]{2,1,0:T(8,128)(2,1)}) custom-call(bf16[240,1024]{1,0:T(8,128)(2,1)} %pad_maximum_fusion.7.shard, bf16[16,1792]{1,0:T(8,128)(2,1)} %reshape.340.edge, bf16[224,1280]{1,0:T(8,128)(2,1)} %pad.24.refs_0_, ...), custom_call_target="tpu_custom_call" | custom-call | flops 99999997952 | bytes 1 | tf_op jit(solution)/shard_map/pallas_call | solution.py:191
  133.7 15.9 %shard_map.256 = (bf16[4,512,448]{2,1,0:T(8,128)(2,1)}, f32[4,512,448]{2,1,0:T(8,128)}, f32[4,2,16,448]{3,2,1,0:T(8,128)}, bf16[4,2,4,128,128]{4,3,2,1,0:T(8,128...) custom-call(bf16[512,1792]{1,0:T(8,128)(2,1)} %fusion.3.x_ref, ...), custom_call_target="tpu_custom_call" | custom-call | flops 11274289152 | bytes 1 | tf_op jit(solution)/shard_map/pallas_call | solution.py:1015
  171.9 38.9 %all-to-all-done = bf16[32,144,128]{2,1,0:T(8,128)(2,1)S(1)} async-done(((bf16[32,144,128]{2,1,0:T(8,128)(2,1)}), bf16[32,144,128]{2,1,0:T(8,128)(2,1)S(1)}, u32[]{:S(2)}, u32[]{:S(2)}) %all-to-all-start) | async-done | bytes 1179680 | tf_op jit(solution)/shard_map/all_to_all | solution.py:758
  219.7 21.7 %shard_map.257 = (f32[4096,128]{1,0:T(8,128)}, bf16[4096,128]{1,0:T(8,128)(2,1)}) custom-call(bf16[4096,128]{1,0:T(8,128)(2,1)} %bitcast.321, bf16[4096,16]{1,0:T(8,128)(2,1)} %bitcast.315, f32[4096,1]{1,0:T(8,128)} %copy.161.seg_col, f32[8,1,512]{2,1,0:T(1,128)} %bitcast.343), custom_call_target="tpu_custom_call" | custom-call | flops 25769803776 | bytes 1 | tf_op jit(solution)/shard_map/pallas_call | solution.py:823
  241.4 60.8 %all-to-all-done.2 = bf16[32,144,128]{2,1,0:T(8,128)(2,1)} async-done(((bf16[32,144,128]{2,1,0:T(8,128)(2,1)}), bf16[32,144,128]{2,1,0:T(8,128)(2,1)}, u32[]{:S(2)}, u32[]{:S(2)}) %all-to-all-start.2) | async-done | bytes 1179680 | tf_op jit(solution)/shard_map/all_to_all | solution.py:758
  312.1 21.7 %shard_map.258 = (f32[4096,128]{1,0:T(8,128)}, bf16[4096,128]{1,0:T(8,128)(2,1)}) custom-call(bf16[4096,128]{1,0:T(8,128)(2,1)} %bitcast.319, bf16[4096,16]{1,0:T(8,128)(2,1)} %bitcast.313, f32[4096,1]{1,0:T(8,128)} %copy.161.seg_col, f32[8,1,512]{2,1,0:T(1,128)} %bitcast.344), custom_call_target="tpu_custom_call" | custom-call | flops 25769803776 | bytes 1 | tf_op jit(solution)/shard_map/pallas_call | solution.py:823
  333.8 20.1 %all-to-all-done.1 = bf16[32,128,128]{2,1,0:T(8,128)(2,1)S(1)} async-done(((bf16[32,128,128]{2,1,0:T(8,128)(2,1)}), bf16[32,128,128]{2,1,0:T(8,128)(2,1)S(1)}, u32[]{:S(2)}, u32[]{:S(2)}) %all-to-all-start.1) | async-done | bytes 1048608 | tf_op jit(solution)/shard_map/all_to_all | solution.py:758
  368.1 39.5 %collective-permute-done.7.refs_5_.refs_3_ = bf16[2,224,512]{2,1,0:T(8,128)(2,1)S(1)} collective-permute-done((bf16[2,224,512]{2,1,0:T(8,128)(2,1)S(1)}, bf16[2,224,512]{2,1,0:T(8,128)(2,1)S(1)}, u32[]{:S(2)}, u32[]{:S(2)}) %collective-permute-start.7) | collective-permute-done | bytes 458784 | tf_op jit(solution)/shard_map/ppermute | solution.py:47
  413.0 11.6 %shard_map.259 = (bf16[4,1,512,512]{3,2,1,0:T(8,128)(2,1)}, f32[512,1792]{1,0:T(8,128)}) custom-call(s32[10]{0:T(128)} %xor_multiply_fusion.offsets, s32[4]{0:T(128)} %iota_xor_fusion.places, bf16[4,2,4,128,128]{4,3,2,1,0:T(8,128)(2,1)} %bitcast.323, bf16[4,2,4,128,128]{4,3,2,1,0:T(8,128)(2,1)} %bitcast.32.refs_1_, ...), custom_call_target="tpu_custom_call" | custom-call | flops 5637144576 | bytes 1 | tf_op jit(solution)/shard_map/pallas_call | solution.py:561
  434.2 26.5 %shard_map.260 = (bf16[4,512,1216]{2,1,0:T(8,128)(2,1)}, bf16[4,512,1216]{2,1,0:T(8,128)(2,1)}, bf16[4,1,512,1280]{3,2,1,0:T(8,128)(2,1)}) custom-call(bf16[512,1792]{1,0:T(8,128)(2,1)} %multiply_convert_fusion.x_ref, bf16[8,4,2,224,1216]{4,3,2,1,0:T(8,128)(2,1)} %bitcast.286), custom_call_target="tpu_custom_call" | custom-call | flops 26776436736 | bytes 1 | tf_op jit(solution)/shard_map/pallas_call | solution.py:654
  461.0 18.0 %shard_map.261.grad_ref = f32[4,512,1280]{2,1,0:T(8,128)} custom-call(s32[10]{0:T(128)} %xor_multiply_fusion.offsets, s32[4]{0:T(128)} %iota_xor_fusion.places, bf16[512,1792]{1,0:T(8,128)(2,1)} %bitcast.288, bf16[4,224,1280]{2,1,0:T(8,128)(2,1)} %get-tuple-element.141.refs_0_, bf16[4,224,1280]{2,1,0:T(8,128)(2,1)} %collective-permute-done.3.refs_1_, ...), custom_call_target="tpu_custom_call" | custom-call | flops 14092861440 | bytes 1 | tf_op jit(solution)/shard_map/pallas_call | solution.py:592
  479.0 8.9 shard_map.262
  488.0 9.1 shard_map.263
  497.0 28.5 %shard_map.264 = (bf16[4,2,512,1280]{3,2,1,0:T(8,128)(2,1)}, f32[512,1792]{1,0:T(8,128)}) custom-call(f32[4,512,1280]{2,1,0:T(8,128)} %shard_map.261.grad_ref, bf16[8,4,2,224,1216]{4,3,2,1,0:T(8,128)(2,1)} %bitcast.287, bf16[4,512,1216]{2,1,0:T(8,128)(2,1)} %get-tuple-element.164.slope_ref, bf16[4,512,1216]{2,1,0:T(8,128)(2,1)} %get-tuple-element.165.silu_ref), custom_call_target="tpu_custom_call" | custom-call | flops 1 | bytes 1 | tf_op jit(solution)/shard_map/pallas_call | solution.py:687
  539.8 10.2 shard_map.265
  560.6 8.9 shard_map.266
  569.5 8.9 shard_map.267
  578.4 14.4 %collective-permute-done.23 = bf16[2,2,224,1280]{3,2,1,0:T(8,128)(2,1)} collective-permute-done((bf16[2,2,224,1280]{3,2,1,0:T(8,128)(2,1)}, bf16[2,2,224,1280]{3,2,1,0:T(8,128)(2,1)}, u32[]{:S(2)}, u32[]{:S(2)}) %collective-permute-start.23) | collective-permute-done | bytes 2293792 | tf_op jit(solution)/shard_map/ppermute | solution.py:47
  618.1 8.9 shard_map.268
  627.0 8.9 shard_map.269
  636.9 44.8 %shard_map.272 = (bf16[4096,128]{1,0:T(8,128)(2,1)}, bf16[4096,16]{1,0:T(8,128)(2,1)}) custom-call(bf16[4096,128]{1,0:T(8,128)(2,1)} %bitcast.322, bf16[4096,16]{1,0:T(8,128)(2,1)} %bitcast.316, f32[4096,128]{1,0:T(8,128)} %get-tuple-element.158.kept, bf16[4096,128]{1,0:T(8,128)(2,1)} %bitcast.327, f32[4096,1]{1,0:T(8,128)} %copy.161.seg_col, ...), custom_call_target="tpu_custom_call" | custom-call | flops 51539607552 | bytes 1 | tf_op jit(solution)/shard_map/pallas_call | solution.py:922
  704.9 44.7 %shard_map.273 = (bf16[4096,128]{1,0:T(8,128)(2,1)}, bf16[4096,16]{1,0:T(8,128)(2,1)}) custom-call(bf16[4096,128]{1,0:T(8,128)(2,1)} %bitcast.320, bf16[4096,16]{1,0:T(8,128)(2,1)} %bitcast.314, f32[4096,128]{1,0:T(8,128)} %get-tuple-element.188.kept, bf16[4096,128]{1,0:T(8,128)(2,1)} %bitcast.57.grad, f32[4096,1]{1,0:T(8,128)} %copy.161.seg_col, ...), custom_call_target="tpu_custom_call" | custom-call | flops 51539607552 | bytes 1 | tf_op jit(solution)/shard_map/pallas_call | solution.py:922
  752.3 8.6 collective-permute-done.30
  789.4 36.7 %collective-permute-done.37 = bf16[224,1280]{1,0:T(8,128)(2,1)} collective-permute-done((bf16[224,1280]{1,0:T(8,128)(2,1)S(1)}, bf16[224,1280]{1,0:T(8,128)(2,1)}, u32[]{:S(2)}, u32[]{:S(2)}) %collective-permute-start.37) | collective-permute-done | bytes 573472 | tf_op jit(solution)/shard_map/ppermute | solution.py:47
  826.1 9.8 collective-permute-done.35
  846.9 12.4 %shard_map.274 = (bf16[4,512,1024]{2,1,0:T(8,128)(2,1)}, f32[4,3,448]{2,1,0:T(4,128)}) custom-call(bf16[4,512,448]{2,1,0:T(8,128)(2,1)} %get-tuple-element.155.v_ref, f32[4,512,448]{2,1,0:T(8,128)} %get-tuple-element.156.f_ref, f32[4,2,16,448]{3,2,1,0:T(8,128)} %get-tuple-element.157.side_ref, f32[512,4]{1,0:T(8,128)} %stack.88.same_ref, ...), custom_call_target="tpu_custom_call" | custom-call | flops 1 | bytes 1 | tf_op jit(solution)/shard_map/pallas_call | solution.py:1090
  907.4 13.4 %shard_map.277 = f32[512,1792]{1,0:T(8,128)} custom-call(bf16[4,512,1024]{2,1,0:T(8,128)(2,1)} %get-tuple-element.224.y_ref, bf16[8,4,1,240,1024]{4,3,2,1,0:T(8,128)(2,1)} %get-tuple-element.129.w_ref), custom_call_target="tpu_custom_call" | custom-call | flops 1 | bytes 1 | tf_op jit(solution)/shard_map/pallas_call | solution.py:494
  960.5 15.2 %collective-permute-done.43 = bf16[2,224,1024]{2,1,0:T(8,128)(2,1)S(1)} collective-permute-done((bf16[2,224,1024]{2,1,0:T(8,128)(2,1)S(1)}, bf16[2,224,1024]{2,1,0:T(8,128)(2,1)S(1)}, u32[]{:S(2)}, u32[]{:S(2)}) %collective-permute-start.43) | collective-permute-done | bytes 917536 | tf_op jit(solution)/shard_map/ppermute | solution.py:47
  981.1 8.7 collective-permute-done.49
  996.9 18.0 %shard_map.278 = f32[512,1792]{1,0:T(8,128)} custom-call(s32[10]{0:T(128)} %xor_multiply_fusion.offsets, s32[4]{0:T(128)} %iota_xor_fusion.places, bf16[4,1,512,1280]{3,2,1,0:T(8,128)(2,1)} %get-tuple-element.232.right0.y_ref, bf16[4,224,1280]{2,1,0:T(8,128)(2,1)} %get-tuple-element.141.refs_0_, bf16[4,224,1280]{2,1,0:T(8,128)(2,1)} %collective-permute-done.3.refs_1_, ...), custom_call_target="tpu_custom_call" | custom-call | flops 14092861440 | bytes 1 | tf_op jit(solution)/shard_map/pallas_call | solution.py:620
  1015.0 7.8 fusion.8
  1034.1 15.9 %all-to-all-done.8 = f32[32,1,280]{2,1,0:T(1,128)S(1)} async-done(((f32[32,1,280]{2,1,0:T(1,128)}), f32[32,1,280]{2,1,0:T(1,128)S(1)}, u32[]{:S(2)}, u32[]{:S(2)}) %all-to-all-start.8) | async-done | bytes 35872 | tf_op jit(solution)/shard_map/all_to_all | solution.py:1324
  (409 shorter events, 336.3 us)
Async XLA Ops:
  7.2 427.1 %all-gather.3.cloned.1.call-start = ((), (), s32[]{:S(2)}) async-start(), calls=%async_computation.9 | async-start | bytes 37847040 | tf_op jit(solution)/shard_map/all_gather | solution.py:59
  154.2 56.6 %all-to-all-start = ((bf16[32,144,128]{2,1,0:T(8,128)(2,1)}), bf16[32,144,128]{2,1,0:T(8,128)(2,1)S(1)}, u32[]{:S(2)}, u32[]{:S(2)}) async-start(bf16[32,144,128]{2,1,0:T(8,128)(2,1)} %pad_maximum_fusion.1), calls=%async_computation | async-start | bytes 2359296 | tf_op jit(solution)/shard_map/all_to_all | solution.py:758
  158.3 149.9 %collective-permute-start.1 = (bf16[4,224,512]{2,1,0:T(8,128)(2,1)}, bf16[4,224,512]{2,1,0:T(8,128)(2,1)}, u32[]{:S(2)}, u32[]{:S(2)}) collective-permute-start(bf16[4,224,512]{2,1,0:T(8,128)(2,1)} %get-tuple-element.140.refs_2_.refs_0_), channel_id=1, source_target_pairs={{0,8},{4,12},{8,0},{12,4},{16,24},{20,28},{24,16},{28,20},{1,9},{5... | collective-permute-start | bytes 2752520 | tf_op jit(solution)/shard_map/ppermute | solution.py:47
  160.2 148.1 %collective-permute-start.2 = (bf16[4,224,512]{2,1,0:T(8,128)(2,1)}, bf16[4,224,512]{2,1,0:T(8,128)(2,1)}, u32[]{:S(2)}, u32[]{:S(2)}) collective-permute-start(bf16[4,224,512]{2,1,0:T(8,128)(2,1)} %get-tuple-element.140.refs_2_.refs_0_), channel_id=1, source_target_pairs={{0,16},{4,20},{8,24},{12,28},{16,0},{20,4},{24,8},{28,12},{1,17},{... | collective-permute-start | bytes 2752520 | tf_op jit(solution)/shard_map/ppermute | solution.py:47
  161.6 146.6 %collective-permute-start.3 = (bf16[4,224,1280]{2,1,0:T(8,128)(2,1)}, bf16[4,224,1280]{2,1,0:T(8,128)(2,1)}, u32[]{:S(2)}, u32[]{:S(2)}) collective-permute-start(bf16[4,224,1280]{2,1,0:T(8,128)(2,1)} %get-tuple-element.141.refs_0_), channel_id=1, source_target_pairs={{0,8},{4,12},{8,0},{12,4},{16,24},{20,28},{24,16},{28,20},{1,9},{5... | collective-permute-start | bytes 6881288 | tf_op jit(solution)/shard_map/ppermute | solution.py:47
  162.2 146.1 %collective-permute-start.4 = (bf16[4,224,1280]{2,1,0:T(8,128)(2,1)}, bf16[4,224,1280]{2,1,0:T(8,128)(2,1)}, u32[]{:S(2)}, u32[]{:S(2)}) collective-permute-start(bf16[4,224,1280]{2,1,0:T(8,128)(2,1)} %get-tuple-element.141.refs_0_), channel_id=1, source_target_pairs={{0,16},{4,20},{8,24},{12,28},{16,0},{20,4},{24,8},{28,12},{1,17},{... | collective-permute-start | bytes 6881288 | tf_op jit(solution)/shard_map/ppermute | solution.py:47
  211.9 90.3 %all-to-all-start.2 = ((bf16[32,144,128]{2,1,0:T(8,128)(2,1)}), bf16[32,144,128]{2,1,0:T(8,128)(2,1)}, u32[]{:S(2)}, u32[]{:S(2)}) async-start(bf16[32,144,128]{2,1,0:T(8,128)(2,1)} %bitcast.297), calls=%async_computation.2 | async-start | bytes 2359296 | tf_op jit(solution)/shard_map/all_to_all | solution.py:758
  302.2 51.7 %all-to-all-start.1 = ((bf16[32,128,128]{2,1,0:T(8,128)(2,1)}), bf16[32,128,128]{2,1,0:T(8,128)(2,1)S(1)}, u32[]{:S(2)}, u32[]{:S(2)}) async-start(bf16[32,128,128]{2,1,0:T(8,128)(2,1)} %bitcast.328), calls=%async_computation.1 | async-start | bytes 2097152 | tf_op jit(solution)/shard_map/all_to_all | solution.py:758
  353.9 56.5 %all-to-all-start.3 = ((bf16[32,128,128]{2,1,0:T(8,128)(2,1)}), bf16[32,128,128]{2,1,0:T(8,128)(2,1)}, u32[]{:S(2)}, u32[]{:S(2)}) async-start(bf16[32,128,128]{2,1,0:T(8,128)(2,1)} %bitcast.325), calls=%async_computation.3 | async-start | bytes 2097152 | tf_op jit(solution)/shard_map/all_to_all | solution.py:758
  361.7 46.4 %collective-permute-start.5 = (bf16[2,224,1280]{2,1,0:T(8,128)(2,1)S(1)}, bf16[2,224,1280]{2,1,0:T(8,128)(2,1)S(1)}, u32[]{:S(2)}, u32[]{:S(2)}) collective-permute-start(bf16[2,224,1280]{2,1,0:T(8,128)(2,1)S(1)} %slice.361), channel_id=1, source_target_pairs={{0,16},{4,20},{8,24},{12,28},{16,0},{20,4},{24,8},{28,12},{1,17},{... | collective-permute-start | bytes 3440648 | tf_op jit(solution)/shard_map/ppermute | solution.py:47
  368.1 57.3 %collective-permute-start.15 = (bf16[4,224,1280]{2,1,0:T(8,128)(2,1)}, bf16[4,224,1280]{2,1,0:T(8,128)(2,1)}, u32[]{:S(2)}, u32[]{:S(2)}) collective-permute-start(bf16[4,224,1280]{2,1,0:T(8,128)(2,1)} %get-tuple-element.141.refs_0_), channel_id=1, source_target_pairs={{0,4},{4,0},{8,12},{12,8},{16,20},{20,16},{24,28},{28,24},{1,5},{5... | collective-permute-start | bytes 6881288 | tf_op jit(solution)/shard_map/ppermute | solution.py:47
  531.4 61.4 %collective-permute-start.23 = (bf16[2,2,224,1280]{3,2,1,0:T(8,128)(2,1)}, bf16[2,2,224,1280]{3,2,1,0:T(8,128)(2,1)}, u32[]{:S(2)}, u32[]{:S(2)}) collective-permute-start(bf16[2,2,224,1280]{3,2,1,0:T(8,128)(2,1)} %get-tuple-element.161), channel_id=1, source_target_pairs={{0,8},{4,12},{8,0},{12,4},{16,24},{20,28},{24,16},{28,20},{1,9},{5... | collective-permute-start | bytes 6881288 | tf_op jit(solution)/shard_map/ppermute | solution.py:47
  531.9 61.4 %collective-permute-start.24 = (bf16[2,2,224,1280]{3,2,1,0:T(8,128)(2,1)}, bf16[2,2,224,1280]{3,2,1,0:T(8,128)(2,1)}, u32[]{:S(2)}, u32[]{:S(2)}) collective-permute-start(bf16[2,2,224,1280]{3,2,1,0:T(8,128)(2,1)} %get-tuple-element.162), channel_id=1, source_target_pairs={{0,16},{4,20},{8,24},{12,28},{16,0},{20,4},{24,8},{28,12},{1,17},{... | collective-permute-start | bytes 6881288 | tf_op jit(solution)/shard_map/ppermute | solution.py:47
  550.0 46.3 %all-to-all-start.5 = ((bf16[32,128,128]{2,1,0:T(8,128)(2,1)}), bf16[32,128,128]{2,1,0:T(8,128)(2,1)}, u32[]{:S(2)}, u32[]{:S(2)}) async-start(bf16[32,128,128]{2,1,0:T(8,128)(2,1)} %bitcast.326), calls=%async_computation.5 | async-start | bytes 2097152 | tf_op jit(solution)/shard_map/all_to_all | solution.py:758
  559.3 48.6 %collective-permute-start.25 = (bf16[4,224,512]{2,1,0:T(8,128)(2,1)}, bf16[4,224,512]{2,1,0:T(8,128)(2,1)}, u32[]{:S(2)}, u32[]{:S(2)}) collective-permute-start(bf16[4,224,512]{2,1,0:T(8,128)(2,1)} %get-tuple-element.321), channel_id=1, source_target_pairs={{0,4},{4,0},{8,12},{12,8},{16,20},{20,16},{24,28},{28,24},{1,5},{5... | collective-permute-start | bytes 2752520 | tf_op jit(solution)/shard_map/ppermute | solution.py:47
  604.6 89.5 %collective-permute-start.28 = (bf16[2,224,1280]{2,1,0:T(8,128)(2,1)}, bf16[2,224,1280]{2,1,0:T(8,128)(2,1)}, u32[]{:S(2)}, u32[]{:S(2)}) collective-permute-start(bf16[2,224,1280]{2,1,0:T(8,128)(2,1)} %fusion.25), channel_id=1, source_target_pairs={{0,16},{4,20},{8,24},{12,28},{16,0},{20,4},{24,8},{28,12},{1,17},{... | collective-permute-start | bytes 3440648 | tf_op jit(solution)/shard_map/ppermute | solution.py:47
  606.4 87.8 %collective-permute-start.29 = (bf16[2,224,1280]{2,1,0:T(8,128)(2,1)}, bf16[2,224,1280]{2,1,0:T(8,128)(2,1)}, u32[]{:S(2)}, u32[]{:S(2)}) collective-permute-start(bf16[2,224,1280]{2,1,0:T(8,128)(2,1)} %fusion.26), channel_id=1, source_target_pairs={{0,8},{4,12},{8,0},{12,4},{16,24},{20,28},{24,16},{28,20},{1,9},{5... | collective-permute-start | bytes 3440648 | tf_op jit(solution)/shard_map/ppermute | solution.py:47
  636.0 66.0 %collective-permute-start.26 = (bf16[2,2,224,1280]{3,2,1,0:T(8,128)(2,1)}, bf16[2,2,224,1280]{3,2,1,0:T(8,128)(2,1)}, u32[]{:S(2)}, u32[]{:S(2)}) collective-permute-start(bf16[2,2,224,1280]{3,2,1,0:T(8,128)(2,1)} %get-tuple-element.190), channel_id=1, source_target_pairs={{0,8},{4,12},{8,0},{12,4},{16,24},{20,28},{24,16},{28,20},{1,9},{5... | collective-permute-start | bytes 6881288 | tf_op jit(solution)/shard_map/ppermute | solution.py:47
  636.6 65.4 %collective-permute-start.27 = (bf16[2,2,224,1280]{3,2,1,0:T(8,128)(2,1)}, bf16[2,2,224,1280]{3,2,1,0:T(8,128)(2,1)}, u32[]{:S(2)}, u32[]{:S(2)}) collective-permute-start(bf16[2,2,224,1280]{3,2,1,0:T(8,128)(2,1)} %get-tuple-element.191), channel_id=1, source_target_pairs={{0,16},{4,20},{8,24},{12,28},{16,0},{20,4},{24,8},{28,12},{1,17},{... | collective-permute-start | bytes 6881288 | tf_op jit(solution)/shard_map/ppermute | solution.py:47
  687.9 76.4 %all-to-all-start.6 = ((bf16[32,160,128]{2,1,0:T(8,128)(2,1)}), bf16[32,160,128]{2,1,0:T(8,128)(2,1)}, u32[]{:S(2)}, u32[]{:S(2)}) async-start(bf16[32,160,128]{2,1,0:T(8,128)(2,1)} %fusion.23), calls=%async_computation.6 | async-start | bytes 2621440 | tf_op jit(solution)/shard_map/all_to_all | solution.py:758
  700.1 52.2 %collective-permute-start.32 = (bf16[2,224,1280]{2,1,0:T(8,128)(2,1)}, bf16[2,224,1280]{2,1,0:T(8,128)(2,1)}, u32[]{:S(2)}, u32[]{:S(2)}) collective-permute-start(bf16[2,224,1280]{2,1,0:T(8,128)(2,1)} %pad_maximum_fusion.4), channel_id=1, source_target_pairs={{0,1},{1,0},{2,3},{3,2},{4,5},{5,4},{6,7},{7,6},{8,9},{9,8},{10,11... | collective-permute-start | bytes 3440648 | tf_op jit(solution)/shard_map/ppermute | solution.py:47
  702.0 59.0 %collective-permute-start.30 = (bf16[2,2,224,1280]{3,2,1,0:T(8,128)(2,1)}, bf16[2,2,224,1280]{3,2,1,0:T(8,128)(2,1)}, u32[]{:S(2)}, u32[]{:S(2)}) collective-permute-start(bf16[2,2,224,1280]{3,2,1,0:T(8,128)(2,1)} %get-tuple-element.196), channel_id=1, source_target_pairs={{0,8},{4,12},{8,0},{12,4},{16,24},{20,28},{24,16},{28,20},{1,9},{5... | collective-permute-start | bytes 6881288 | tf_op jit(solution)/shard_map/ppermute | solution.py:47
  703.4 57.5 %collective-permute-start.31 = (bf16[2,2,224,1280]{3,2,1,0:T(8,128)(2,1)}, bf16[2,2,224,1280]{3,2,1,0:T(8,128)(2,1)}, u32[]{:S(2)}, u32[]{:S(2)}) collective-permute-start(bf16[2,2,224,1280]{3,2,1,0:T(8,128)(2,1)} %get-tuple-element.197), channel_id=1, source_target_pairs={{0,16},{4,20},{8,24},{12,28},{16,0},{20,4},{24,8},{28,12},{1,17},{... | collective-permute-start | bytes 6881288 | tf_op jit(solution)/shard_map/ppermute | solution.py:47
  764.3 72.0 %all-to-all-start.7 = ((bf16[32,160,128]{2,1,0:T(8,128)(2,1)}), bf16[32,160,128]{2,1,0:T(8,128)(2,1)}, u32[]{:S(2)}, u32[]{:S(2)}) async-start(bf16[32,160,128]{2,1,0:T(8,128)(2,1)} %fusion.24), calls=%async_computation.7 | async-start | bytes 2621440 | tf_op jit(solution)/shard_map/all_to_all | solution.py:758
  772.7 53.4 %collective-permute-start.33 = (bf16[2,224,1280]{2,1,0:T(8,128)(2,1)}, bf16[2,224,1280]{2,1,0:T(8,128)(2,1)}, u32[]{:S(2)}, u32[]{:S(2)}) collective-permute-start(bf16[2,224,1280]{2,1,0:T(8,128)(2,1)} %fusion.27), channel_id=1, source_target_pairs={{0,16},{4,20},{8,24},{12,28},{16,0},{20,4},{24,8},{28,12},{1,17},{... | collective-permute-start | bytes 3440648 | tf_op jit(solution)/shard_map/ppermute | solution.py:47
  777.2 49.0 %collective-permute-start.34 = (bf16[2,224,1280]{2,1,0:T(8,128)(2,1)}, bf16[2,224,1280]{2,1,0:T(8,128)(2,1)}, u32[]{:S(2)}, u32[]{:S(2)}) collective-permute-start(bf16[2,224,1280]{2,1,0:T(8,128)(2,1)} %fusion.28), channel_id=1, source_target_pairs={{0,8},{4,12},{8,0},{12,4},{16,24},{20,28},{24,16},{28,20},{1,9},{5... | collective-permute-start | bytes 3440648 | tf_op jit(solution)/shard_map/ppermute | solution.py:47
  781.2 54.7 %collective-permute-start.35 = (bf16[2,224,1280]{2,1,0:T(8,128)(2,1)}, bf16[2,224,1280]{2,1,0:T(8,128)(2,1)}, u32[]{:S(2)}, u32[]{:S(2)}) collective-permute-start(bf16[2,224,1280]{2,1,0:T(8,128)(2,1)} %fusion.29), channel_id=1, source_target_pairs={{0,16},{4,20},{8,24},{12,28},{16,0},{20,4},{24,8},{28,12},{1,17},{... | collective-permute-start | bytes 3440648 | tf_op jit(solution)/shard_map/ppermute | solution.py:47
  784.5 51.8 %collective-permute-start.36 = (bf16[2,224,1280]{2,1,0:T(8,128)(2,1)}, bf16[2,224,1280]{2,1,0:T(8,128)(2,1)}, u32[]{:S(2)}, u32[]{:S(2)}) collective-permute-start(bf16[2,224,1280]{2,1,0:T(8,128)(2,1)} %fusion.30), channel_id=1, source_target_pairs={{0,8},{4,12},{8,0},{12,4},{16,24},{20,28},{24,16},{28,20},{1,9},{5... | collective-permute-start | bytes 3440648 | tf_op jit(solution)/shard_map/ppermute | solution.py:47
  873.2 52.6 %collective-permute-start.52 = (bf16[2,2,224,1280]{3,2,1,0:T(8,128)(2,1)}, bf16[2,2,224,1280]{3,2,1,0:T(8,128)(2,1)}, u32[]{:S(2)}, u32[]{:S(2)}) collective-permute-start(bf16[2,2,224,1280]{3,2,1,0:T(8,128)(2,1)} %pad_maximum_fusion), channel_id=1, source_target_pairs={{0,1},{1,0},{2,3},{3,2},{4,5},{5,4},{6,7},{7,6},{8,9},{9,8},{10,11... | collective-permute-start | bytes 6881288 | tf_op jit(solution)/shard_map/ppermute | solution.py:47
  905.2 52.0 %collective-permute-start.44 = (bf16[2,224,512]{2,1,0:T(8,128)(2,1)}, bf16[2,224,512]{2,1,0:T(8,128)(2,1)}, u32[]{:S(2)}, u32[]{:S(2)}) collective-permute-start(bf16[2,224,512]{2,1,0:T(8,128)(2,1)} %fusion.48), channel_id=1, source_target_pairs={{0,16},{4,20},{8,24},{12,28},{16,0},{20,4},{24,8},{28,12},{1,17},{... | collective-permute-start | bytes 1376264 | tf_op jit(solution)/shard_map/ppermute | solution.py:47
  906.4 52.2 %collective-permute-start.46 = (bf16[2,224,512]{2,1,0:T(8,128)(2,1)}, bf16[2,224,512]{2,1,0:T(8,128)(2,1)S(1)}, u32[]{:S(2)}, u32[]{:S(2)}) collective-permute-start(bf16[2,224,512]{2,1,0:T(8,128)(2,1)} %fusion.49), channel_id=1, source_target_pairs={{0,8},{4,12},{8,0},{12,4},{16,24},{20,28},{24,16},{28,20},{1,9},{5... | collective-permute-start | bytes 1376264 | tf_op jit(solution)/shard_map/ppermute | solution.py:47
  927.4 64.1 %collective-permute-start.53 = (bf16[2,224,1280]{2,1,0:T(8,128)(2,1)S(1)}, bf16[2,224,1280]{2,1,0:T(8,128)(2,1)S(1)}, u32[]{:S(2)}, u32[]{:S(2)}) collective-permute-start(bf16[2,224,1280]{2,1,0:T(8,128)(2,1)S(1)} %fusion.31), channel_id=1, source_target_pairs={{0,2},{1,3},{2,0},{3,1},{4,6},{5,7},{6,4},{7,5},{8,10},{9,11},{10,... | collective-permute-start | bytes 3440648 | tf_op jit(solution)/shard_map/ppermute | solution.py:47
  (95 other events, 1684.0 us)
Sparse Core Ops, SparseCore 0:
  114.0 310.5 all-gather.2

commit v5 on v4

--- a/solution.py
+++ b/solution.py
@@ -1245,7 +1245,6 @@
     two_left = Left(normed_two)
     gate_sum = Scatter(two_left, grads_gu)
     up_sum = Scatter(two_left, grads_gu, False, *gate_sum.other_side(), kind=1)
-    gain_two_grad = jnp.sum(back_two * residual * scale_two, axis=0)
     grad_residual = cot_low.astype(f32) + norm_back(residual, scale_two, gain_two, back_two)
     grad_res_low = grad_residual.astype(bf16)
 
@@ -1259,6 +1258,7 @@
         terms.right = tie(terms.right, *down_sends)
     up_sum.right = tie(up_sum.right, *arrived[1:])
     made += up_sum.products() + out_sum.products()
+    gain_two_grad = jnp.sum(tie(back_two, *made) * residual * scale_two, axis=0)
     gate_sum.go(*down_sends)
     arrived[0] = tie(arrived[0], *made)
     backs, grad_keys = [], []

time: 1070 us -> 1090 us (1.019)
  transfers between devices with their start and end apart: 64 -> 64, of which waited for: 21 -> 21; matrix products, arithmetic and copies ran while one was open for 16% -> 16% of each run, Pallas kernels for 28% -> 27%
where the time goes in v5:
time: 1090 us; the launch traced here: 1070 us
  Pallas kernels  471 us (43%)
  waiting for transfers between devices  298 us (27%)
  other arithmetic  105 us (10%)
  local copies, waits for them, and re-layouts  98.1 us (9%)
  starting transfers between devices  86.9 us (8%)
  between operations  15.7 us (1%)
    ppermute x54, waiting for transfers between devices, swap(): return lax.ppermute(block, axis, [(i, i ^ bit) for i in devices])  168 us
    all_to_all x8, waiting for transfers between devices, exchange(): lax.all_to_all(blocks, BOTH, 0, 0, tiled=True, axis_index_groups=self.gro...  120 us
    pallas_call x1, Pallas kernels, gather_first(): pl.pallas_call(gather_kernel, in_specs=[anywhere] * (2 + count), out_spec...  94.3 us
    pallas_call x2, Pallas kernels, attend_back(): pl.pallas_call(functools.partial(attend_back_kernel, chunk), grid=(steps,...  89.6 us
    pallas_call x10, Pallas kernels, weight_grads(): pl.pallas_call(functools.partial(grad_kernel, first), grid_spec=pltpu.Pre...  89.1 us
    ppermute x54, starting transfers between devices, swap(): return lax.ppermute(block, axis, [(i, i ^ bit) for i in devices])  47.7 us
    pallas_call x2, Pallas kernels, attend(): pl.pallas_call(functools.partial(attend_kernel, chunk), grid=(steps,), in...  43.4 us
    all_to_all x8, starting transfers between devices, exchange(): lax.all_to_all(blocks, BOTH, 0, 0, tiled=True, axis_index_groups=self.gro...  35.2 us
  transfers between devices with their start and end apart: 64, of which 21 were waited for; matrix products, arithmetic and copies ran while one was open for 16% of the time, Pallas kernels for 27%

profile of v5, /device:TPU:0, one launch (start us, length us, event | category | flops | bytes accessed | tf_op | source)
XLA Modules:
  0.0 1074.2 jit_solution(4772764084038633251)
XLA Ops:
  19.6 94.3 %shard_map.255 = (bf16[8,4,1,240,1024]{4,3,2,1,0:T(8,128)(2,1)}, bf16[2,16,1792]{2,1,0:T(8,128)(2,1)}, bf16[4,224,1280]{2,1,0:T(8,128)(2,1)}, bf16[4,224,512]{2,1,0:T(8,128)(2,1)}) custom-call(bf16[240,1024]{1,0:T(8,128)(2,1)} %pad_maximum_fusion.7.shard, bf16[16,1792]{1,0:T(8,128)(2,1)} %reshape.340.edge, bf16[224,1280]{1,0:T(8,128)(2,1)} %pad.24.refs_0_, ...), custom_call_target="tpu_custom_call" | custom-call | flops 99999997952 | bytes 1 | tf_op jit(solution)/shard_map/pallas_call | solution.py:191
  133.8 15.9 %shard_map.256 = (bf16[4,512,448]{2,1,0:T(8,128)(2,1)}, f32[4,512,448]{2,1,0:T(8,128)}, f32[4,2,16,448]{3,2,1,0:T(8,128)}, bf16[4,2,4,128,128]{4,3,2,1,0:T(8,128...) custom-call(bf16[512,1792]{1,0:T(8,128)(2,1)} %fusion.3.x_ref, ...), custom_call_target="tpu_custom_call" | custom-call | flops 11274289152 | bytes 1 | tf_op jit(solution)/shard_map/pallas_call | solution.py:1015
  172.0 38.9 %all-to-all-done = bf16[32,144,128]{2,1,0:T(8,128)(2,1)S(1)} async-done(((bf16[32,144,128]{2,1,0:T(8,128)(2,1)}), bf16[32,144,128]{2,1,0:T(8,128)(2,1)S(1)}, u32[]{:S(2)}, u32[]{:S(2)}) %all-to-all-start) | async-done | bytes 1179680 | tf_op jit(solution)/shard_map/all_to_all | solution.py:758
  219.9 21.7 %shard_map.257 = (f32[4096,128]{1,0:T(8,128)}, bf16[4096,128]{1,0:T(8,128)(2,1)}) custom-call(bf16[4096,128]{1,0:T(8,128)(2,1)} %bitcast.324, bf16[4096,16]{1,0:T(8,128)(2,1)} %bitcast.318, f32[4096,1]{1,0:T(8,128)} %copy.161.seg_col, f32[8,1,512]{2,1,0:T(1,128)} %bitcast.346), custom_call_target="tpu_custom_call" | custom-call | flops 25769803776 | bytes 1 | tf_op jit(solution)/shard_map/pallas_call | solution.py:823
  241.6 60.7 %all-to-all-done.2 = bf16[32,144,128]{2,1,0:T(8,128)(2,1)} async-done(((bf16[32,144,128]{2,1,0:T(8,128)(2,1)}), bf16[32,144,128]{2,1,0:T(8,128)(2,1)}, u32[]{:S(2)}, u32[]{:S(2)}) %all-to-all-start.2) | async-done | bytes 1179680 | tf_op jit(solution)/shard_map/all_to_all | solution.py:758
  312.2 21.7 %shard_map.258 = (f32[4096,128]{1,0:T(8,128)}, bf16[4096,128]{1,0:T(8,128)(2,1)}) custom-call(bf16[4096,128]{1,0:T(8,128)(2,1)} %bitcast.322, bf16[4096,16]{1,0:T(8,128)(2,1)} %bitcast.316, f32[4096,1]{1,0:T(8,128)} %copy.161.seg_col, f32[8,1,512]{2,1,0:T(1,128)} %bitcast.347), custom_call_target="tpu_custom_call" | custom-call | flops 25769803776 | bytes 1 | tf_op jit(solution)/shard_map/pallas_call | solution.py:823
  333.8 20.2 %all-to-all-done.1 = bf16[32,128,128]{2,1,0:T(8,128)(2,1)S(1)} async-done(((bf16[32,128,128]{2,1,0:T(8,128)(2,1)}), bf16[32,128,128]{2,1,0:T(8,128)(2,1)S(1)}, u32[]{:S(2)}, u32[]{:S(2)}) %all-to-all-start.1) | async-done | bytes 1048608 | tf_op jit(solution)/shard_map/all_to_all | solution.py:758
  368.1 39.2 %collective-permute-done.8.refs_6_.refs_4_ = bf16[2,224,512]{2,1,0:T(8,128)(2,1)S(1)} collective-permute-done((bf16[2,224,512]{2,1,0:T(8,128)(2,1)S(1)}, bf16[2,224,512]{2,1,0:T(8,128)(2,1)S(1)}, u32[]{:S(2)}, u32[]{:S(2)}) %collective-permute-start.8) | collective-permute-done | bytes 458784 | tf_op jit(solution)/shard_map/ppermute | solution.py:47
  413.0 11.5 %shard_map.259 = (bf16[4,1,512,512]{3,2,1,0:T(8,128)(2,1)}, f32[512,1792]{1,0:T(8,128)}) custom-call(s32[10]{0:T(128)} %xor_multiply_fusion.offsets, s32[4]{0:T(128)} %iota_xor_fusion.places, bf16[4,2,4,128,128]{4,3,2,1,0:T(8,128)(2,1)} %bitcast.326, bf16[4,2,4,128,128]{4,3,2,1,0:T(8,128)(2,1)} %bitcast.32.refs_1_, ...), custom_call_target="tpu_custom_call" | custom-call | flops 5637144576 | bytes 1 | tf_op jit(solution)/shard_map/pallas_call | solution.py:561
  434.1 26.6 %shard_map.260 = (bf16[4,512,1216]{2,1,0:T(8,128)(2,1)}, bf16[4,512,1216]{2,1,0:T(8,128)(2,1)}, bf16[4,1,512,1280]{3,2,1,0:T(8,128)(2,1)}) custom-call(bf16[512,1792]{1,0:T(8,128)(2,1)} %multiply_convert_fusion.x_ref, bf16[8,4,2,224,1216]{4,3,2,1,0:T(8,128)(2,1)} %bitcast.289), custom_call_target="tpu_custom_call" | custom-call | flops 26776436736 | bytes 1 | tf_op jit(solution)/shard_map/pallas_call | solution.py:654
  460.8 18.0 %shard_map.261.grad_ref = f32[4,512,1280]{2,1,0:T(8,128)} custom-call(s32[10]{0:T(128)} %xor_multiply_fusion.offsets, s32[4]{0:T(128)} %iota_xor_fusion.places, bf16[512,1792]{1,0:T(8,128)(2,1)} %bitcast.291, bf16[4,224,1280]{2,1,0:T(8,128)(2,1)} %get-tuple-element.142.refs_0_, bf16[4,224,1280]{2,1,0:T(8,128)(2,1)} %collective-permute-done.3.refs_1_, ...), custom_call_target="tpu_custom_call" | custom-call | flops 14092861440 | bytes 1 | tf_op jit(solution)/shard_map/pallas_call | solution.py:592
  478.8 8.9 shard_map.263
  487.7 19.0 %shard_map.262 = (bf16[2,2,224,1280]{3,2,1,0:T(8,128)(2,1)}, bf16[2,2,224,1280]{3,2,1,0:T(8,128)(2,1)}) custom-call(s32[1]{0:T(128)} %bitcast.36.plane, bf16[4,224,512]{2,1,0:T(8,128)(2,1)} %get-tuple-element.326.left0, bf16[4,224,512]{2,1,0:T(8,128)(2,1)} %collective-permute-done.left1, bf16[4,1,512,1280]{3,2,1,0:T(8,128)(2,1)} %get-tuple-element.233.right0.y_ref, ...), custom_call_target="tpu_custom_call" | custom-call | flops 5872025600 | bytes 1 | tf_op jit(solution)/shard_map/pallas_call | solution.py:307
  506.7 28.5 %shard_map.264 = (bf16[4,2,512,1280]{3,2,1,0:T(8,128)(2,1)}, f32[512,1792]{1,0:T(8,128)}) custom-call(f32[4,512,1280]{2,1,0:T(8,128)} %shard_map.261.grad_ref, bf16[8,4,2,224,1216]{4,3,2,1,0:T(8,128)(2,1)} %bitcast.290, bf16[4,512,1216]{2,1,0:T(8,128)(2,1)} %get-tuple-element.165.slope_ref, bf16[4,512,1216]{2,1,0:T(8,128)(2,1)} %get-tuple-element.166.silu_ref), custom_call_target="tpu_custom_call" | custom-call | flops 1 | bytes 1 | tf_op jit(solution)/shard_map/pallas_call | solution.py:687
  549.5 10.3 shard_map.265
  568.6 8.9 shard_map.267
  577.5 8.9 shard_map.266
  586.4 16.0 %collective-permute-done.24 = bf16[2,2,224,1280]{3,2,1,0:T(8,128)(2,1)} collective-permute-done((bf16[2,2,224,1280]{3,2,1,0:T(8,128)(2,1)}, bf16[2,2,224,1280]{3,2,1,0:T(8,128)(2,1)}, u32[]{:S(2)}, u32[]{:S(2)}) %collective-permute-start.24) | collective-permute-done | bytes 2293792 | tf_op jit(solution)/shard_map/ppermute | solution.py:47
  627.2 8.9 shard_map.269
  636.1 8.9 shard_map.268
  646.0 44.8 %shard_map.272 = (bf16[4096,128]{1,0:T(8,128)(2,1)}, bf16[4096,16]{1,0:T(8,128)(2,1)}) custom-call(bf16[4096,128]{1,0:T(8,128)(2,1)} %bitcast.325, bf16[4096,16]{1,0:T(8,128)(2,1)} %bitcast.319, f32[4096,128]{1,0:T(8,128)} %get-tuple-element.159.kept, bf16[4096,128]{1,0:T(8,128)(2,1)} %bitcast.330, f32[4096,1]{1,0:T(8,128)} %copy.161.seg_col, ...), custom_call_target="tpu_custom_call" | custom-call | flops 51539607552 | bytes 1 | tf_op jit(solution)/shard_map/pallas_call | solution.py:922
  714.2 44.8 %shard_map.273 = (bf16[4096,128]{1,0:T(8,128)(2,1)}, bf16[4096,16]{1,0:T(8,128)(2,1)}) custom-call(bf16[4096,128]{1,0:T(8,128)(2,1)} %bitcast.323, bf16[4096,16]{1,0:T(8,128)(2,1)} %bitcast.317, f32[4096,128]{1,0:T(8,128)} %get-tuple-element.189.kept, bf16[4096,128]{1,0:T(8,128)(2,1)} %bitcast.57.grad, f32[4096,1]{1,0:T(8,128)} %copy.161.seg_col, ...), custom_call_target="tpu_custom_call" | custom-call | flops 51539607552 | bytes 1 | tf_op jit(solution)/shard_map/pallas_call | solution.py:922
  799.6 35.6 %collective-permute-done.37 = bf16[224,1280]{1,0:T(8,128)(2,1)S(1)} collective-permute-done((bf16[224,1280]{1,0:T(8,128)(2,1)S(1)}, bf16[224,1280]{1,0:T(8,128)(2,1)S(1)}, u32[]{:S(2)}, u32[]{:S(2)}) %collective-permute-start.37) | collective-permute-done | bytes 573472 | tf_op jit(solution)/shard_map/ppermute | solution.py:47
  836.1 8.9 collective-permute-done.34
  857.2 12.4 %shard_map.274 = (bf16[4,512,1024]{2,1,0:T(8,128)(2,1)}, f32[4,3,448]{2,1,0:T(4,128)}) custom-call(bf16[4,512,448]{2,1,0:T(8,128)(2,1)} %get-tuple-element.156.v_ref, f32[4,512,448]{2,1,0:T(8,128)} %get-tuple-element.157.f_ref, f32[4,2,16,448]{3,2,1,0:T(8,128)} %get-tuple-element.158.side_ref, f32[512,4]{1,0:T(8,128)} %stack.88.same_ref, ...), custom_call_target="tpu_custom_call" | custom-call | flops 1 | bytes 1 | tf_op jit(solution)/shard_map/pallas_call | solution.py:1090
  915.1 13.5 %shard_map.277 = f32[512,1792]{1,0:T(8,128)} custom-call(bf16[4,512,1024]{2,1,0:T(8,128)(2,1)} %get-tuple-element.225.y_ref, bf16[8,4,1,240,1024]{4,3,2,1,0:T(8,128)(2,1)} %get-tuple-element.130.w_ref), custom_call_target="tpu_custom_call" | custom-call | flops 1 | bytes 1 | tf_op jit(solution)/shard_map/pallas_call | solution.py:494
  932.6 9.7 collective-permute-done.52
  946.3 8.5 collective-permute-done.42
  968.7 14.2 %collective-permute-done.47 = bf16[2,224,1024]{2,1,0:T(8,128)(2,1)S(1)} collective-permute-done((bf16[2,224,1024]{2,1,0:T(8,128)(2,1)S(1)}, bf16[2,224,1024]{2,1,0:T(8,128)(2,1)S(1)}, u32[]{:S(2)}, u32[]{:S(2)}) %collective-permute-start.47) | collective-permute-done | bytes 917536 | tf_op jit(solution)/shard_map/ppermute | solution.py:47
  989.1 15.8 %collective-permute-done.49 = bf16[2,224,512]{2,1,0:T(8,128)(2,1)S(1)} collective-permute-done((bf16[2,224,512]{2,1,0:T(8,128)(2,1)S(1)}, bf16[2,224,512]{2,1,0:T(8,128)(2,1)S(1)}, u32[]{:S(2)}, u32[]{:S(2)}) %collective-permute-start.49) | collective-permute-done | bytes 458784 | tf_op jit(solution)/shard_map/ppermute | solution.py:47
  1009.5 17.9 %shard_map.278 = f32[512,1792]{1,0:T(8,128)} custom-call(s32[10]{0:T(128)} %xor_multiply_fusion.offsets, s32[4]{0:T(128)} %iota_xor_fusion.places, bf16[4,1,512,1280]{3,2,1,0:T(8,128)(2,1)} %get-tuple-element.233.right0.y_ref, bf16[4,224,1280]{2,1,0:T(8,128)(2,1)} %get-tuple-element.142.refs_0_, bf16[4,224,1280]{2,1,0:T(8,128)(2,1)} %collective-permute-done.3.refs_1_, ...), custom_call_target="tpu_custom_call" | custom-call | flops 14092861440 | bytes 1 | tf_op jit(solution)/shard_map/pallas_call | solution.py:620
  1050.2 10.3 all-to-all-done.8
  (417 shorter events, 335.2 us)
Async XLA Ops:
  7.2 426.9 %all-gather.3.cloned.1.call-start = ((), (), s32[]{:S(2)}) async-start(), calls=%async_computation.9 | async-start | bytes 37847040 | tf_op jit(solution)/shard_map/all_gather | solution.py:59
  154.3 56.6 %all-to-all-start = ((bf16[32,144,128]{2,1,0:T(8,128)(2,1)}), bf16[32,144,128]{2,1,0:T(8,128)(2,1)S(1)}, u32[]{:S(2)}, u32[]{:S(2)}) async-start(bf16[32,144,128]{2,1,0:T(8,128)(2,1)} %pad_maximum_fusion.1), calls=%async_computation | async-start | bytes 2359296 | tf_op jit(solution)/shard_map/all_to_all | solution.py:758
  158.4 149.9 %collective-permute-start.3 = (bf16[4,224,1280]{2,1,0:T(8,128)(2,1)}, bf16[4,224,1280]{2,1,0:T(8,128)(2,1)}, u32[]{:S(2)}, u32[]{:S(2)}) collective-permute-start(bf16[4,224,1280]{2,1,0:T(8,128)(2,1)} %get-tuple-element.142.refs_0_), channel_id=1, source_target_pairs={{0,8},{4,12},{8,0},{12,4},{16,24},{20,28},{24,16},{28,20},{1,9},{5... | collective-permute-start | bytes 6881288 | tf_op jit(solution)/shard_map/ppermute | solution.py:47
  160.2 148.1 %collective-permute-start.4 = (bf16[4,224,1280]{2,1,0:T(8,128)(2,1)}, bf16[4,224,1280]{2,1,0:T(8,128)(2,1)}, u32[]{:S(2)}, u32[]{:S(2)}) collective-permute-start(bf16[4,224,1280]{2,1,0:T(8,128)(2,1)} %get-tuple-element.142.refs_0_), channel_id=1, source_target_pairs={{0,16},{4,20},{8,24},{12,28},{16,0},{20,4},{24,8},{28,12},{1,17},{... | collective-permute-start | bytes 6881288 | tf_op jit(solution)/shard_map/ppermute | solution.py:47
  161.7 146.6 %collective-permute-start.1 = (bf16[4,224,512]{2,1,0:T(8,128)(2,1)}, bf16[4,224,512]{2,1,0:T(8,128)(2,1)}, u32[]{:S(2)}, u32[]{:S(2)}) collective-permute-start(bf16[4,224,512]{2,1,0:T(8,128)(2,1)} %get-tuple-element.141.refs_2_.refs_0_), channel_id=1, source_target_pairs={{0,8},{4,12},{8,0},{12,4},{16,24},{20,28},{24,16},{28,20},{1,9},{5... | collective-permute-start | bytes 2752520 | tf_op jit(solution)/shard_map/ppermute | solution.py:47
  162.3 146.1 %collective-permute-start.2 = (bf16[4,224,512]{2,1,0:T(8,128)(2,1)}, bf16[4,224,512]{2,1,0:T(8,128)(2,1)}, u32[]{:S(2)}, u32[]{:S(2)}) collective-permute-start(bf16[4,224,512]{2,1,0:T(8,128)(2,1)} %get-tuple-element.141.refs_2_.refs_0_), channel_id=1, source_target_pairs={{0,16},{4,20},{8,24},{12,28},{16,0},{20,4},{24,8},{28,12},{1,17},{... | collective-permute-start | bytes 2752520 | tf_op jit(solution)/shard_map/ppermute | solution.py:47
  212.1 90.2 %all-to-all-start.2 = ((bf16[32,144,128]{2,1,0:T(8,128)(2,1)}), bf16[32,144,128]{2,1,0:T(8,128)(2,1)}, u32[]{:S(2)}, u32[]{:S(2)}) async-start(bf16[32,144,128]{2,1,0:T(8,128)(2,1)} %bitcast.300), calls=%async_computation.2 | async-start | bytes 2359296 | tf_op jit(solution)/shard_map/all_to_all | solution.py:758
  302.3 51.7 %all-to-all-start.1 = ((bf16[32,128,128]{2,1,0:T(8,128)(2,1)}), bf16[32,128,128]{2,1,0:T(8,128)(2,1)S(1)}, u32[]{:S(2)}, u32[]{:S(2)}) async-start(bf16[32,128,128]{2,1,0:T(8,128)(2,1)} %bitcast.331), calls=%async_computation.1 | async-start | bytes 2097152 | tf_op jit(solution)/shard_map/all_to_all | solution.py:758
  354.0 56.7 %all-to-all-start.3 = ((bf16[32,128,128]{2,1,0:T(8,128)(2,1)}), bf16[32,128,128]{2,1,0:T(8,128)(2,1)}, u32[]{:S(2)}, u32[]{:S(2)}) async-start(bf16[32,128,128]{2,1,0:T(8,128)(2,1)} %bitcast.328), calls=%async_computation.3 | async-start | bytes 2097152 | tf_op jit(solution)/shard_map/all_to_all | solution.py:758
  368.1 57.2 %collective-permute-start.15 = (bf16[4,224,1280]{2,1,0:T(8,128)(2,1)}, bf16[4,224,1280]{2,1,0:T(8,128)(2,1)}, u32[]{:S(2)}, u32[]{:S(2)}) collective-permute-start(bf16[4,224,1280]{2,1,0:T(8,128)(2,1)} %get-tuple-element.142.refs_0_), channel_id=1, source_target_pairs={{0,4},{4,0},{8,12},{12,8},{16,20},{20,16},{24,28},{28,24},{1,5},{5... | collective-permute-start | bytes 6881288 | tf_op jit(solution)/shard_map/ppermute | solution.py:47
  541.0 61.4 %collective-permute-start.24 = (bf16[2,2,224,1280]{3,2,1,0:T(8,128)(2,1)}, bf16[2,2,224,1280]{3,2,1,0:T(8,128)(2,1)}, u32[]{:S(2)}, u32[]{:S(2)}) collective-permute-start(bf16[2,2,224,1280]{3,2,1,0:T(8,128)(2,1)} %get-tuple-element.163), channel_id=1, source_target_pairs={{0,16},{4,20},{8,24},{12,28},{16,0},{20,4},{24,8},{28,12},{1,17},{... | collective-permute-start | bytes 6881288 | tf_op jit(solution)/shard_map/ppermute | solution.py:47
  542.5 61.4 %collective-permute-start.23 = (bf16[2,2,224,1280]{3,2,1,0:T(8,128)(2,1)}, bf16[2,2,224,1280]{3,2,1,0:T(8,128)(2,1)}, u32[]{:S(2)}, u32[]{:S(2)}) collective-permute-start(bf16[2,2,224,1280]{3,2,1,0:T(8,128)(2,1)} %get-tuple-element.162), channel_id=1, source_target_pairs={{0,8},{4,12},{8,0},{12,4},{16,24},{20,28},{24,16},{28,20},{1,9},{5... | collective-permute-start | bytes 6881288 | tf_op jit(solution)/shard_map/ppermute | solution.py:47
  559.8 47.2 %all-to-all-start.5 = ((bf16[32,128,128]{2,1,0:T(8,128)(2,1)}), bf16[32,128,128]{2,1,0:T(8,128)(2,1)}, u32[]{:S(2)}, u32[]{:S(2)}) async-start(bf16[32,128,128]{2,1,0:T(8,128)(2,1)} %bitcast.329), calls=%async_computation.5 | async-start | bytes 2097152 | tf_op jit(solution)/shard_map/all_to_all | solution.py:758
  567.5 49.4 %collective-permute-start.25 = (bf16[4,224,512]{2,1,0:T(8,128)(2,1)}, bf16[4,224,512]{2,1,0:T(8,128)(2,1)}, u32[]{:S(2)}, u32[]{:S(2)}) collective-permute-start(bf16[4,224,512]{2,1,0:T(8,128)(2,1)} %get-tuple-element.322), channel_id=1, source_target_pairs={{0,4},{4,0},{8,12},{12,8},{16,20},{20,16},{24,28},{28,24},{1,5},{5... | collective-permute-start | bytes 2752520 | tf_op jit(solution)/shard_map/ppermute | solution.py:47
  612.8 90.6 %collective-permute-start.29 = (bf16[2,224,1280]{2,1,0:T(8,128)(2,1)}, bf16[2,224,1280]{2,1,0:T(8,128)(2,1)}, u32[]{:S(2)}, u32[]{:S(2)}) collective-permute-start(bf16[2,224,1280]{2,1,0:T(8,128)(2,1)} %fusion.26), channel_id=1, source_target_pairs={{0,8},{4,12},{8,0},{12,4},{16,24},{20,28},{24,16},{28,20},{1,9},{5... | collective-permute-start | bytes 3440648 | tf_op jit(solution)/shard_map/ppermute | solution.py:47
  614.7 88.8 %collective-permute-start.28 = (bf16[2,224,1280]{2,1,0:T(8,128)(2,1)}, bf16[2,224,1280]{2,1,0:T(8,128)(2,1)}, u32[]{:S(2)}, u32[]{:S(2)}) collective-permute-start(bf16[2,224,1280]{2,1,0:T(8,128)(2,1)} %fusion.25), channel_id=1, source_target_pairs={{0,16},{4,20},{8,24},{12,28},{16,0},{20,4},{24,8},{28,12},{1,17},{... | collective-permute-start | bytes 3440648 | tf_op jit(solution)/shard_map/ppermute | solution.py:47
  616.2 95.1 %collective-permute-start.27 = (bf16[2,2,224,1280]{3,2,1,0:T(8,128)(2,1)}, bf16[2,2,224,1280]{3,2,1,0:T(8,128)(2,1)}, u32[]{:S(2)}, u32[]{:S(2)}) collective-permute-start(bf16[2,2,224,1280]{3,2,1,0:T(8,128)(2,1)} %get-tuple-element.192), channel_id=1, source_target_pairs={{0,16},{4,20},{8,24},{12,28},{16,0},{20,4},{24,8},{28,12},{1,17},{... | collective-permute-start | bytes 6881288 | tf_op jit(solution)/shard_map/ppermute | solution.py:47
  616.7 94.5 %collective-permute-start.26 = (bf16[2,2,224,1280]{3,2,1,0:T(8,128)(2,1)}, bf16[2,2,224,1280]{3,2,1,0:T(8,128)(2,1)}, u32[]{:S(2)}, u32[]{:S(2)}) collective-permute-start(bf16[2,2,224,1280]{3,2,1,0:T(8,128)(2,1)} %get-tuple-element.191), channel_id=1, source_target_pairs={{0,8},{4,12},{8,0},{12,4},{16,24},{20,28},{24,16},{28,20},{1,9},{5... | collective-permute-start | bytes 6881288 | tf_op jit(solution)/shard_map/ppermute | solution.py:47
  697.0 77.4 %all-to-all-start.6 = ((bf16[32,160,128]{2,1,0:T(8,128)(2,1)}), bf16[32,160,128]{2,1,0:T(8,128)(2,1)}, u32[]{:S(2)}, u32[]{:S(2)}) async-start(bf16[32,160,128]{2,1,0:T(8,128)(2,1)} %fusion.23), calls=%async_computation.6 | async-start | bytes 2621440 | tf_op jit(solution)/shard_map/all_to_all | solution.py:758
  709.4 52.3 %collective-permute-start.32 = (bf16[2,224,1280]{2,1,0:T(8,128)(2,1)}, bf16[2,224,1280]{2,1,0:T(8,128)(2,1)}, u32[]{:S(2)}, u32[]{:S(2)}) collective-permute-start(bf16[2,224,1280]{2,1,0:T(8,128)(2,1)} %pad_maximum_fusion.4), channel_id=1, source_target_pairs={{0,1},{1,0},{2,3},{3,2},{4,5},{5,4},{6,7},{7,6},{8,9},{9,8},{10,11... | collective-permute-start | bytes 3440648 | tf_op jit(solution)/shard_map/ppermute | solution.py:47
  711.3 58.7 %collective-permute-start.31 = (bf16[2,2,224,1280]{3,2,1,0:T(8,128)(2,1)}, bf16[2,2,224,1280]{3,2,1,0:T(8,128)(2,1)}, u32[]{:S(2)}, u32[]{:S(2)}) collective-permute-start(bf16[2,2,224,1280]{3,2,1,0:T(8,128)(2,1)} %get-tuple-element.198), channel_id=1, source_target_pairs={{0,16},{4,20},{8,24},{12,28},{16,0},{20,4},{24,8},{28,12},{1,17},{... | collective-permute-start | bytes 6881288 | tf_op jit(solution)/shard_map/ppermute | solution.py:47
  712.7 58.3 %collective-permute-start.30 = (bf16[2,2,224,1280]{3,2,1,0:T(8,128)(2,1)}, bf16[2,2,224,1280]{3,2,1,0:T(8,128)(2,1)}, u32[]{:S(2)}, u32[]{:S(2)}) collective-permute-start(bf16[2,2,224,1280]{3,2,1,0:T(8,128)(2,1)} %get-tuple-element.197), channel_id=1, source_target_pairs={{0,8},{4,12},{8,0},{12,4},{16,24},{20,28},{24,16},{28,20},{1,9},{5... | collective-permute-start | bytes 6881288 | tf_op jit(solution)/shard_map/ppermute | solution.py:47
  774.4 71.2 %all-to-all-start.7 = ((bf16[32,160,128]{2,1,0:T(8,128)(2,1)}), bf16[32,160,128]{2,1,0:T(8,128)(2,1)}, u32[]{:S(2)}, u32[]{:S(2)}) async-start(bf16[32,160,128]{2,1,0:T(8,128)(2,1)} %fusion.24), calls=%async_computation.7 | async-start | bytes 2621440 | tf_op jit(solution)/shard_map/all_to_all | solution.py:758
  782.0 53.3 %collective-permute-start.36 = (bf16[2,224,1280]{2,1,0:T(8,128)(2,1)}, bf16[2,224,1280]{2,1,0:T(8,128)(2,1)S(1)}, u32[]{:S(2)}, u32[]{:S(2)}) collective-permute-start(bf16[2,224,1280]{2,1,0:T(8,128)(2,1)} %fusion.30), channel_id=1, source_target_pairs={{0,8},{4,12},{8,0},{12,4},{16,24},{20,28},{24,16},{28,20},{1,9},{5... | collective-permute-start | bytes 3440648 | tf_op jit(solution)/shard_map/ppermute | solution.py:47
  786.4 49.7 %collective-permute-start.35 = (bf16[2,224,1280]{2,1,0:T(8,128)(2,1)}, bf16[2,224,1280]{2,1,0:T(8,128)(2,1)}, u32[]{:S(2)}, u32[]{:S(2)}) collective-permute-start(bf16[2,224,1280]{2,1,0:T(8,128)(2,1)} %fusion.29), channel_id=1, source_target_pairs={{0,16},{4,20},{8,24},{12,28},{16,0},{20,4},{24,8},{28,12},{1,17},{... | collective-permute-start | bytes 3440648 | tf_op jit(solution)/shard_map/ppermute | solution.py:47
  790.5 54.5 %collective-permute-start.34 = (bf16[2,224,1280]{2,1,0:T(8,128)(2,1)}, bf16[2,224,1280]{2,1,0:T(8,128)(2,1)}, u32[]{:S(2)}, u32[]{:S(2)}) collective-permute-start(bf16[2,224,1280]{2,1,0:T(8,128)(2,1)} %fusion.28), channel_id=1, source_target_pairs={{0,8},{4,12},{8,0},{12,4},{16,24},{20,28},{24,16},{28,20},{1,9},{5... | collective-permute-start | bytes 3440648 | tf_op jit(solution)/shard_map/ppermute | solution.py:47
  793.8 51.8 %collective-permute-start.33 = (bf16[2,224,1280]{2,1,0:T(8,128)(2,1)}, bf16[2,224,1280]{2,1,0:T(8,128)(2,1)}, u32[]{:S(2)}, u32[]{:S(2)}) collective-permute-start(bf16[2,224,1280]{2,1,0:T(8,128)(2,1)} %fusion.27), channel_id=1, source_target_pairs={{0,16},{4,20},{8,24},{12,28},{16,0},{20,4},{24,8},{28,12},{1,17},{... | collective-permute-start | bytes 3440648 | tf_op jit(solution)/shard_map/ppermute | solution.py:47
  890.0 52.3 %collective-permute-start.52 = (bf16[2,2,224,1280]{3,2,1,0:T(8,128)(2,1)}, bf16[2,2,224,1280]{3,2,1,0:T(8,128)(2,1)}, u32[]{:S(2)}, u32[]{:S(2)}) collective-permute-start(bf16[2,2,224,1280]{3,2,1,0:T(8,128)(2,1)} %pad_maximum_fusion), channel_id=1, source_target_pairs={{0,1},{1,0},{2,3},{3,2},{4,5},{5,4},{6,7},{7,6},{8,9},{9,8},{10,11... | collective-permute-start | bytes 6881288 | tf_op jit(solution)/shard_map/ppermute | solution.py:47
  913.4 51.2 %collective-permute-start.46 = (bf16[2,224,512]{2,1,0:T(8,128)(2,1)}, bf16[2,224,512]{2,1,0:T(8,128)(2,1)}, u32[]{:S(2)}, u32[]{:S(2)}) collective-permute-start(bf16[2,224,512]{2,1,0:T(8,128)(2,1)} %fusion.49), channel_id=1, source_target_pairs={{0,8},{4,12},{8,0},{12,4},{16,24},{20,28},{24,16},{28,20},{1,9},{5... | collective-permute-start | bytes 1376264 | tf_op jit(solution)/shard_map/ppermute | solution.py:47
  914.3 51.7 %collective-permute-start.44 = (bf16[2,224,512]{2,1,0:T(8,128)(2,1)}, bf16[2,224,512]{2,1,0:T(8,128)(2,1)}, u32[]{:S(2)}, u32[]{:S(2)}) collective-permute-start(bf16[2,224,512]{2,1,0:T(8,128)(2,1)} %fusion.48), channel_id=1, source_target_pairs={{0,16},{4,20},{8,24},{12,28},{16,0},{20,4},{24,8},{28,12},{1,17},{... | collective-permute-start | bytes 1376264 | tf_op jit(solution)/shard_map/ppermute | solution.py:47
  943.9 61.9 %collective-permute-start.53 = (bf16[2,224,1280]{2,1,0:T(8,128)(2,1)S(1)}, bf16[2,224,1280]{2,1,0:T(8,128)(2,1)S(1)}, u32[]{:S(2)}, u32[]{:S(2)}) collective-permute-start(bf16[2,224,1280]{2,1,0:T(8,128)(2,1)S(1)} %fusion.31), channel_id=1, source_target_pairs={{0,2},{1,3},{2,0},{3,1},{4,6},{5,7},{6,4},{7,5},{8,10},{9,11},{10,... | collective-permute-start | bytes 3440648 | tf_op jit(solution)/shard_map/ppermute | solution.py:47
  988.0 50.9 %collective-permute-start.48 = (bf16[2,224,1024]{2,1,0:T(8,128)(2,1)}, bf16[2,224,1024]{2,1,0:T(8,128)(2,1)}, u32[]{:S(2)}, u32[]{:S(2)}) collective-permute-start(bf16[2,224,1024]{2,1,0:T(8,128)(2,1)} %pad_maximum_fusion.6), channel_id=1, source_target_pairs={{0,1},{1,0},{2,3},{3,2},{4,5},{5,4},{6,7},{7,6},{8,9},{9,8},{10,11... | collective-permute-start | bytes 2752520 | tf_op jit(solution)/shard_map/ppermute | solution.py:47
  (99 other events, 1657.2 us)
Sparse Core Ops, SparseCore 0:
  114.1 310.5 all-gather.2
